TPU v7x, 256 devices: a whole 4x4x8 slice. The times are simulated.
256 devices in a mesh: dp: 16 (over y, x_lo, core), ctx: 16 (over x_hi, z).
Axes of the slice: x: 4 (x_hi: 2, x_lo: 2; x = x_hi * 2 + x_lo), y: 4, z: 8, core: 2. Of those that a mesh axis runs over, the one named last changes fastest.
Arguments:
- signal: bfloat16 [16, 4096, 4096], P('dp', 'ctx'), may hold values from -11 to 11
- cotangent: bfloat16 [16, 4096, 4096], P('dp', 'ctx'), may hold values from -6 to 6
- input_map: bfloat16 [16, 4096, 1024], P('dp', 'ctx'), may hold values from -1.75 to 1.75
- output_map: bfloat16 [16, 4096, 1024], P('dp', 'ctx'), may hold values from -1.75 to 1.75
- step_raw: float32 [16, 64, 4096], P('dp', None, 'ctx'), may hold values from -3 to 3
- decay_log: float32 [64], replicated, may hold values from -12 to 0
- step_bias: float32 [64], replicated, may hold values from -4 to -2.5
- skip_gain: float32 [64], replicated, may hold values from 0.5 to 2
- checkpoints: bfloat16 [16, 16, 64, 64, 128], P('dp', 'ctx'), may hold values from -1.75 to 1.75
Outputs:
- signal_grad: float32 [16, 4096, 4096], P('dp', 'ctx')
- input_map_grad: float32 [16, 4096, 1024], P('dp', 'ctx')
- output_map_grad: float32 [16, 4096, 1024], P('dp', 'ctx')
- step_raw_grad: float32 [16, 64, 4096], P('dp', None, 'ctx')
- decay_log_grad: float32 [64], replicated
- skip_gain_grad: float32 [64], replicated
- step_bias_grad: float32 [64], replicated
All inputs are finite; a program needn't handle non-finite values.
Results may differ from a plain program's by a relative error of at most 0.0003.
Values sent between devices are 32-bit elements; how exact they have to be, the bound alone decides.
No kernel may reach another device: no remote copies, remote signals or barrier semaphores. Data moves between devices by JAX's collectives and lax.ppermute only.
A program may use at most 128 MiB of HBM per device.

v0:
```python
import jax
import jax.numpy as jnp
from jax import lax
from jax.sharding import PartitionSpec as P

G = 8


highest = lax.Precision.HIGHEST


def carried_in(array, axis, combine, identity):
    count, position = (lax.axis_size(axis), lax.axis_index(axis))
    everything = jax.tree.map(lambda part: lax.all_gather(part, axis), array)
    start = jax.tree.map(
        lambda part, zero: jnp.broadcast_to(jnp.asarray(zero, part.dtype), part.shape),
        array,
        identity,
    )

    def step(k, before):
        at = count - 1 - k
        reached = at > position
        new = combine(before, jax.tree.map(lambda part: part[at], everything))
        return jax.tree.map(lambda a, b: jnp.where(reached, a, b), new, before)

    return lax.fori_loop(0, count, step, start)


def prepare(raw_steps, decay_log, step_bias):
    pre_act = raw_steps + step_bias[:, None]
    step_size = jax.nn.softplus(pre_act)
    rate = -jnp.exp(decay_log)[:, None] * step_size
    cumul = jnp.cumsum(rate, axis=1)
    return (pre_act, step_size, cumul)


def local_state(grads_out, out_block, cumul, group_count):
    length = out_block.shape[0]
    head_count = cumul.shape[0]
    per_group = head_count // group_count
    weights = jnp.exp(cumul).reshape(group_count, per_group, length)
    grad_float = grads_out.astype(jnp.float32).reshape(length, group_count, per_group, -1)
    out_float = out_block.astype(jnp.float32).reshape(length, group_count, -1)
    state = jnp.einsum("ghl,lghp,lgn->ghpn", weights, grad_float, out_float, precision=highest)
    return (
        state.reshape(head_count, grad_float.shape[3], out_float.shape[2]),
        jnp.exp(cumul[:, -1]),
    )


def group_grads(
    sig_group,
    grad_group,
    in_group,
    out_group,
    steps_group,
    cumul_group,
    rates,
    skips,
    start_group,
    end_group,
):
    sig_float = sig_group.astype(jnp.float32)
    grad_float = grad_group.astype(jnp.float32)
    in_float = in_group.astype(jnp.float32)
    out_float = out_group.astype(jnp.float32)
    length = sig_float.shape[0]
    rows_index = lax.broadcasted_iota(jnp.int32, (length, length), 0)
    cols_index = lax.broadcasted_iota(jnp.int32, (length, length), 1)
    lower = (rows_index >= cols_index)[None]
    scores = jnp.dot(out_group, in_group.T, preferred_element_type=jnp.float32)
    differ = cumul_group[:, :, None] - cumul_group[:, None, :]
    decay = jnp.where(lower, jnp.exp(jnp.where(lower, differ, 0.0)), 0.0)
    mixing = decay * scores[None] * steps_group[:, None, :]
    mix_grad = jnp.einsum("thp,shp->hts", grad_group, sig_group, preferred_element_type=jnp.float32)
    final = cumul_group[:, -1:]
    carry_weight = jnp.exp(final - cumul_group) * steps_group
    end_in = jnp.einsum("hpn,sn->shp", end_group, in_float, precision=highest)
    sig_grad = jnp.einsum("hts,thp->shp", mixing, grad_float, precision=highest)
    sig_grad = sig_grad + skips[None, :, None] * grad_float + carry_weight.T[:, :, None] * end_in
    weighted = mix_grad * decay
    score_grad = jnp.sum(weighted * steps_group[:, None, :], axis=0)
    entry = jnp.exp(cumul_group)
    start_out = jnp.einsum("hpn,tn->thp", start_group, out_float, precision=highest)
    out_grad = jnp.dot(score_grad, in_float, precision=highest)
    out_grad = out_grad + jnp.einsum(
        "hpn,thp,ht->tn", start_group, grad_float, entry, precision=highest
    )
    in_grad = jnp.dot(score_grad.T, out_float, precision=highest)
    in_grad = in_grad + jnp.einsum(
        "hpn,shp,hs->sn", end_group, sig_float, carry_weight, precision=highest
    )
    product = mix_grad * mixing
    cumul_grad = jnp.sum(product, axis=2) - jnp.sum(product, axis=1)
    cumul_grad = cumul_grad + entry * jnp.einsum("thp,thp->ht", grad_float, start_out)
    pushed = jnp.einsum("shp,shp->hs", sig_float, end_in)
    cumul_grad = cumul_grad - carry_weight * pushed
    tail = jnp.exp(final[:, 0]) * jnp.sum(end_group * start_group, axis=(1, 2)) + jnp.sum(
        carry_weight * pushed, axis=1
    )
    cumul_grad = jnp.concatenate([cumul_grad[:, :-1], cumul_grad[:, -1:] + tail[:, None]], axis=1)
    rate_grad = jnp.cumsum(cumul_grad[:, ::-1], axis=1)[:, ::-1]
    step_grad = jnp.einsum("hts,ts->hs", weighted, scores, precision=highest)
    step_grad = step_grad + jnp.exp(final - cumul_group) * pushed - rate_grad * rates[:, None]
    decay_grad = jnp.sum(rate_grad * (-rates[:, None] * steps_group), axis=1)
    skip_grad = jnp.einsum("thp,thp->h", grad_group, sig_group, preferred_element_type=jnp.float32)
    return (sig_grad, in_grad, out_grad, step_grad, decay_grad, skip_grad)


def block_grads(
    sig_block,
    grad_block,
    in_block,
    out_block,
    raw_steps,
    decay_log,
    step_bias,
    skip_gain,
    start_state,
    end_state,
    group_count,
):
    length = sig_block.shape[0]
    head_count = raw_steps.shape[0]
    per_group = head_count // group_count
    head_width = sig_block.shape[1] // head_count
    state_width = in_block.shape[1] // group_count
    pre_act, step_size, cumul = prepare(raw_steps, decay_log, step_bias)
    sig_groups = sig_block.reshape(length, group_count, per_group, head_width).transpose(1, 0, 2, 3)
    grad_groups = grad_block.reshape(length, group_count, per_group, head_width).transpose(
        1, 0, 2, 3
    )
    in_groups = in_block.reshape(length, group_count, state_width).transpose(1, 0, 2)
    out_groups = out_block.reshape(length, group_count, state_width).transpose(1, 0, 2)
    step_groups = step_size.reshape(group_count, per_group, length)
    cumul_groups = cumul.reshape(group_count, per_group, length)
    rate_groups = jnp.exp(decay_log).reshape(group_count, per_group)
    skip_groups = skip_gain.reshape(group_count, per_group)
    start_groups = start_state.astype(jnp.float32).reshape(
        group_count, per_group, head_width, state_width
    )
    end_groups = end_state.reshape(group_count, per_group, head_width, state_width)
    results = lax.map(
        lambda pieces: group_grads(*pieces),
        (
            sig_groups,
            grad_groups,
            in_groups,
            out_groups,
            step_groups,
            cumul_groups,
            rate_groups,
            skip_groups,
            start_groups,
            end_groups,
        ),
    )
    sig_grad = results[0].transpose(1, 0, 2, 3).reshape(length, head_count * head_width)
    in_grad = results[1].transpose(1, 0, 2).reshape(length, group_count * state_width)
    out_grad = results[2].transpose(1, 0, 2).reshape(length, group_count * state_width)
    pre_grad = results[3].reshape(head_count, length) * jax.nn.sigmoid(pre_act)
    return (
        sig_grad,
        in_grad,
        out_grad,
        pre_grad,
        results[4].reshape(head_count),
        results[5].reshape(head_count),
        jnp.sum(pre_grad, axis=1),
    )


def combine(earlier, later):
    return (later[0] * earlier[0], later[1] + later[0][:, None, None] * earlier[1])


def local(
    signal, cotangent, input_map, output_map, step_raw, decay_log, step_bias, skip_gain, checkpoints
):
    raw_steps = step_raw[0]
    cumul = prepare(raw_steps, decay_log, step_bias)[2]
    state, total = local_state(cotangent[0], output_map[0], cumul, G)
    ends = carried_in(
        (total, state), "ctx", combine, (jnp.ones_like(total), jnp.zeros_like(state))
    )[1]
    grads = block_grads(
        signal[0],
        cotangent[0],
        input_map[0],
        output_map[0],
        raw_steps,
        decay_log,
        step_bias,
        skip_gain,
        checkpoints[0, 0],
        ends,
        G,
    )
    sums = lax.psum((grads[4], grads[5], grads[6]), ("dp", "ctx"))
    factor = 1.0 / (lax.axis_size("dp") * lax.axis_size("ctx") * signal.shape[1])
    return (
        grads[0][None],
        grads[1][None],
        grads[2][None],
        grads[3][None],
        sums[0] * factor,
        sums[1] * factor,
        sums[2] * factor,
    )


def solution(mesh):
    placed = (
        P("dp", "ctx", None),
        P("dp", "ctx", None),
        P("dp", "ctx", None),
        P("dp", "ctx", None),
        P("dp", None, "ctx"),
        P(),
        P(),
        P(),
        P("dp", "ctx", None, None, None),
    )
    return jax.shard_map(
        local,
        mesh=mesh,
        in_specs=placed,
        out_specs=(
            P("dp", "ctx", None),
            P("dp", "ctx", None),
            P("dp", "ctx", None),
            P("dp", None, "ctx"),
            P(),
            P(),
            P(),
        ),
        check_vma=False,
    )
```

profile of v0, /device:TPU:1, one launch (start us, length us, event | category | flops | bytes accessed | tf_op | source)
XLA Modules:
  0.0 786.0 jit_solution(17047756089433240317)
XLA Ops:
  10.6 3.3 copy.100
  15.2 4.6 fusion.78
  22.3 39.5 %all-reduce = f32[1024]{0:T(1024)S(1)} all-reduce(f32[1024]{0:T(1024)S(1)} %dynamic-update-slice), channel_id=2, replica_groups=mesh['dp'=16,'ctx'=16] {'ctx'}, use_global_device_ids=true, to_apply=%add | all-reduce | flops 1024 | bytes 8192
  62.0 4.1 copy.107
  70.5 365.9 %all-gather.3.cloned.1.call-done = f32[16,64,64,128]{3,2,1,0:T(8,128)} async-done(((f32[1,64,64,128]{3,2,1,0:T(8,128)}), f32[16,64,64,128]{3,2,1,0:T(8,128)}) %all-gather.3.cloned.1.call-update) | async-done | bytes 33554448 | tf_op jit(solution)/shard_map/all_gather | solution.py:14
  436.4 34.1 %while.39 = (s32[]{:T(128)}, f32[64,64,128]{2,1,0:T(8,128)S(1)}, s32[]{:T(128)}, f32[16,64,64,128]{3,2,1,0:T(8,128)}, f32[16,64]{1,0:T(8,128)S(1)}) while((s32[]{:T(128)}, f32[64,64,128]{2,1,0:T(8,128)S(1)}, s32[]{:T(128)}, f32[16,64,64,128]{3,2,1,0:T(8,128)}, f32[16,64]{1,0:T(8,128)S(1)}) %tuple.96), condition=%wide.region_3.4_spmd.clone.clone, body=%wide.region_2.3_spmd.clone.sunk.clone | while | flops 2097160 | bytes 6292359 | solution.py:27
  438.5 2.1 fusion.168
  440.7 2.1 fusion.168
  442.8 2.1 fusion.168
  445.0 2.1 fusion.168
  447.1 2.1 fusion.168
  449.2 2.1 fusion.168
  451.4 2.1 fusion.168
  453.5 2.1 fusion.168
  455.6 2.1 fusion.168
  457.8 2.1 fusion.168
  459.9 2.1 fusion.168
  462.1 2.1 fusion.168
  464.2 2.1 fusion.168
  466.3 2.1 fusion.168
  468.5 2.1 fusion.168
  470.6 220.2 %while.38 = (s32[]{:T(128)}, f32[8,256,8,64]{1,3,2,0:T(8,128)}, f32[8,256,128]{2,1,0:T(8,128)}, f32[8,256,128]{2,1,0:T(8,128)}, f32[8,8,256]{2,1,0:T(8,128)S(1)}...) while((s32[]{:T(128)}, f32[8,256,8,64]{1,3,2,0:T(8,128)}, ...), condition=%wide.region_13.14_spmd.clone, body=%wide.region_4.13_spmd.sunk.clone | while | flops 1507682304 | bytes 22025220 | solution.py:144
  473.5 3.6 fusion.161
  482.6 2.4 multiply_reduce_fusion.12
  485.8 2.3 fusion.160
  501.0 3.6 fusion.161
  510.1 2.4 multiply_reduce_fusion.12
  513.3 2.3 fusion.160
  528.5 3.6 fusion.161
  537.6 2.4 multiply_reduce_fusion.12
  540.8 2.3 fusion.160
  556.0 3.6 fusion.161
  565.1 2.4 multiply_reduce_fusion.12
  568.3 2.3 fusion.160
  583.5 3.6 fusion.161
  592.6 2.4 multiply_reduce_fusion.12
  595.8 2.4 fusion.160
  611.0 3.6 fusion.161
  620.2 2.4 multiply_reduce_fusion.12
  623.3 2.3 fusion.160
  638.6 3.6 fusion.161
  647.7 2.4 multiply_reduce_fusion.12
  650.9 2.3 fusion.160
  666.1 3.6 fusion.161
  675.2 2.4 multiply_reduce_fusion.12
  678.4 2.4 fusion.160
  693.9 75.0 %all-reduce.1 = (f32[64]{0:T(128)S(1)}, f32[64]{0:T(128)S(1)}, f32[64]{0:T(128)S(1)}) all-reduce(f32[64]{0:T(128)S(1)} %reshape.143, f32[64]{0:T(128)S(1)} %reshape.144, f32[64]{0:T(128)S(1)} %reduce_sum.70), channel_id=1, replica_groups=mesh['dp'=16,'ctx'=16] {'dp','ctx'}, use_global_device_ids=true, to_apply=%region_14.15 | all-reduce | flops 192 | bytes 1536 | tf_op jit(solution)/shard_map/psum | solution.py:200
  769.4 5.7 copy.112
  (343 shorter events, 173.5 us)
Async XLA Ops:
  7.2 429.2 %all-gather.3.cloned.1.call-start = ((), (), s32[]{:S(2)}) async-start(), calls=%async_computation | async-start | bytes 35651584 | tf_op jit(solution)/shard_map/all_gather | solution.py:14
  10.6 3.4 copy-start.6
  14.0 5.8 copy-start
  19.8 0.7 copy-start.7
  19.8 0.8 copy-start.9
  62.0 4.1 copy-start.2
  66.2 3.6 copy-start.8
  66.2 4.3 copy-start.3
  482.6 3.2 copy-start.1
  510.1 3.2 copy-start.1
  537.6 3.2 copy-start.1
  565.1 3.2 copy-start.1
  592.6 3.2 copy-start.1
  620.2 3.2 copy-start.1
  647.7 3.2 copy-start.1
  675.2 3.2 copy-start.1
  769.4 5.7 copy-start.4
  775.1 1.7 copy-start.5
Sparse Core Ops, SparseCore 0:
  19.9 416.4 all-gather.2
where the time goes:
time: 790 us; the launch traced here: 786 us
  waiting for transfers between devices  366 us (46%)
  matrix products  144 us (18%)
  blocking collectives  115 us (15%)
  other arithmetic  87.4 us (11%)
  local copies, waits for them, and re-layouts  58.1 us (7%)
  between operations  14.9 us (2%)
    all_gather x1, waiting for transfers between devices, carried_in(): everything = jax.tree.map(lambda part: lax.all_gather(part, axis), array)  366 us
    psum x1, blocking collectives, local(): sums = lax.psum((grads[4], grads[5], grads[6]), ('dp', 'ctx'))  75 us
    unnamed x1, blocking collectives  39.5 us
    select_n x16, other arithmetic, step(): return jax.tree.map(lambda a, b: jnp.where(reached, a, b), new, before)  33.3 us
    dot_general x8, matrix products, group_grads(): jnp.einsum('thp,shp->hts', grad_group, sig_group, preferred_element_type=...  29 us
    dynamic_update_slice x16, local copies, waits for them, and re-layouts, block_grads(): lax.map(lambda pieces: group_grads(*pieces), (sig_groups, grad_groups, in...  20.6 us
    dot_general x8, other arithmetic, group_grads(): step_grad = jnp.einsum('hts,ts->hs', weighted, scores, precision=highest)  19.2 us
    dot_general x8, matrix products, group_grads(): sig_grad = jnp.einsum('hts,thp->shp', mixing, grad_float, precision=highest)  18.7 us
  transfers between devices with their start and end apart: 1, of which 1 were waited for; matrix products, arithmetic and copies ran while one was open for 1% of the time, Pallas kernels for 0%

commit v1 on v0

v1 whole, which is shorter than its diff:
```python
import jax
import jax.numpy as jnp
from jax import lax
from jax.experimental import pallas as pl
from jax.experimental.pallas import tpu as pltpu
from jax.sharding import PartitionSpec as P

T = 256
H = 64
G = 8
D = 64
N = 128
PER = H // G
WIDE = PER * D
F32 = jnp.float32
BF16 = jnp.bfloat16
VMEM_LIMIT = 40 * 1024 * 1024


def split(x, parts):
    pieces = []
    for _ in range(parts):
        piece = x.astype(BF16)
        pieces.append(piece)
        x = x - piece.astype(F32)
    return pieces


def mm(a, b):
    return lax.dot_general(a, b, (((1,), (0,)), ((), ())), preferred_element_type=F32)


def mm_nt(a, b):
    return lax.dot_general(a, b, (((1,), (1,)), ((), ())), preferred_element_type=F32)


def mm_tn(a, b):
    return lax.dot_general(a, b, (((0,), (0,)), ((), ())), preferred_element_type=F32)


def rows_times_mask(rows, mask):
    out = mm(jnp.concatenate(split(rows, 3), axis=0), mask)
    return out[:PER] + out[PER : 2 * PER] + out[2 * PER :]


def mask_of(relation):
    i = lax.broadcasted_iota(jnp.int32, (T, T), 0)
    j = lax.broadcasted_iota(jnp.int32, (T, T), 1)
    return jnp.where(relation(i, j), 1.0, 0.0).astype(BF16)


def steps_of(raw, bias, decay_log):
    pre_act = raw + bias
    step = jnp.maximum(pre_act, 0.0) + jnp.log1p(jnp.exp(-jnp.abs(pre_act)))
    decay = jnp.exp(decay_log)
    rate = -decay * step
    cumul = rows_times_mask(rate, mask_of(lambda i, j: i <= j))
    return pre_act, step, decay, cumul


def spread(rows):
    head = lax.broadcasted_iota(jnp.int32, (PER, WIDE), 0)
    column = lax.broadcasted_iota(jnp.int32, (PER, WIDE), 1)
    own = jnp.where(column // D == head, 1.0, 0.0).astype(BF16)
    return mm_tn(jnp.concatenate(split(rows, 3), axis=0), jnp.concatenate([own] * 3, axis=0))


def columns(rows):
    pad = jnp.zeros((128 - PER * len(rows), T), F32)
    return jnp.transpose(jnp.concatenate(list(rows) + [pad], axis=0))


def state_kernel(cot_ref, out_ref, raw_ref, decay_ref, bias_ref, sent_ref):
    cumul = steps_of(raw_ref[...], bias_ref[...], decay_ref[...])[3]
    entry = jnp.exp(cumul)
    weighted = cot_ref[...].astype(F32) * spread(entry)
    out_map = out_ref[...]
    high, low = split(weighted, 2)
    state = mm_tn(high, out_map) + mm_tn(low, out_map)
    total = jnp.broadcast_to(entry[:, T - 1 :], (PER, N))
    half = WIDE // 2
    sent_ref[0, :half] = state[:half]
    sent_ref[1, :half] = state[half:]
    sent_ref[0, half:] = total
    sent_ref[1, half:] = jnp.concatenate([total[PER // 2 :], total[: PER // 2]], axis=0)


def scan_kernel(state_ref, total_ref, end_ref):
    head = pl.program_id(0)
    carry = jnp.zeros((D, N), F32)
    for b in reversed(range(state_ref.shape[0])):
        end_ref[b] = carry
        carry = state_ref[b] + total_ref[b, pl.ds(head, 1), :] * carry


def inner_kernel(
    sig_ref,
    cot_ref,
    in_ref,
    out_ref,
    raw_ref,
    decay_ref,
    bias_ref,
    skip_ref,
    start_ref,
    sig_grad_ref,
    in_grad_ref,
    out_grad_ref,
    step_grad_ref,
    by_decay_ref,
    by_bias_ref,
    sums_ref,
):
    pre_act, step, decay, cumul = steps_of(raw_ref[...], bias_ref[...], decay_ref[...])
    slope = jax.nn.sigmoid(pre_act)
    entry = jnp.exp(cumul)
    final = cumul[:, T - 1 :]
    total = jnp.exp(final)
    leave = jnp.exp(final - cumul)
    later = rows_times_mask(slope, mask_of(lambda i, j: i > j))
    cols = columns([cumul - jnp.log(step), entry])
    in_map = in_ref[...]
    out_map = out_ref[...]
    out_float = out_map.astype(F32)
    scores = mm_nt(in_map, out_map)
    valid = lax.broadcasted_iota(jnp.int32, (T, T), 0) <= lax.broadcasted_iota(jnp.int32, (T, T), 1)
    lane = lax.broadcasted_iota(jnp.int32, (T, N), 1)
    first = lane < D
    score_grad = jnp.zeros((T, T), F32)
    out_grad = jnp.zeros((T, N), F32)
    found = jnp.zeros((T, N), F32)
    row_sums = []
    for pair in range(PER // 2):
        at = slice(pair * N, (pair + 1) * N)
        sig = sig_ref[:, at]
        cot = cot_ref[:, at]
        zero = jnp.zeros_like(sig)
        sig_grad = jnp.zeros((T, N), F32)
        start = start_ref[at, :]
        top = lax.broadcasted_iota(jnp.int32, (N, N), 0) < D
        none = jnp.zeros_like(start)
        both = jnp.concatenate(
            [jnp.where(top, start, none), jnp.where(top, none, start)], axis=1
        )
        began = mm(cot, both)
        for k in range(2):
            j = 2 * pair + k
            mine = first if k == 0 else jnp.logical_not(first)
            own_sig = jnp.where(mine, sig, zero)
            own_cot = jnp.where(mine, cot, zero)
            mix_grad = mm_nt(own_sig, cot)
            fade = jnp.where(valid, jnp.exp(cumul[j : j + 1, :] - cols[:, j : j + 1]), 0.0)
            mixing = fade * scores
            high, low = split(mixing, 2)
            sig_grad = sig_grad + (mm(high, own_cot) + mm(low, own_cot))
            score_grad = score_grad + mix_grad * fade
            product = mix_grad * mixing
            row_sums.append(jnp.sum(product, axis=0, keepdims=True))
            found = jnp.where(lane == j, jnp.sum(product, axis=1, keepdims=True), found)
            own = began[:, k * N : (k + 1) * N]
            out_grad = out_grad + own * cols[:, PER + j : PER + j + 1]
            found = jnp.where(
                lane == PER + j, jnp.sum(own * out_float, axis=1, keepdims=True), found
            )
        sig_grad_ref[:, at] = sig_grad
    sig_float = sig_ref[...].astype(F32)
    cot_float = cot_ref[...].astype(F32)
    skip = skip_ref[...]
    sig_grad_ref[...] = sig_grad_ref[...] + skip * cot_float
    high, low = split(score_grad, 2)
    in_grad_ref[...] = mm(high, out_map) + mm(low, out_map)
    out_grad_ref[...] = out_grad + (mm_tn(high, in_map) + mm_tn(low, in_map))
    found = jnp.transpose(found)
    col_sum = found[:PER]
    from_start = found[PER : 2 * PER]
    cumul_grad = jnp.concatenate(row_sums, axis=0) - col_sum + entry * from_start
    rate_grad = rows_times_mask(cumul_grad, mask_of(lambda i, j: i >= j))
    step_grad = col_sum / step - rate_grad * decay
    step_grad_ref[...] = step_grad
    into_decay = (final - cumul) * leave * step
    into_bias = leave * (slope - decay * step * later)
    start = start_ref[...].astype(F32).reshape(PER, D, N)
    for rows, weight, ref in (
        (into_decay, final * total, by_decay_ref),
        (into_bias, -decay * total * jnp.sum(slope, axis=1, keepdims=True), by_bias_ref),
    ):
        high, low = split(sig_float * spread(rows), 2)
        grown = mm_tn(high, in_map) + mm_tn(low, in_map)
        ref[...] = grown + (start * weight[:, :, None]).reshape(WIDE, N)
    own = jnp.where(
        lax.broadcasted_iota(jnp.int32, (PER, WIDE), 1) // D
        == lax.broadcasted_iota(jnp.int32, (PER, WIDE), 0),
        1.0,
        0.0,
    )
    skip_sum = jnp.sum(
        own * jnp.sum(sig_float * cot_float, axis=0, keepdims=True), axis=1, keepdims=True
    )
    decay_sum = -decay * jnp.sum(rate_grad * step, axis=1, keepdims=True)
    bias_sum = jnp.sum(step_grad * slope, axis=1, keepdims=True)
    which = lax.broadcasted_iota(jnp.int32, (PER, N), 1)
    sums_ref[...] = jnp.where(
        which == 0, decay_sum, jnp.where(which == 1, bias_sum, jnp.where(which == 2, skip_sum, 0.0))
    )


def sums_kernel(end_ref, by_decay_ref, by_bias_ref, sums_ref, sent_ref, kept):
    group = pl.program_id(0)
    end = end_ref[...]
    which = lax.broadcasted_iota(jnp.int32, (PER, N), 1)
    sums = sums_ref[...]
    for k, ref in enumerate((by_decay_ref, by_bias_ref)):
        partial = jnp.sum((end * ref[...]).reshape(PER, D, N), axis=1)
        sums = sums + jnp.where(which == k, jnp.sum(partial, axis=1, keepdims=True), 0.0)

    @pl.when(group == 0)
    def _():
        kept[...] = jnp.zeros_like(kept)

    kept[pl.ds(pl.multiple_of(group * PER, PER), PER), :] = sums

    @pl.when(group == G - 1)
    def _():
        rows = jnp.transpose(kept[...])[:8]
        sent_ref[...] = jnp.broadcast_to(rows[None], sent_ref.shape)


def outer_kernel(
    end_ref,
    sig_ref,
    in_ref,
    raw_ref,
    decay_ref,
    bias_ref,
    start_ref,
    sig_part_ref,
    in_part_ref,
    step_part_ref,
    sig_grad_ref,
    in_grad_ref,
    step_grad_ref,
):
    pre_act, step, decay, cumul = steps_of(raw_ref[...], bias_ref[...], decay_ref[...])
    slope = jax.nn.sigmoid(pre_act)
    final = cumul[:, T - 1 :]
    leave = jnp.exp(final - cumul)
    carry = leave * step
    end = end_ref[...]
    in_map = in_ref[...]
    sig = sig_ref[...].astype(F32)
    wide = spread(carry)
    end_high, end_low = split(end, 2)
    end_in = mm_nt(in_map, end_high) + mm_nt(in_map, end_low)
    sig_grad_ref[...] = sig_part_ref[...] + wide * end_in
    high, low = split(sig * wide, 2)
    in_grad_ref[...] = (
        in_part_ref[...] + mm(high, end_high) + (mm(high, end_low) + mm(low, end_high))
    )
    own = jnp.where(
        lax.broadcasted_iota(jnp.int32, (PER, WIDE), 1) // D
        == lax.broadcasted_iota(jnp.int32, (PER, WIDE), 0),
        1.0,
        0.0,
    ).astype(BF16)
    high, low = split(sig * end_in, 2)
    pushed = mm_nt(own, high) + mm_nt(own, low)
    before = rows_times_mask(carry * pushed, mask_of(lambda i, j: i < j))
    held = jnp.sum((end * start_ref[...].astype(F32)).reshape(PER, D, N), axis=1)
    held = jnp.exp(final) * jnp.sum(held, axis=1, keepdims=True)
    step_grad = step_part_ref[...] + leave * pushed - decay * (before + held)
    step_grad_ref[...] = step_grad * slope


def call(kernel, grid, ins, outs, args, flops, scratch=()):
    moved = sum(a.size * a.dtype.itemsize for a in args) + sum(4 * s.size for _, s in outs)
    return pl.pallas_call(
        kernel,
        grid=(grid,),
        in_specs=ins,
        out_specs=[spec for spec, _ in outs],
        out_shape=[shape for _, shape in outs],
        scratch_shapes=list(scratch),
        compiler_params=pltpu.CompilerParams(
            dimension_semantics=("arbitrary",), vmem_limit_bytes=VMEM_LIMIT
        ),
        cost_estimate=pl.CostEstimate(flops=flops, bytes_accessed=moved, transcendentals=0),
    )(*args)


def f32(*shape):
    return jax.ShapeDtypeStruct(shape, F32)


WIDE_COLS = pl.BlockSpec((T, WIDE), lambda g: (0, g))
MAP_COLS = pl.BlockSpec((T, N), lambda g: (0, g))
HEAD_ROWS = pl.BlockSpec((PER, T), lambda g: (g, 0))
HEAD_ONE = pl.BlockSpec((PER, 1), lambda g: (g, 0))
HEAD_LANES = pl.BlockSpec((PER, N), lambda g: (g, 0))
STATE_ROWS = pl.BlockSpec((WIDE, N), lambda g: (g, 0))
SKIP_COLS = pl.BlockSpec((1, WIDE), lambda g: (0, g))


def local(
    signal, cotangent, input_map, output_map, step_raw, decay_log, step_bias, skip_gain, checkpoints
):
    sig, cot, in_map, out_map, raw = (
        signal[0],
        cotangent[0],
        input_map[0],
        output_map[0],
        step_raw[0],
    )
    decay_col, bias_col = decay_log[:, None], step_bias[:, None]
    skip_row = jnp.repeat(skip_gain, D)[None, :]
    start = checkpoints.reshape(H * D, N)
    blocks = lax.axis_size("ctx")
    rows = H * D // blocks
    own = H // blocks

    sent = call(
        state_kernel,
        G,
        [WIDE_COLS, MAP_COLS, HEAD_ROWS, HEAD_ONE, HEAD_ONE],
        [
            (
                pl.BlockSpec((blocks // G, rows + 8, N), lambda g: (g, 0, 0)),
                f32(blocks, rows + 8, N),
            )
        ],
        (cot, out_map, raw, decay_col, bias_col),
        4 * H * D * N * T,
    )[0]
    states = lax.all_to_all(sent, "ctx", 0, 0)
    ends = call(
        scan_kernel,
        own,
        [
            pl.BlockSpec((blocks, D, N), lambda i: (0, i, 0)),
            pl.BlockSpec((blocks, 8, N), lambda i: (0, rows // 8, 0)),
        ],
        [(pl.BlockSpec((blocks, D, N), lambda i: (0, i, 0)), f32(blocks, rows, N))],
        (states, states),
        2 * H * D * N,
    )[0]
    end = lax.all_to_all(ends, "ctx", 0, 0).reshape(H * D, N)

    sig_part, in_part, out_grad, step_part, by_decay, by_bias, sums = call(
        inner_kernel,
        G,
        [
            WIDE_COLS,
            WIDE_COLS,
            MAP_COLS,
            MAP_COLS,
            HEAD_ROWS,
            HEAD_ONE,
            HEAD_ONE,
            SKIP_COLS,
            STATE_ROWS,
        ],
        [
            (WIDE_COLS, f32(T, H * D)),
            (MAP_COLS, f32(T, G * N)),
            (MAP_COLS, f32(T, G * N)),
            (HEAD_ROWS, f32(H, T)),
            (STATE_ROWS, f32(H * D, N)),
            (STATE_ROWS, f32(H * D, N)),
            (HEAD_LANES, f32(H, N)),
        ],
        (sig, cot, in_map, out_map, raw, decay_col, bias_col, skip_row, start),
        H * T * T * N * 20,
    )

    sent = call(
        sums_kernel,
        G,
        [STATE_ROWS, STATE_ROWS, STATE_ROWS, HEAD_LANES],
        [(pl.BlockSpec((blocks, 8, N), lambda g: (0, 0, 0)), f32(blocks, 8, N))],
        (end, by_decay, by_bias, sums),
        4 * H * D * N,
        [pltpu.VMEM((N, N), F32)],
    )[0]
    summed = jnp.sum(lax.all_to_all(sent, "ctx", 0, 0), axis=0)
    sent = jnp.broadcast_to(summed[None], (lax.axis_size("dp"),) + summed.shape)
    summed = jnp.sum(lax.all_to_all(sent, "dp", 0, 0), axis=0)
    summed = summed * (1.0 / (lax.axis_size("dp") * blocks * T))

    sig_grad, in_grad, step_grad = call(
        outer_kernel,
        G,
        [
            STATE_ROWS,
            WIDE_COLS,
            MAP_COLS,
            HEAD_ROWS,
            HEAD_ONE,
            HEAD_ONE,
            STATE_ROWS,
            WIDE_COLS,
            MAP_COLS,
            HEAD_ROWS,
        ],
        [(WIDE_COLS, f32(T, H * D)), (MAP_COLS, f32(T, G * N)), (HEAD_ROWS, f32(H, T))],
        (end, sig, in_map, raw, decay_col, bias_col, start, sig_part, in_part, step_part),
        8 * H * D * N * T,
    )
    return (
        sig_grad[None],
        in_grad[None],
        out_grad[None],
        step_grad[None],
        summed[0, :H],
        summed[2, :H],
        summed[1, :H],
    )


def solution(mesh):
    rows = P("dp", "ctx", None)
    placed = (rows, rows, rows, rows, P("dp", None, "ctx"), P(), P(), P())
    return jax.shard_map(
        local,
        mesh=mesh,
        in_specs=placed + (P("dp", "ctx", None, None, None),),
        out_specs=(rows, rows, rows, P("dp", None, "ctx"), P(), P(), P()),
        check_vma=False,
    )
```

time: 790 us -> 177 us (0.22)
  waiting for transfers between devices: 366 us -> 6.65 us
  matrix products: 144 us -> 0 us
  other arithmetic: 87.4 us -> 0.04 us
  Pallas kernels: 0 us -> 52.7 us
  blocking collectives: 115 us -> 78.5 us
  local copies, waits for them, and re-layouts: 58.1 us -> 25.7 us
  between operations: 14.9 us -> 0.74 us
  starting transfers between devices: 0.04 us -> 12 us
    all_gather x1 -> x0, waiting for transfers between devices: 366 us -> none  [carried_in(): everything = jax.tree.map(lambda part: lax.all_gather(part, axis), array)]
    dot_general x73 -> x0, matrix products: 144 us -> none  [the longest x8 29 us: group_grads(): jnp.einsum('thp,shp->hts', grad_group, sig_group, preferred_element_type=...]
    all_to_all x0 -> x2, blocking collectives: none -> 78.5 us  [the longest x1 63.8 us: local(): states = lax.all_to_all(sent, 'ctx', 0, 0)]
    psum x1 -> x0, blocking collectives: 75 us -> none  [local(): sums = lax.psum((grads[4], grads[5], grads[6]), ('dp', 'ctx'))]
    pallas_call x0 -> x5, Pallas kernels: none -> 52.7 us  [call(): pl.pallas_call(kernel, grid=(grid,), in_specs=ins, out_specs=[spec for sp...]
    unnamed x1 -> x0, blocking collectives: 39.5 us -> none
    select_n x17 -> x0, other arithmetic: 33.4 us -> none  [the longest x16 33.3 us: step(): return jax.tree.map(lambda a, b: jnp.where(reached, a, b), new, before)]
    dot_general x16 -> x0, other arithmetic: 28.2 us -> none  [the longest x8 19.2 us: group_grads(): step_grad = jnp.einsum('hts,ts->hs', weighted, scores, precision=highest)]
  transfers between devices with their start and end apart: 1 -> 2, of which waited for: 1 -> 1; matrix products, arithmetic and copies ran while one was open for 1% -> 0% of each run, Pallas kernels for 0% -> 25%
where the time goes in v1:
time: 177 us; the launch traced here: 176 us
  blocking collectives  78.5 us (44%)
  Pallas kernels  52.7 us (30%)
  local copies, waits for them, and re-layouts  25.7 us (15%)
  starting transfers between devices  12 us (7%)
  waiting for transfers between devices  6.65 us (4%)
    all_to_all x1, blocking collectives, local(): states = lax.all_to_all(sent, 'ctx', 0, 0)  63.8 us
    pallas_call x5, Pallas kernels, call(): pl.pallas_call(kernel, grid=(grid,), in_specs=ins, out_specs=[spec for sp...  52.7 us
    unnamed x40, local copies, waits for them, and re-layouts  22.9 us
    all_to_all x1, blocking collectives, local(): summed = jnp.sum(lax.all_to_all(sent, 'ctx', 0, 0), axis=0)  14.7 us
    all_to_all x1, starting transfers between devices, local(): summed = jnp.sum(lax.all_to_all(sent, 'dp', 0, 0), axis=0)  7.6 us
    all_to_all x1, waiting for transfers between devices, local(): end = lax.all_to_all(ends, 'ctx', 0, 0).reshape(H * D, N)  6.65 us
    all_to_all x1, starting transfers between devices, local(): end = lax.all_to_all(ends, 'ctx', 0, 0).reshape(H * D, N)  4.36 us
  transfers between devices with their start and end apart: 2, of which 1 were waited for; matrix products, arithmetic and copies ran while one was open for 0% of the time, Pallas kernels for 25%

profile of v1, /device:TPU:1, one launch (start us, length us, event | category | flops | bytes accessed | tf_op | source)
XLA Modules:
  0.0 176.3 jit_solution(17318372367137918507)
XLA Ops:
  0.6 0.7 copy.22.decay_ref
  1.4 0.7 copy.23.bias_ref
  2.1 0.0 copy-start.6
  2.1 1.6 copy-done.6
  3.7 0.0 copy-start.13
  3.7 1.0 copy-done.13
  4.8 0.0 copy-start.17
  4.8 0.8 copy-done.17
  5.6 6.9 %shard_map.144 = f32[16,264,128]{2,1,0:T(8,128)S(1)} custom-call(bf16[256,4096]{1,0:T(8,128)(2,1)S(1)} %bitcast.21, bf16[256,1024]{1,0:T(8,128)(2,1)S(1)} %bitcast.27, f32[64,256]{1,0:T(8,128)S(1)} %bitcast.31, f32[64,1]{1,0:T(8,128)S(1)} %copy.22.decay_ref, f32[64,1]{1,0:T(8,128)S(1)} %copy.23.bias_ref), custom_call_target="tpu_custom_call" | custom-call | flops 536870912 | bytes 4850176 | tf_op jit(solution)/shard_map/pallas_call | solution.py:276
  12.5 63.8 %all_to_all.20.state_ref.total_ref = f32[16,264,128]{2,1,0:T(8,128)S(1)} all-to-all(f32[16,264,128]{2,1,0:T(8,128)S(1)} %shard_map.144), channel_id=1, replica_groups=mesh['dp'=16,'ctx'=16] {'ctx'}, dimensions={0} | all-to-all | bytes 4325376 | tf_op jit(solution)/shard_map/all_to_all | solution.py:333
  76.3 0.6 shard_map.145
  76.9 0.0 copy-start
  76.9 1.3 copy-done
  78.3 0.0 copy-start.19
  78.3 0.0 copy-start.10
  78.3 0.0 copy-start.18
  78.3 4.4 %all-to-all-start.1 = ((f32[16,256,128]{2,1,0:T(8,128)}), f32[16,256,128]{2,1,0:T(8,128)S(1)}, u32[]{:S(2)}, u32[]{:S(2)}) async-start(f32[16,256,128]{2,1,0:T(8,128)} %copy-done), calls=%async_computation.1 | async-start | bytes 4194304 | tf_op jit(solution)/shard_map/all_to_all | solution.py:345
  82.6 0.0 copy-done.19
  82.6 0.1 broadcast_in_dim.29
  82.7 0.1 broadcast_in_dim_reshape.3.skip_ref
  82.8 0.0 copy-done.10
  82.8 0.0 copy-done.18
  82.8 0.0 copy-start.7
  82.8 1.6 copy-done.7
  84.4 0.0 copy-start.8
  84.4 1.6 copy-done.8
  86.0 1.0 copy-done.14
  87.1 0.0 copy-start.15
  87.1 1.0 copy-done.15
  88.1 32.9 %shard_map.146 = (f32[256,4096]{1,0:T(8,128)}, f32[256,1024]{1,0:T(8,128)S(1)}, f32[256,1024]{1,0:T(8,128)}, f32[64,256]{1,0:T(8,128)S(1)}, f32[4096,128]{1,0:T(...) custom-call(bf16[256,4096]{1,0:T(8,128)(2,1)S(1)} %bitcast.23, bf16[256,4096]{1,0:T(8,128)(2,1)S(1)} %bitcast.22, ...), custom_call_target="tpu_custom_call" | custom-call | flops 10737418240 | bytes 16957952 | tf_op jit(solution)/shard_map/pallas_call | solution.py:276
  120.9 0.0 copy-start.2
  121.0 1.3 copy-done.2
  122.3 1.3 copy-done.4
  123.6 1.0 copy-done.11
  124.6 6.6 %all-to-all-done.1 = f32[16,256,128]{2,1,0:T(8,128)S(1)} async-done(((f32[16,256,128]{2,1,0:T(8,128)}), f32[16,256,128]{2,1,0:T(8,128)S(1)}, u32[]{:S(2)}, u32[]{:S(2)}) %all-to-all-start.1) | async-done | bytes 2097184 | tf_op jit(solution)/shard_map/all_to_all | solution.py:345
  131.2 1.6 copy-done.3
  132.8 1.6 copy-done.5
  134.4 1.2 shard_map.148
  135.7 14.7 %all_to_all.21 = f32[16,8,128]{2,1,0:T(8,128)S(1)} all-to-all(f32[16,8,128]{2,1,0:T(8,128)S(1)} %shard_map.148), channel_id=1, replica_groups=mesh['dp'=16,'ctx'=16] {'ctx'}, dimensions={0} | all-to-all | bytes 131072 | tf_op jit(solution)/shard_map/all_to_all | solution.py:383
  150.4 0.6 broadcast_in_dim.34
  151.0 7.6 %all-to-all-start.3 = ((f32[16,8,128]{2,1,0:T(8,128)}), f32[16,8,128]{2,1,0:T(8,128)S(1)}, u32[]{:S(2)}, u32[]{:S(2)}) async-start(f32[16,8,128]{2,1,0:T(8,128)} %broadcast_in_dim.34), calls=%async_computation.3 | async-start | bytes 131072 | tf_op jit(solution)/shard_map/all_to_all | solution.py:385
  158.6 2.2 %copy-done.1 = f32[256,4096]{1,0:T(8,128)S(1)} copy-done((f32[256,4096]{1,0:T(8,128)S(1)}, f32[256,4096]{1,0:T(8,128)}, u32[]{:S(2)}) %copy-start.1) | copy-done | bytes 4194328
  160.8 1.6 copy-done.9
  162.4 1.2 copy-done.12
  163.6 1.0 copy-done.16
  164.6 11.1 %shard_map.147 = (f32[256,4096]{1,0:T(8,128)}, f32[256,1024]{1,0:T(8,128)}, f32[64,256]{1,0:T(8,128)}) custom-call(f32[4096,128]{1,0:T(8,128)S(1)} %bitcast.20, bf16[256,4096]{1,0:T(8,128)(2,1)S(1)} %bitcast.24, bf16[256,1024]{1,0:T(8,128)(2,1)S(1)} %bitcast.30, f32[64,256]{1,0:T(8,128)S(1)} %bitcast.33, f32[64,1]{1,0:T(8,128)S(1)} %copy.22.decay_ref, ...), custom_call_target="tpu_custom_call" | custom-call | flops 1073741824 | bytes 16450048 | tf_op jit(solution)/shard_map/pallas_call | solution.py:276
  175.8 0.0 all-to-all-done.3
  175.8 0.5 slice_bitcast_fusion
  (12 shorter events, 0.1 us)
Async XLA Ops:
  2.1 1.6 copy-start.6
  3.7 1.0 copy-start.13
  4.8 0.8 copy-start.17
  76.9 1.3 copy-start
  78.3 4.4 %copy-start.19 = (f32[64]{0:T(128)S(1)}, f32[64]{0:T(128)}, u32[]{:S(2)}) copy-start(f32[64]{0:T(128)} %param.16) | copy-start | bytes 772
  78.3 4.6 %copy-start.10 = (bf16[1,1,64,64,128]{4,3,2,1,0:T(8,128)(2,1)S(1)}, bf16[1,1,64,64,128]{4,3,2,1,0:T(8,128)(2,1)}, u32[]{:S(2)}) copy-start(bf16[1,1,64,64,128]{4,3,2,1,0:T(8,128)(2,1)} %param.17) | copy-start | bytes 3145732
  78.3 4.6 %copy-start.18 = (f32[1,64,256]{2,1,0:T(8,128)S(1)}, f32[1,64,256]{2,1,0:T(8,128)}, u32[]{:S(2)}) copy-start(f32[1,64,256]{2,1,0:T(8,128)} %param.13) | copy-start | bytes 196612
  78.3 53.0 %all-to-all-start.1 = ((f32[16,256,128]{2,1,0:T(8,128)}), f32[16,256,128]{2,1,0:T(8,128)S(1)}, u32[]{:S(2)}, u32[]{:S(2)}) async-start(f32[16,256,128]{2,1,0:T(8,128)} %copy-done), calls=%async_computation.1 | async-start | bytes 4194304 | tf_op jit(solution)/shard_map/all_to_all | solution.py:345
  82.8 1.6 copy-start.7
  84.4 1.6 copy-start.8
  86.0 1.0 copy-start.14
  87.1 1.0 copy-start.15
  120.9 1.3 copy-start.2
  122.3 1.3 copy-start.4
  123.6 1.0 copy-start.11
  131.2 1.6 copy-start.3
  132.8 1.6 copy-start.5
  151.0 24.8 %all-to-all-start.3 = ((f32[16,8,128]{2,1,0:T(8,128)}), f32[16,8,128]{2,1,0:T(8,128)S(1)}, u32[]{:S(2)}, u32[]{:S(2)}) async-start(f32[16,8,128]{2,1,0:T(8,128)} %broadcast_in_dim.34), calls=%async_computation.3 | async-start | bytes 131072 | tf_op jit(solution)/shard_map/all_to_all | solution.py:385
  158.6 2.2 %copy-start.1 = (f32[256,4096]{1,0:T(8,128)S(1)}, f32[256,4096]{1,0:T(8,128)}, u32[]{:S(2)}) copy-start(f32[256,4096]{1,0:T(8,128)} %get-tuple-element.17.sig_part_ref) | copy-start | bytes 12582916
  160.8 1.6 copy-start.9
  162.4 1.2 copy-start.12
  163.6 1.0 copy-start.16

commit v2 on v1

v2 whole, which is shorter than its diff:
```python
import math

import jax
import jax.numpy as jnp
from jax import lax
from jax.experimental import pallas as pl
from jax.experimental.pallas import tpu as pltpu
from jax.sharding import PartitionSpec as P

T = 256
H = 64
G = 8
D = 64
N = 128
PER = H // G
WIDE = PER * D
F32 = jnp.float32
BF16 = jnp.bfloat16
AT_ONCE = 2
MIB = 1024 * 1024


def split(x, parts):
    pieces = []
    for _ in range(parts):
        piece = x.astype(BF16)
        pieces.append(piece)
        x = x - piece.astype(F32)
    return pieces


def mm(a, b):
    return lax.dot_general(a, b, (((1,), (0,)), ((), ())), preferred_element_type=F32)


def mm_nt(a, b):
    return lax.dot_general(a, b, (((1,), (1,)), ((), ())), preferred_element_type=F32)


def mm_tn(a, b):
    return lax.dot_general(a, b, (((0,), (0,)), ((), ())), preferred_element_type=F32)


def rows_times_mask(rows, mask):
    n = rows.shape[0]
    out = mm(jnp.concatenate(split(rows, 3), axis=0), mask)
    return out[:n] + out[n : 2 * n] + out[2 * n :]


def mask_of(relation):
    i = lax.broadcasted_iota(jnp.int32, (T, T), 0)
    j = lax.broadcasted_iota(jnp.int32, (T, T), 1)
    return jnp.where(relation(i, j), 1.0, 0.0).astype(BF16)


def column_of(row, first, count):
    i = lax.broadcasted_iota(jnp.int32, (count, H), 0) + first
    j = lax.broadcasted_iota(jnp.int32, (count, H), 1)
    return jnp.sum(jnp.where(i == j, row, 0.0), axis=1, keepdims=True)


def steps_of(raw, bias, decay_log):
    pre_act = raw + bias
    step = jnp.maximum(pre_act, 0.0) + jnp.log1p(jnp.exp(-jnp.abs(pre_act)))
    decay = jnp.exp(decay_log)
    rate = -decay * step
    cumul = rows_times_mask(rate, mask_of(lambda i, j: i <= j))
    return pre_act, step, decay, cumul


def spread(rows):
    head = lax.broadcasted_iota(jnp.int32, (PER, WIDE), 0)
    column = lax.broadcasted_iota(jnp.int32, (PER, WIDE), 1)
    own = jnp.where(column // D == head, 1.0, 0.0).astype(BF16)
    return mm_tn(jnp.concatenate(split(rows, 3), axis=0), jnp.concatenate([own] * 3, axis=0))


def columns(rows):
    pad = jnp.zeros((128 - PER * len(rows), T), F32)
    return jnp.transpose(jnp.concatenate(list(rows) + [pad], axis=0))


def state_kernel(cot_ref, out_ref, raw_ref, decay_ref, bias_ref, sent_ref, entry_ref):
    step = pl.program_id(0)

    @pl.when(step == 0)
    def _():
        bias = column_of(bias_ref[...], 0, H)
        decay_log = column_of(decay_ref[...], 0, H)
        entry_ref[...] = jnp.exp(steps_of(raw_ref[...], bias, decay_log)[3])

    half = WIDE // 2
    for k in range(AT_ONCE):
        at = pl.multiple_of((step * AT_ONCE + k) * PER, PER)
        entry = entry_ref[pl.ds(at, PER), :]
        cot = jnp.transpose(cot_ref[:, k * WIDE : (k + 1) * WIDE]).astype(F32)
        weighted = (cot.reshape(PER, D, T) * entry[:, None, :]).reshape(WIDE, T)
        out_map = out_ref[:, k * N : (k + 1) * N]
        high, low = split(weighted, 2)
        state = mm(high, out_map) + mm(low, out_map)
        total = jnp.broadcast_to(entry[:, T - 1 :], (PER, N))
        sent_ref[2 * k, :half] = state[:half]
        sent_ref[2 * k + 1, :half] = state[half:]
        sent_ref[2 * k, half:] = total
        sent_ref[2 * k + 1, half:] = jnp.concatenate(
            [total[PER // 2 :], total[: PER // 2]], axis=0
        )


def scan_kernel(state_ref, total_ref, end_ref):
    head = pl.program_id(0)
    carry = jnp.zeros((D, N), F32)
    for b in reversed(range(state_ref.shape[0])):
        end_ref[b] = carry
        carry = state_ref[b] + total_ref[b, pl.ds(head, 1), :] * carry


def inner_kernel(
    sig_ref,
    cot_ref,
    in_ref,
    out_ref,
    raw_ref,
    decay_ref,
    bias_ref,
    skip_ref,
    start_ref,
    sig_grad_ref,
    in_grad_ref,
    out_grad_ref,
    step_grad_ref,
    by_decay_ref,
    by_bias_ref,
    sums_ref,
    carry_ref,
    leave_ref,
    slope_ref,
    sig_high_ref,
    sig_low_ref,
):
    head = pl.program_id(0) * PER
    bias = column_of(bias_ref[...], head, PER)
    decay_log = column_of(decay_ref[...], head, PER)
    pre_act, step, decay, cumul = steps_of(raw_ref[...], bias, decay_log)
    slope = jax.nn.sigmoid(pre_act)
    entry = jnp.exp(cumul)
    final = cumul[:, T - 1 :]
    total = jnp.exp(final)
    leave = jnp.exp(final - cumul)
    carry = leave * step
    carry_ref[...] = carry
    leave_ref[...] = leave
    slope_ref[...] = slope
    later = rows_times_mask(slope, mask_of(lambda i, j: i > j))
    cols = columns([cumul - jnp.log(step), entry])
    in_map = in_ref[...]
    out_map = out_ref[...]
    out_float = out_map.astype(F32)
    scores = mm_nt(in_map, out_map)
    valid = lax.broadcasted_iota(jnp.int32, (T, T), 0) <= lax.broadcasted_iota(jnp.int32, (T, T), 1)
    lane = lax.broadcasted_iota(jnp.int32, (T, N), 1)
    first = lane < D
    score_grad = jnp.zeros((T, T), F32)
    out_grad = jnp.zeros((T, N), F32)
    found = jnp.zeros((T, N), F32)
    row_sums = []
    for pair in range(PER // 2):
        at = slice(pair * N, (pair + 1) * N)
        sig = sig_ref[:, at]
        cot = cot_ref[:, at]
        zero = jnp.zeros_like(sig)
        sig_grad = jnp.zeros((T, N), F32)
        start = start_ref[at, :]
        top = lax.broadcasted_iota(jnp.int32, (N, N), 0) < D
        none = jnp.zeros_like(start)
        both = jnp.concatenate(
            [jnp.where(top, start, none), jnp.where(top, none, start)], axis=1
        )
        began = mm(cot, both)
        for k in range(2):
            j = 2 * pair + k
            mine = first if k == 0 else jnp.logical_not(first)
            own_sig = jnp.where(mine, sig, zero)
            own_cot = jnp.where(mine, cot, zero)
            mix_grad = mm_nt(own_sig, cot)
            fade = jnp.where(valid, jnp.exp(cumul[j : j + 1, :] - cols[:, j : j + 1]), 0.0)
            mixing = fade * scores
            high, low = split(mixing, 2)
            sig_grad = sig_grad + (mm(high, own_cot) + mm(low, own_cot))
            score_grad = score_grad + mix_grad * fade
            product = mix_grad * mixing
            row_sums.append(jnp.sum(product, axis=0, keepdims=True))
            found = jnp.where(lane == j, jnp.sum(product, axis=1, keepdims=True), found)
            own = began[:, k * N : (k + 1) * N]
            out_grad = out_grad + own * cols[:, PER + j : PER + j + 1]
            found = jnp.where(
                lane == PER + j, jnp.sum(own * out_float, axis=1, keepdims=True), found
            )
        sig_grad_ref[:, at] = sig_grad
    sig_float = sig_ref[...].astype(F32)
    cot_float = cot_ref[...].astype(F32)
    own = jnp.where(
        lax.broadcasted_iota(jnp.int32, (PER, WIDE), 1) // D
        == lax.broadcasted_iota(jnp.int32, (PER, WIDE), 0),
        1.0,
        0.0,
    )
    skip = jnp.sum(own * column_of(skip_ref[...], head, PER), axis=0, keepdims=True)
    sig_grad_ref[...] = sig_grad_ref[...] + skip * cot_float
    sig_high_ref[...], sig_low_ref[...] = split(sig_float * spread(carry), 2)
    high, low = split(score_grad, 2)
    in_grad_ref[...] = mm(high, out_map) + mm(low, out_map)
    out_grad_ref[...] = out_grad + (mm_tn(high, in_map) + mm_tn(low, in_map))
    found = jnp.transpose(found)
    col_sum = found[:PER]
    from_start = found[PER : 2 * PER]
    cumul_grad = jnp.concatenate(row_sums, axis=0) - col_sum + entry * from_start
    rate_grad = rows_times_mask(cumul_grad, mask_of(lambda i, j: i >= j))
    step_grad = col_sum / step - rate_grad * decay
    step_grad_ref[...] = step_grad
    into_decay = (final - cumul) * carry
    into_bias = leave * (slope - decay * step * later)
    start = start_ref[...].astype(F32).reshape(PER, D, N)
    for rows, weight, ref in (
        (into_decay, final * total, by_decay_ref),
        (into_bias, -decay * total * jnp.sum(slope, axis=1, keepdims=True), by_bias_ref),
    ):
        high, low = split(sig_float * spread(rows), 2)
        grown = mm_tn(high, in_map) + mm_tn(low, in_map)
        ref[...] = grown + (start * weight[:, :, None]).reshape(WIDE, N)
    skip_sum = jnp.sum(
        own * jnp.sum(sig_float * cot_float, axis=0, keepdims=True), axis=1, keepdims=True
    )
    decay_sum = -decay * jnp.sum(rate_grad * step, axis=1, keepdims=True)
    bias_sum = jnp.sum(step_grad * slope, axis=1, keepdims=True)
    which = lax.broadcasted_iota(jnp.int32, (PER, N), 1)
    sums = jnp.zeros((PER, N), F32)
    for k, column in enumerate((decay_sum, bias_sum, skip_sum, total, decay)):
        sums = jnp.where(which == k, column, sums)
    sums_ref[...] = sums


def sums_kernel(end_ref, by_decay_ref, by_bias_ref, sums_ref, sent_ref, kept):
    step = pl.program_id(0)
    heads = sums_ref.shape[0]
    end = end_ref[...]
    which = lax.broadcasted_iota(jnp.int32, (heads, N), 1)
    sums = sums_ref[...]
    for k, ref in enumerate((by_decay_ref, by_bias_ref)):
        partial = jnp.sum((end * ref[...]).reshape(heads, D, N), axis=1)
        sums = sums + jnp.where(which == k, jnp.sum(partial, axis=1, keepdims=True), 0.0)

    @pl.when(step == 0)
    def _():
        kept[...] = jnp.zeros_like(kept)

    kept[pl.ds(pl.multiple_of(step * heads, heads), heads), :] = sums

    @pl.when(step == pl.num_programs(0) - 1)
    def _():
        rows = jnp.transpose(kept[...])[:8]
        sent_ref[...] = jnp.broadcast_to(rows[None], sent_ref.shape)


def relay_kernel(received_ref, after_ref, sent_ref):
    summed = jnp.sum(received_ref[...], axis=0)
    sent_ref[...] = jnp.broadcast_to(summed[None], sent_ref.shape)


def signal_kernel(
    end_ref,
    sig_ref,
    in_ref,
    start_ref,
    sums_ref,
    carry_ref,
    leave_ref,
    slope_ref,
    sig_part_ref,
    step_part_ref,
    sig_grad_ref,
    step_grad_ref,
):
    own = jnp.where(
        lax.broadcasted_iota(jnp.int32, (PER, WIDE), 1) // D
        == lax.broadcasted_iota(jnp.int32, (PER, WIDE), 0),
        1.0,
        0.0,
    ).astype(BF16)
    earlier = mask_of(lambda i, j: i < j)
    for k in range(AT_ONCE):
        wide = slice(k * WIDE, (k + 1) * WIDE)
        head = slice(k * PER, (k + 1) * PER)
        end = end_ref[wide, :]
        in_map = in_ref[:, k * N : (k + 1) * N]
        carry = carry_ref[head, :]
        total = sums_ref[head, 3:4]
        decay = sums_ref[head, 4:5]
        end_high, end_low = split(end, 2)
        end_in = mm_nt(in_map, end_high) + mm_nt(in_map, end_low)
        sig_grad_ref[:, wide] = sig_part_ref[:, wide] + spread(carry) * end_in
        high, low = split(sig_ref[:, wide].astype(F32) * end_in, 2)
        pushed = mm_nt(own, high) + mm_nt(own, low)
        before = rows_times_mask(carry * pushed, earlier)
        held = jnp.sum((end * start_ref[wide, :].astype(F32)).reshape(PER, D, N), axis=1)
        held = total * jnp.sum(held, axis=1, keepdims=True)
        step_grad = step_part_ref[head, :] + leave_ref[head, :] * pushed - decay * (before + held)
        step_grad_ref[head, :] = step_grad * slope_ref[head, :]


def input_kernel(end_ref, sig_high_ref, sig_low_ref, in_part_ref, after_ref, in_grad_ref):
    for k in range(AT_ONCE):
        wide = slice(k * WIDE, (k + 1) * WIDE)
        cols = slice(k * N, (k + 1) * N)
        end_high, end_low = split(end_ref[wide, :], 2)
        high = sig_high_ref[:, wide]
        in_grad_ref[:, cols] = in_part_ref[:, cols] + (
            mm(high, end_high) + (mm(high, end_low) + mm(sig_low_ref[:, wide], end_high))
        )


def call(kernel, grid, ins, outs, args, flops, mib, scratch=()):
    moved = sum(a.size * a.dtype.itemsize for a in args)
    moved += sum(math.prod(s.shape) * s.dtype.itemsize for _, s in outs)
    return pl.pallas_call(
        kernel,
        grid=(grid,),
        in_specs=ins,
        out_specs=[spec for spec, _ in outs],
        out_shape=[shape for _, shape in outs],
        scratch_shapes=list(scratch),
        compiler_params=pltpu.CompilerParams(
            dimension_semantics=("arbitrary",), vmem_limit_bytes=mib * MIB
        ),
        cost_estimate=pl.CostEstimate(flops=flops, bytes_accessed=moved, transcendentals=0),
    )(*args)


def far(*arrays):
    return [pltpu.with_memory_space_constraint(a, pltpu.HBM) for a in arrays]


def near(*arrays):
    return [pltpu.with_memory_space_constraint(a, pltpu.VMEM) for a in arrays]


def f32(*shape):
    return pltpu.HBM(shape, F32)


def f32_near(*shape):
    return pltpu.VMEM(shape, F32)


WIDE_COLS = pl.BlockSpec((T, WIDE), lambda g: (0, g))
MAP_COLS = pl.BlockSpec((T, N), lambda g: (0, g))
HEAD_ROWS = pl.BlockSpec((PER, T), lambda g: (g, 0))
HEAD_LANES = pl.BlockSpec((PER, N), lambda g: (g, 0))
HEAD_ALL = pl.BlockSpec((1, H), lambda g: (0, 0))
HALF_ROWS = pl.BlockSpec((H * D // 2, N), lambda g: (g, 0))
STATE_ROWS = pl.BlockSpec((WIDE, N), lambda g: (g, 0))


def many(rows, cols):
    if rows == T:
        return pl.BlockSpec((rows, AT_ONCE * cols), lambda g: (0, g))
    return pl.BlockSpec((AT_ONCE * rows, cols), lambda g: (g, 0))


ELSEWHERE = pl.BlockSpec(memory_space=pl.ANY)


def local(
    signal, cotangent, input_map, output_map, step_raw, decay_log, step_bias, skip_gain, checkpoints
):
    sig, cot, in_map, out_map, raw = (
        signal[0],
        cotangent[0],
        input_map[0],
        output_map[0],
        step_raw[0],
    )
    decay_row, bias_row, skip_row = decay_log[None], step_bias[None], skip_gain[None]
    start = checkpoints.reshape(H * D, N)
    blocks = lax.axis_size("ctx")
    rows = H * D // blocks
    own = H // blocks

    sent = call(
        state_kernel,
        G // AT_ONCE,
        [
            pl.BlockSpec((T, AT_ONCE * WIDE), lambda g: (0, g)),
            pl.BlockSpec((T, AT_ONCE * N), lambda g: (0, g)),
            pl.BlockSpec((H, T), lambda g: (0, 0)),
            HEAD_ALL,
            HEAD_ALL,
        ],
        [
            (
                pl.BlockSpec((AT_ONCE * blocks // G, rows + 8, N), lambda g: (g, 0, 0)),
                f32(blocks, rows + 8, N),
            )
        ],
        far(cot, out_map, raw, decay_row, bias_row),
        4 * H * D * N * T,
        60,
        [pltpu.VMEM((H, T), F32)],
    )[0]
    states = lax.all_to_all(sent, "ctx", 0, 0)
    ends = call(
        scan_kernel,
        own,
        [
            pl.BlockSpec((blocks, D, N), lambda i: (0, i, 0)),
            pl.BlockSpec((blocks, 8, N), lambda i: (0, rows // 8, 0)),
        ],
        [(pl.BlockSpec((blocks, D, N), lambda i: (0, i, 0)), f32(blocks, rows, N))],
        (states, states),
        2 * H * D * N,
        16,
    )[0]
    end = lax.all_to_all(ends, "ctx", 0, 0).reshape(H * D, N)

    (
        sig_part,
        in_part,
        out_grad,
        step_part,
        by_decay,
        by_bias,
        sums,
        carry,
        leave,
        slope,
        sig_high,
        sig_low,
    ) = call(
        inner_kernel,
        G,
        [
            WIDE_COLS,
            WIDE_COLS,
            MAP_COLS,
            MAP_COLS,
            HEAD_ROWS,
            HEAD_ALL,
            HEAD_ALL,
            HEAD_ALL,
            STATE_ROWS,
        ],
        [
            (WIDE_COLS, f32(T, H * D)),
            (MAP_COLS, f32(T, G * N)),
            (MAP_COLS, f32(T, G * N)),
            (HEAD_ROWS, f32_near(H, T)),
            (STATE_ROWS, f32(H * D, N)),
            (STATE_ROWS, f32(H * D, N)),
            (HEAD_LANES, f32_near(H, N)),
            (HEAD_ROWS, f32_near(H, T)),
            (HEAD_ROWS, f32_near(H, T)),
            (HEAD_ROWS, f32_near(H, T)),
            (WIDE_COLS, pltpu.HBM((T, H * D), BF16)),
            (WIDE_COLS, pltpu.HBM((T, H * D), BF16)),
        ],
        far(sig, cot, in_map, out_map, raw, decay_row, bias_row, skip_row, start),
        H * T * T * N * 20,
        24,
    )

    sent = call(
        sums_kernel,
        2,
        [HALF_ROWS, HALF_ROWS, HALF_ROWS, pl.BlockSpec((H // 2, N), lambda g: (g, 0))],
        [(pl.BlockSpec((blocks, 8, N), lambda g: (0, 0, 0)), f32(blocks, 8, N))],
        near(end) + far(by_decay, by_bias) + near(sums),
        4 * H * D * N,
        24,
        [pltpu.VMEM((N, N), F32)],
    )[0]
    received = lax.all_to_all(sent, "ctx", 0, 0)
    sig_grad, step_grad = call(
        signal_kernel,
        G // AT_ONCE,
        [
            many(WIDE, N),
            many(T, WIDE),
            many(T, N),
            many(WIDE, N),
            many(PER, N),
            many(PER, T),
            many(PER, T),
            many(PER, T),
            many(T, WIDE),
            many(PER, T),
        ],
        [(many(T, WIDE), f32(T, H * D)), (many(PER, T), f32(H, T))],
        near(end)
        + far(sig, in_map, start)
        + near(sums, carry, leave, slope)
        + far(sig_part)
        + near(step_part),
        8 * H * D * N * T,
        32,
    )
    deals = lax.axis_size("dp")
    sent = call(
        relay_kernel,
        1,
        [pl.BlockSpec((blocks, 8, N), lambda i: (0, 0, 0)), ELSEWHERE],
        [(pl.BlockSpec((deals, 8, N), lambda i: (0, 0, 0)), f32(deals, 8, N))],
        [received] + far(step_grad),
        blocks * 8 * N,
        16,
    )[0]
    summed = jnp.sum(lax.all_to_all(sent, "dp", 0, 0), axis=0)
    summed = summed * (1.0 / (deals * blocks * T))
    in_grad = call(
        input_kernel,
        G // AT_ONCE,
        [many(WIDE, N), many(T, WIDE), many(T, WIDE), many(T, N), ELSEWHERE],
        [(many(T, N), f32(T, G * N))],
        near(end) + far(sig_high, sig_low, in_part, sent),
        6 * H * D * N * T,
        32,
    )[0]
    return (
        sig_grad[None],
        in_grad[None],
        out_grad[None],
        step_grad[None],
        summed[0, :H],
        summed[2, :H],
        summed[1, :H],
    )


def solution(mesh):
    rows = P("dp", "ctx", None)
    placed = (rows, rows, rows, rows, P("dp", None, "ctx"), P(), P(), P())
    return jax.shard_map(
        local,
        mesh=mesh,
        in_specs=placed + (P("dp", "ctx", None, None, None),),
        out_specs=(rows, rows, rows, P("dp", None, "ctx"), P(), P(), P()),
        check_vma=False,
    )
```

time: 177 us -> 158 us (0.89)
  local copies, waits for them, and re-layouts: 25.7 us -> 0.52 us
  blocking collectives: 78.5 us -> 64 us
  waiting for transfers between devices: 6.65 us -> 15.8 us
  starting transfers between devices: 12 us -> 17.8 us
  Pallas kernels: 52.7 us -> 58.5 us
    unnamed x40 -> x0, local copies, waits for them, and re-layouts: 22.9 us -> none
    all_to_all x1 -> x0, blocking collectives: 14.7 us -> none  [local(): summed = jnp.sum(lax.all_to_all(sent, 'ctx', 0, 0), axis=0)]
    all_to_all x1, waiting for transfers between devices: 6.65 us -> 14.6 us  [local(): end = lax.all_to_all(ends, 'ctx', 0, 0).reshape(H * D, N)]
    all_to_all x0 -> x1, starting transfers between devices: none -> 5.99 us  [local(): received = lax.all_to_all(sent, 'ctx', 0, 0)]
    pallas_call x5 -> x7, Pallas kernels: 52.7 us -> 58.5 us  [call(): pl.pallas_call(kernel, grid=(grid,), in_specs=ins, out_specs=[spec for sp...]
    broadcast_in_dim x4 -> x0, local copies, waits for them, and re-layouts: 2.19 us -> none  [the longest x2 1.49 us: local(): decay_col, bias_col = (decay_log[:, None], step_bias[:, None])]
  transfers between devices with their start and end apart: 2 -> 3, of which waited for: 1 -> 3; matrix products, arithmetic and copies ran while one was open for 0% -> 0% of each run, Pallas kernels for 25% -> 30%
where the time goes in v2:
time: 158 us; the launch traced here: 157 us
  blocking collectives  64 us (41%)
  Pallas kernels  58.5 us (37%)
  starting transfers between devices  17.8 us (11%)
  waiting for transfers between devices  15.8 us (10%)
    all_to_all x1, blocking collectives, local(): states = lax.all_to_all(sent, 'ctx', 0, 0)  64 us
    pallas_call x7, Pallas kernels, call(): pl.pallas_call(kernel, grid=(grid,), in_specs=ins, out_specs=[spec for sp...  58.5 us
    all_to_all x1, waiting for transfers between devices, local(): end = lax.all_to_all(ends, 'ctx', 0, 0).reshape(H * D, N)  14.6 us
    all_to_all x1, starting transfers between devices, local(): summed = jnp.sum(lax.all_to_all(sent, 'dp', 0, 0), axis=0)  7.61 us
    all_to_all x1, starting transfers between devices, local(): received = lax.all_to_all(sent, 'ctx', 0, 0)  5.99 us
    all_to_all x1, starting transfers between devices, local(): end = lax.all_to_all(ends, 'ctx', 0, 0).reshape(H * D, N)  4.23 us
  transfers between devices with their start and end apart: 3, of which 3 were waited for; matrix products, arithmetic and copies ran while one was open for 0% of the time, Pallas kernels for 30%

profile of v2, /device:TPU:1, one launch (start us, length us, event | category | flops | bytes accessed | tf_op | source)
XLA Modules:
  0.0 157.3 jit_solution(4582827312589759446)
XLA Ops:
  0.6 5.1 %shard_map.144 = f32[16,264,128]{2,1,0:T(8,128)} custom-call(bf16[256,4096]{1,0:T(8,128)(2,1)} %bitcast.25, bf16[256,1024]{1,0:T(8,128)(2,1)} %bitcast.32, f32[64,256]{1,0:T(8,128)} %bitcast.34, f32[1,64]{1,0:T(1,128)} %bitcast.37, f32[1,64]{1,0:T(1,128)} %bitcast.39), custom_call_target="tpu_custom_call" | custom-call | flops 536870912 | bytes 4850176 | tf_op jit(solution)/shard_map/pallas_call | solution.py:325
  5.8 64.0 %all_to_all.20.state_ref.total_ref = f32[16,264,128]{2,1,0:T(8,128)S(1)} all-to-all(f32[16,264,128]{2,1,0:T(8,128)} %shard_map.144), channel_id=1, replica_groups=mesh['dp'=16,'ctx'=16] {'ctx'}, dimensions={0} | all-to-all | bytes 4325376 | tf_op jit(solution)/shard_map/all_to_all | solution.py:410
  69.8 2.0 %shard_map.145 = f32[16,256,128]{2,1,0:T(8,128)} custom-call(f32[16,264,128]{2,1,0:T(8,128)S(1)} %all_to_all.20.state_ref.total_ref, f32[16,264,128]{2,1,0:T(8,128)S(1)} %all_to_all.20.state_ref.total_ref), custom_call_target="tpu_custom_call" | custom-call | flops 1048576 | bytes 6422528 | tf_op jit(solution)/shard_map/pallas_call | solution.py:325
  71.8 4.2 %all-to-all-start.1 = ((f32[16,256,128]{2,1,0:T(8,128)}), f32[16,256,128]{2,1,0:T(8,128)S(1)}, u32[]{:S(2)}, u32[]{:S(2)}) async-start(f32[16,256,128]{2,1,0:T(8,128)} %shard_map.145), calls=%async_computation.1 | async-start | bytes 4194304 | tf_op jit(solution)/shard_map/all_to_all | solution.py:423
  76.0 34.0 %shard_map.146 = (f32[256,4096]{1,0:T(8,128)}, f32[256,1024]{1,0:T(8,128)}, f32[256,1024]{1,0:T(8,128)}, f32[64,256]{1,0:T(8,128)S(1)}, f32[4096,128]{1,0:T(8,12...) custom-call(bf16[256,4096]{1,0:T(8,128)(2,1)} %bitcast.23, ...), custom_call_target="tpu_custom_call" | custom-call | flops 10737418240 | bytes 21332736 | tf_op jit(solution)/shard_map/pallas_call | solution.py:325
  110.1 14.6 %all-to-all-done.1 = f32[16,256,128]{2,1,0:T(8,128)S(1)} async-done(((f32[16,256,128]{2,1,0:T(8,128)}), f32[16,256,128]{2,1,0:T(8,128)S(1)}, u32[]{:S(2)}, u32[]{:S(2)}) %all-to-all-start.1) | async-done | bytes 2097184 | tf_op jit(solution)/shard_map/all_to_all | solution.py:423
  124.6 3.2 %shard_map.148 = f32[16,8,128]{2,1,0:T(8,128)} custom-call(f32[4096,128]{1,0:T(8,128)S(1)} %bitcast.20, f32[4096,128]{1,0:T(8,128)} %get-tuple-element.31.by_decay_ref, f32[4096,128]{1,0:T(8,128)} %get-tuple-element.32.by_bias_ref, f32[64,128]{1,0:T(8,128)S(1)} %get-tuple-element.21.sums_ref), custom_call_target="tpu_custom_call" | custom-call | flops 2097152 | bytes 6389760 | tf_op jit(solution)/shard_map/pallas_call | solution.py:325
  127.8 6.0 %all-to-all-start.2 = ((f32[16,8,128]{2,1,0:T(8,128)}), f32[16,8,128]{2,1,0:T(8,128)S(1)}, u32[]{:S(2)}, u32[]{:S(2)}) async-start(f32[16,8,128]{2,1,0:T(8,128)} %shard_map.148), calls=%async_computation.2 | async-start | bytes 131072 | tf_op jit(solution)/shard_map/all_to_all | solution.py:481
  133.8 8.3 %shard_map.147 = (f32[256,4096]{1,0:T(8,128)}, f32[64,256]{1,0:T(8,128)}) custom-call(f32[4096,128]{1,0:T(8,128)S(1)} %bitcast.21, bf16[256,4096]{1,0:T(8,128)(2,1)} %bitcast.24, bf16[256,1024]{1,0:T(8,128)(2,1)} %bitcast.31, bf16[4096,128]{1,0:T(8,128)(2,1)} %bitcast.28, f32[64,128]{1,0:T(8,128)S(1)} %get-tuple-element.21.sums_ref, ...), custom_call_target="tpu_custom_call" | custom-call | flops 1073741824 | bytes 14516224 | tf_op jit(solution)/shard_map/pallas_call | solution.py:325
  142.1 0.6 all-to-all-done.2.received_ref
  142.7 0.6 shard_map.149.after_ref
  143.4 7.6 %all-to-all-start.3 = ((f32[16,8,128]{2,1,0:T(8,128)}), f32[16,8,128]{2,1,0:T(8,128)S(1)}, u32[]{:S(2)}, u32[]{:S(2)}) async-start(f32[16,8,128]{2,1,0:T(8,128)} %shard_map.149.after_ref), calls=%async_computation.3 | async-start | bytes 131072 | tf_op jit(solution)/shard_map/all_to_all | solution.py:516
  151.0 5.2 %shard_map.150 = f32[256,1024]{1,0:T(8,128)} custom-call(f32[4096,128]{1,0:T(8,128)S(1)} %bitcast.22, bf16[256,4096]{1,0:T(8,128)(2,1)} %get-tuple-element.28.sig_high_ref, bf16[256,4096]{1,0:T(8,128)(2,1)} %get-tuple-element.29.sig_low_ref, f32[256,1024]{1,0:T(8,128)} %get-tuple-element.30.in_part_ref, f32[16,8,128]{2,1,0:T(8,128)} %shard_map.149.after_ref), custom_call_target="tpu_custom_call" | custom-call | flops 805306368 | bytes 8454144 | tf_op jit(solution)/shard_map/pallas_call | solution.py:325
  156.1 0.6 all-to-all-done.3
  156.8 0.5 slice_bitcast_fusion
  (2 shorter events, 0.0 us)
Async XLA Ops:
  71.8 52.8 %all-to-all-start.1 = ((f32[16,256,128]{2,1,0:T(8,128)}), f32[16,256,128]{2,1,0:T(8,128)S(1)}, u32[]{:S(2)}, u32[]{:S(2)}) async-start(f32[16,256,128]{2,1,0:T(8,128)} %shard_map.145), calls=%async_computation.1 | async-start | bytes 4194304 | tf_op jit(solution)/shard_map/all_to_all | solution.py:423
  127.8 14.9 %all-to-all-start.2 = ((f32[16,8,128]{2,1,0:T(8,128)}), f32[16,8,128]{2,1,0:T(8,128)S(1)}, u32[]{:S(2)}, u32[]{:S(2)}) async-start(f32[16,8,128]{2,1,0:T(8,128)} %shard_map.148), calls=%async_computation.2 | async-start | bytes 131072 | tf_op jit(solution)/shard_map/all_to_all | solution.py:481
  143.4 13.4 %all-to-all-start.3 = ((f32[16,8,128]{2,1,0:T(8,128)}), f32[16,8,128]{2,1,0:T(8,128)S(1)}, u32[]{:S(2)}, u32[]{:S(2)}) async-start(f32[16,8,128]{2,1,0:T(8,128)} %shard_map.149.after_ref), calls=%async_computation.3 | async-start | bytes 131072 | tf_op jit(solution)/shard_map/all_to_all | solution.py:516

commit v3 on v2

v3 whole, which is shorter than its diff:
```python
import math

import jax
import jax.numpy as jnp
from jax import lax
from jax.experimental import pallas as pl
from jax.experimental.pallas import tpu as pltpu
from jax.sharding import PartitionSpec as P

T = 256
H = 64
G = 8
D = 64
N = 128
PER = H // G
WIDE = PER * D
F32 = jnp.float32
BF16 = jnp.bfloat16
MIB = 1024 * 1024
STATE_BATCH = 4
SUMS_BATCH = 2
SIGNAL_BATCH = 3
INPUT_BATCH = 3


def split(x, parts):
    pieces = []
    for _ in range(parts):
        piece = x.astype(BF16)
        pieces.append(piece)
        x = x - piece.astype(F32)
    return pieces


def mm(a, b):
    return lax.dot_general(a, b, (((1,), (0,)), ((), ())), preferred_element_type=F32)


def mm_nt(a, b):
    return lax.dot_general(a, b, (((1,), (1,)), ((), ())), preferred_element_type=F32)


def mm_tn(a, b):
    return lax.dot_general(a, b, (((0,), (0,)), ((), ())), preferred_element_type=F32)


def rows_times_mask(rows, mask):
    n = rows.shape[0]
    out = mm(jnp.concatenate(split(rows, 3), axis=0), mask)
    return out[:n] + out[n : 2 * n] + out[2 * n :]


def mask_of(relation):
    i = lax.broadcasted_iota(jnp.int32, (T, T), 0)
    j = lax.broadcasted_iota(jnp.int32, (T, T), 1)
    return jnp.where(relation(i, j), 1.0, 0.0).astype(BF16)


def column_of(row, first, count):
    i = lax.broadcasted_iota(jnp.int32, (count, H), 0) + first
    j = lax.broadcasted_iota(jnp.int32, (count, H), 1)
    return jnp.sum(jnp.where(i == j, row, 0.0), axis=1, keepdims=True)


def steps_of(raw, bias, decay_log):
    pre_act = raw + bias
    step = jnp.maximum(pre_act, 0.0) + jnp.log1p(jnp.exp(-jnp.abs(pre_act)))
    decay = jnp.exp(decay_log)
    rate = -decay * step
    cumul = rows_times_mask(rate, mask_of(lambda i, j: i <= j))
    return pre_act, step, decay, cumul


def spread(rows):
    head = lax.broadcasted_iota(jnp.int32, (PER, WIDE), 0)
    column = lax.broadcasted_iota(jnp.int32, (PER, WIDE), 1)
    own = jnp.where(column // D == head, 1.0, 0.0).astype(BF16)
    return mm_tn(jnp.concatenate(split(rows, 3), axis=0), jnp.concatenate([own] * 3, axis=0))


def columns(rows):
    pad = jnp.zeros((128 - PER * len(rows), T), F32)
    return jnp.transpose(jnp.concatenate(list(rows) + [pad], axis=0))


def fetch(sems, pairs):
    copies = [pltpu.make_async_copy(a, b, sems.at[k]) for k, (a, b) in enumerate(pairs)]
    for copy in copies:
        copy.start()
    return copies


def batches(size):
    return [range(g, min(g + size, G)) for g in range(0, G, size)]


def wide(g):
    return pl.ds(g * WIDE, WIDE)


def narrow(g):
    return pl.ds(g * N, N)


def state_kernel(
    cot_ref,
    out_ref,
    raw_ref,
    decay_ref,
    bias_ref,
    sent_ref,
    cot,
    out,
    raw,
    decay,
    bias,
    got,
):
    half = WIDE // 2
    pairs = [(raw_ref, raw), (decay_ref, decay), (bias_ref, bias)]
    for g in range(G):
        pairs.append((cot_ref.at[:, wide(g)], cot.at[:, wide(g)]))
        pairs.append((out_ref.at[:, narrow(g)], out.at[:, narrow(g)]))
    copies = fetch(got, pairs)
    for copy in copies[:3]:
        copy.wait()
    bias_column = column_of(bias[...], 0, H)
    decay_log = column_of(decay[...], 0, H)
    entries = jnp.exp(steps_of(raw[...], bias_column, decay_log)[3])
    for batch in batches(STATE_BATCH):
        for g in batch:
            copies[2 * g + 3].wait()
            copies[2 * g + 4].wait()
        for g in batch:
            entry = entries[g * PER : (g + 1) * PER]
            turned = jnp.transpose(cot[:, wide(g)]).astype(F32)
            weighted = (turned.reshape(PER, D, T) * entry[:, None, :]).reshape(WIDE, T)
            out_map = out[:, narrow(g)]
            high, low = split(weighted, 2)
            state = mm(high, out_map) + mm(low, out_map)
            total = jnp.broadcast_to(entry[:, T - 1 :], (PER, N))
            sent_ref[2 * g, :half] = state[:half]
            sent_ref[2 * g + 1, :half] = state[half:]
            sent_ref[2 * g, half:] = total
            sent_ref[2 * g + 1, half:] = jnp.concatenate(
                [total[PER // 2 :], total[: PER // 2]], axis=0
            )


def scan_kernel(state_ref, end_ref, end, gone):
    blocks, rows, _ = end.shape
    leaving = []
    for h in range(rows // D):
        at = pl.ds(h * D, D)
        carry = jnp.zeros((D, N), F32)
        for b in reversed(range(blocks)):
            end[b, at, :] = carry
            carry = state_ref[b, at, :] + state_ref[b, rows + h : rows + h + 1, :] * carry
        leaving.append(pltpu.make_async_copy(end.at[:, at], end_ref.at[:, at], gone.at[h]))
        leaving[-1].start()
    for copy in leaving:
        copy.wait()


def inner_kernel(
    sig_ref,
    cot_ref,
    in_ref,
    out_ref,
    raw_ref,
    decay_ref,
    bias_ref,
    skip_ref,
    start_ref,
    sig_grad_ref,
    in_grad_ref,
    out_grad_ref,
    step_grad_ref,
    by_decay_ref,
    by_bias_ref,
    sums_ref,
    carry_ref,
    leave_ref,
    slope_ref,
    sig_high_ref,
    sig_low_ref,
    sig_turned_ref,
):
    head = pl.program_id(0) * PER
    bias = column_of(bias_ref[...], head, PER)
    decay_log = column_of(decay_ref[...], head, PER)
    pre_act, step, decay, cumul = steps_of(raw_ref[...], bias, decay_log)
    slope = jax.nn.sigmoid(pre_act)
    entry = jnp.exp(cumul)
    final = cumul[:, T - 1 :]
    total = jnp.exp(final)
    leave = jnp.exp(final - cumul)
    carry = leave * step
    carry_ref[...] = carry
    leave_ref[...] = leave
    slope_ref[...] = slope
    later = rows_times_mask(slope, mask_of(lambda i, j: i > j))
    cols = columns([cumul - jnp.log(step), entry])
    in_map = in_ref[...]
    out_map = out_ref[...]
    out_float = out_map.astype(F32)
    scores = mm_nt(in_map, out_map)
    valid = lax.broadcasted_iota(jnp.int32, (T, T), 0) <= lax.broadcasted_iota(jnp.int32, (T, T), 1)
    lane = lax.broadcasted_iota(jnp.int32, (T, N), 1)
    first = lane < D
    score_grad = jnp.zeros((T, T), F32)
    out_grad = jnp.zeros((T, N), F32)
    found = jnp.zeros((T, N), F32)
    row_sums = []
    for pair in range(PER // 2):
        at = slice(pair * N, (pair + 1) * N)
        sig = sig_ref[:, at]
        cot = cot_ref[:, at]
        zero = jnp.zeros_like(sig)
        sig_grad = jnp.zeros((T, N), F32)
        start = start_ref[at, :]
        top = lax.broadcasted_iota(jnp.int32, (N, N), 0) < D
        none = jnp.zeros_like(start)
        both = jnp.concatenate(
            [jnp.where(top, start, none), jnp.where(top, none, start)], axis=1
        )
        began = mm(cot, both)
        for k in range(2):
            j = 2 * pair + k
            mine = first if k == 0 else jnp.logical_not(first)
            own_sig = jnp.where(mine, sig, zero)
            own_cot = jnp.where(mine, cot, zero)
            mix_grad = mm_nt(own_sig, cot)
            fade = jnp.where(valid, jnp.exp(cumul[j : j + 1, :] - cols[:, j : j + 1]), 0.0)
            mixing = fade * scores
            high, low = split(mixing, 2)
            sig_grad = sig_grad + (mm(high, own_cot) + mm(low, own_cot))
            score_grad = score_grad + mix_grad * fade
            product = mix_grad * mixing
            row_sums.append(jnp.sum(product, axis=0, keepdims=True))
            found = jnp.where(lane == j, jnp.sum(product, axis=1, keepdims=True), found)
            own = began[:, k * N : (k + 1) * N]
            out_grad = out_grad + own * cols[:, PER + j : PER + j + 1]
            found = jnp.where(
                lane == PER + j, jnp.sum(own * out_float, axis=1, keepdims=True), found
            )
        sig_grad_ref[:, at] = sig_grad
    sig_float = sig_ref[...].astype(F32)
    cot_float = cot_ref[...].astype(F32)
    own = jnp.where(
        lax.broadcasted_iota(jnp.int32, (PER, WIDE), 1) // D
        == lax.broadcasted_iota(jnp.int32, (PER, WIDE), 0),
        1.0,
        0.0,
    )
    skip = jnp.sum(own * column_of(skip_ref[...], head, PER), axis=0, keepdims=True)
    sig_grad_ref[...] = sig_grad_ref[...] + skip * cot_float
    sig_turned_ref[...] = jnp.transpose(sig_ref[...])
    sig_high_ref[...], sig_low_ref[...] = split(sig_float * spread(carry), 2)
    high, low = split(score_grad, 2)
    in_grad_ref[...] = mm(high, out_map) + mm(low, out_map)
    out_grad_ref[...] = out_grad + (mm_tn(high, in_map) + mm_tn(low, in_map))
    found = jnp.transpose(found)
    col_sum = found[:PER]
    from_start = found[PER : 2 * PER]
    cumul_grad = jnp.concatenate(row_sums, axis=0) - col_sum + entry * from_start
    rate_grad = rows_times_mask(cumul_grad, mask_of(lambda i, j: i >= j))
    step_grad = col_sum / step - rate_grad * decay
    step_grad_ref[...] = step_grad
    into_decay = (final - cumul) * carry
    into_bias = leave * (slope - decay * step * later)
    start = start_ref[...].astype(F32).reshape(PER, D, N)
    for rows, weight, ref in (
        (into_decay, final * total, by_decay_ref),
        (into_bias, -decay * total * jnp.sum(slope, axis=1, keepdims=True), by_bias_ref),
    ):
        high, low = split(sig_float * spread(rows), 2)
        grown = mm_tn(high, in_map) + mm_tn(low, in_map)
        ref[...] = grown + (start * weight[:, :, None]).reshape(WIDE, N)
    skip_sum = jnp.sum(
        own * jnp.sum(sig_float * cot_float, axis=0, keepdims=True), axis=1, keepdims=True
    )
    decay_sum = -decay * jnp.sum(rate_grad * step, axis=1, keepdims=True)
    bias_sum = jnp.sum(step_grad * slope, axis=1, keepdims=True)
    which = lax.broadcasted_iota(jnp.int32, (PER, N), 1)
    sums = jnp.zeros((PER, N), F32)
    for k, column in enumerate((decay_sum, bias_sum, skip_sum, total, decay)):
        sums = jnp.where(which == k, column, sums)
    sums_ref[...] = sums


def sums_kernel(
    end_ref, sums_ref, by_decay_ref, by_bias_ref, sent_ref, by_decay, by_bias, kept, got
):
    pairs = []
    for g in range(0, G, SUMS_BATCH):
        at = pl.ds(g * WIDE, SUMS_BATCH * WIDE)
        pairs.append((by_decay_ref.at[at], by_decay.at[at]))
        pairs.append((by_bias_ref.at[at], by_bias.at[at]))
    copies = fetch(got, pairs)
    which = lax.broadcasted_iota(jnp.int32, (PER, N), 1)
    kept[...] = jnp.zeros_like(kept)
    for g in range(G):
        if g % SUMS_BATCH == 0:
            copies[2 * (g // SUMS_BATCH)].wait()
            copies[2 * (g // SUMS_BATCH) + 1].wait()
        end = end_ref[wide(g), :]
        sums = sums_ref[g * PER : (g + 1) * PER, :]
        for k, held in enumerate((by_decay, by_bias)):
            partial = jnp.sum((end * held[wide(g), :]).reshape(PER, D, N), axis=1)
            sums = sums + jnp.where(which == k, jnp.sum(partial, axis=1, keepdims=True), 0.0)
        kept[g * PER : (g + 1) * PER, :] = sums
    rows = jnp.transpose(kept[...])
    first = jnp.concatenate([rows[0:1, :H], rows[1:2, :H]], axis=1)
    odd = lax.broadcasted_iota(jnp.int32, (8, N), 0) % 2 == 1
    both = jnp.where(odd, rows[2:3], first)
    sent_ref[...] = jnp.broadcast_to(both[None], sent_ref.shape)


def signal_kernel(
    end_ref,
    sums_ref,
    carry_ref,
    leave_ref,
    slope_ref,
    step_part_ref,
    sig_turned_ref,
    in_ref,
    start_ref,
    sig_part_ref,
    step_grad_ref,
    sig_grad_ref,
    sig_turned,
    in_maps,
    start,
    sig_part,
    sig_grad,
    step_grads,
    got,
    gone,
):
    pairs = []
    for g in range(G):
        pairs.append((in_ref.at[:, narrow(g)], in_maps.at[:, narrow(g)]))
        pairs.append((sig_turned_ref.at[wide(g)], sig_turned.at[wide(g)]))
        pairs.append((start_ref.at[wide(g)], start.at[wide(g)]))
        pairs.append((sig_part_ref.at[:, wide(g)], sig_part.at[:, wide(g)]))
    copies = fetch(got, pairs)
    earlier = mask_of(lambda i, j: i < j)
    leaving = []
    for batch in batches(SIGNAL_BATCH):
        for g in batch:
            for copy in copies[4 * g : 4 * g + 4]:
                copy.wait()
        for g in batch:
            head = slice(g * PER, (g + 1) * PER)
            end = end_ref[wide(g), :]
            in_map = in_maps[:, narrow(g)]
            carry = carry_ref[head, :]
            total = sums_ref[head, 3:4]
            decay = sums_ref[head, 4:5]
            in_twice = jnp.concatenate([in_map, in_map], axis=1)
            pieces = jnp.concatenate(split(end, 2), axis=1)
            sig_grad[:, wide(g)] = sig_part[:, wide(g)] + spread(carry) * mm_nt(in_twice, pieces)
            turned = mm_nt(pieces, in_twice)
            pushed = (sig_turned[wide(g), :].astype(F32) * turned).reshape(PER, D, T)
            pushed = jnp.sum(pushed, axis=1)
            before = rows_times_mask(carry * pushed, earlier)
            held = jnp.sum((end * start[wide(g), :].astype(F32)).reshape(PER, D, N), axis=1)
            held = total * jnp.sum(held, axis=1, keepdims=True)
            step_grad = leave_ref[head, :] * pushed - decay * (before + held)
            step_grads[head, :] = (step_part_ref[head, :] + step_grad) * slope_ref[head, :]
        at = pl.ds(batch[0] * WIDE, len(batch) * WIDE)
        leaving.append(
            pltpu.make_async_copy(sig_grad.at[:, at], sig_grad_ref.at[:, at], gone.at[batch[0]])
        )
        leaving[-1].start()
    leaving.append(pltpu.make_async_copy(step_grads, step_grad_ref, gone.at[G]))
    leaving[-1].start()
    for copy in leaving:
        copy.wait()


def input_kernel(
    end_ref,
    sig_high_ref,
    sig_low_ref,
    in_part_ref,
    in_grad_ref,
    sig_high,
    sig_low,
    in_part,
    in_grad,
    got,
    gone,
):
    pairs = []
    for g in range(G):
        pairs.append((sig_high_ref.at[:, wide(g)], sig_high.at[:, wide(g)]))
        pairs.append((sig_low_ref.at[:, wide(g)], sig_low.at[:, wide(g)]))
        pairs.append((in_part_ref.at[:, narrow(g)], in_part.at[:, narrow(g)]))
    copies = fetch(got, pairs)
    leaving = []
    for batch in batches(INPUT_BATCH):
        for g in batch:
            for copy in copies[3 * g : 3 * g + 3]:
                copy.wait()
        for g in batch:
            end_high, end_low = split(end_ref[wide(g), :], 2)
            both = mm(sig_high[:, wide(g)], jnp.concatenate([end_high, end_low], axis=1))
            in_grad[:, narrow(g)] = in_part[:, narrow(g)] + (
                both[:, :N] + (both[:, N:] + mm(sig_low[:, wide(g)], end_high))
            )
        at = pl.ds(batch[0] * N, len(batch) * N)
        leaving.append(
            pltpu.make_async_copy(in_grad.at[:, at], in_grad_ref.at[:, at], gone.at[batch[0]])
        )
        leaving[-1].start()
    for copy in leaving:
        copy.wait()


def call(kernel, grid, ins, outs, args, flops, mib, scratch=()):
    moved = sum(a.size * a.dtype.itemsize for a in args)
    moved += sum(math.prod(s.shape) * s.dtype.itemsize for _, s in outs)
    return pl.pallas_call(
        kernel,
        grid=(grid,) if grid else (),
        in_specs=ins,
        out_specs=[spec for spec, _ in outs],
        out_shape=[shape for _, shape in outs],
        scratch_shapes=list(scratch),
        compiler_params=pltpu.CompilerParams(
            dimension_semantics=("arbitrary",) if grid else None, vmem_limit_bytes=mib * MIB
        ),
        cost_estimate=pl.CostEstimate(flops=flops, bytes_accessed=moved, transcendentals=0),
    )(*args)


def far(*arrays):
    return [pltpu.with_memory_space_constraint(a, pltpu.HBM) for a in arrays]


def near(*arrays):
    return [pltpu.with_memory_space_constraint(a, pltpu.VMEM) for a in arrays]


def f32(*shape):
    return pltpu.HBM(shape, F32)


def bf16(*shape):
    return pltpu.HBM(shape, BF16)


def f32_near(*shape):
    return pltpu.VMEM(shape, F32)


WIDE_COLS = pl.BlockSpec((T, WIDE), lambda g: (0, g))
MAP_COLS = pl.BlockSpec((T, N), lambda g: (0, g))
HEAD_ROWS = pl.BlockSpec((PER, T), lambda g: (g, 0))
HEAD_LANES = pl.BlockSpec((PER, N), lambda g: (g, 0))
HEAD_ALL = pl.BlockSpec((1, H), lambda g: (0, 0))
STATE_COLS = pl.BlockSpec((WIDE, T), lambda g: (g, 0))
STATE_ROWS = pl.BlockSpec((WIDE, N), lambda g: (g, 0))


ELSEWHERE = pl.BlockSpec(memory_space=pl.ANY)
HERE = pl.BlockSpec(memory_space=pltpu.VMEM)
COPIES = pltpu.SemaphoreType.DMA


def send_states(cot, out_map, raw, decay_row, bias_row, blocks):
    rows = H * D // blocks + 8
    return call(
        state_kernel,
        0,
        [ELSEWHERE] * 5,
        [(HERE, f32_near(blocks, rows, N))],
        far(cot, out_map, raw, decay_row, bias_row),
        4 * H * D * N * T,
        24,
        [
            pltpu.VMEM((T, H * D), BF16),
            pltpu.VMEM((T, G * N), BF16),
            pltpu.VMEM((H, T), F32),
            pltpu.VMEM((1, H), F32),
            pltpu.VMEM((1, H), F32),
            COPIES((2 * G + 3,)),
        ],
    )[0]


def scan_states(states):
    blocks, rows, _ = states.shape
    rows -= 8
    return call(
        scan_kernel,
        0,
        [HERE],
        [(ELSEWHERE, f32(blocks, rows, N))],
        near(states),
        2 * H * D * N,
        16,
        [pltpu.VMEM((blocks, rows, N), F32), COPIES((rows // D,))],
    )[0]


def inner_part(sig, cot, in_map, out_map, raw, decay_row, bias_row, skip_row, start):
    return call(
        inner_kernel,
        G,
        [
            WIDE_COLS,
            WIDE_COLS,
            MAP_COLS,
            MAP_COLS,
            HEAD_ROWS,
            HEAD_ALL,
            HEAD_ALL,
            HEAD_ALL,
            STATE_ROWS,
        ],
        [
            (WIDE_COLS, f32(T, H * D)),
            (MAP_COLS, f32(T, G * N)),
            (MAP_COLS, f32(T, G * N)),
            (HEAD_ROWS, f32_near(H, T)),
            (STATE_ROWS, f32(H * D, N)),
            (STATE_ROWS, f32(H * D, N)),
            (HEAD_LANES, f32_near(H, N)),
            (HEAD_ROWS, f32_near(H, T)),
            (HEAD_ROWS, f32_near(H, T)),
            (HEAD_ROWS, f32_near(H, T)),
            (WIDE_COLS, bf16(T, H * D)),
            (WIDE_COLS, bf16(T, H * D)),
            (STATE_COLS, bf16(H * D, T)),
        ],
        far(sig, cot, in_map, out_map, raw, decay_row, bias_row, skip_row, start),
        H * T * T * N * 20,
        24,
    )


def send_sums(end, by_decay, by_bias, sums, devices):
    return call(
        sums_kernel,
        0,
        [HERE, HERE, ELSEWHERE, ELSEWHERE],
        [(HERE, f32_near(devices // 4, 8, N))],
        near(end, sums) + far(by_decay, by_bias),
        4 * H * D * N,
        16,
        [
            pltpu.VMEM((H * D, N), F32),
            pltpu.VMEM((H * D, N), F32),
            pltpu.VMEM((N, N), F32),
            COPIES((2 * (G // SUMS_BATCH),)),
        ],
    )[0].reshape(devices, 2, N)


def signal_part(end, sig_turned, in_map, start, sums, carry, leave, slope, sig_part, step_part):
    step_grad, sig_grad = call(
        signal_kernel,
        0,
        [HERE] * 6 + [ELSEWHERE] * 4,
        [(ELSEWHERE, f32(H, T)), (ELSEWHERE, f32(T, H * D))],
        near(end, sums, carry, leave, slope, step_part) + far(sig_turned, in_map, start, sig_part),
        8 * H * D * N * T,
        28,
        [
            pltpu.VMEM((H * D, T), BF16),
            pltpu.VMEM((T, G * N), BF16),
            pltpu.VMEM((H * D, N), BF16),
            pltpu.VMEM((T, H * D), F32),
            pltpu.VMEM((T, H * D), F32),
            pltpu.VMEM((H, T), F32),
            COPIES((4 * G,)),
            COPIES((G + 1,)),
        ],
    )
    return sig_grad, step_grad


def input_part(end, sig_high, sig_low, in_part):
    return call(
        input_kernel,
        0,
        [HERE] + [ELSEWHERE] * 3,
        [(ELSEWHERE, f32(T, G * N))],
        near(end) + far(sig_high, sig_low, in_part),
        6 * H * D * N * T,
        20,
        [
            pltpu.VMEM((T, H * D), BF16),
            pltpu.VMEM((T, H * D), BF16),
            pltpu.VMEM((T, G * N), F32),
            pltpu.VMEM((T, G * N), F32),
            COPIES((3 * G,)),
            COPIES((G,)),
        ],
    )[0]


def local(
    signal, cotangent, input_map, output_map, step_raw, decay_log, step_bias, skip_gain, checkpoints
):
    sig, cot, in_map, out_map, raw = (
        signal[0],
        cotangent[0],
        input_map[0],
        output_map[0],
        step_raw[0],
    )
    decay_row, bias_row, skip_row = decay_log[None], step_bias[None], skip_gain[None]
    start = checkpoints.reshape(H * D, N)
    blocks, deals = lax.axis_size("ctx"), lax.axis_size("dp")

    sent = send_states(cot, out_map, raw, decay_row, bias_row, blocks)
    ends = scan_states(lax.all_to_all(sent, "ctx", 0, 0))
    end = lax.all_to_all(ends, "ctx", 0, 0).reshape(H * D, N)
    (
        sig_part,
        in_part,
        out_grad,
        step_part,
        by_decay,
        by_bias,
        sums,
        carry,
        leave,
        slope,
        sig_high,
        sig_low,
        sig_turned,
    ) = inner_part(sig, cot, in_map, out_map, raw, decay_row, bias_row, skip_row, start)

    devices = blocks * deals
    sent = send_sums(end, by_decay, by_bias, sums, devices)
    received = lax.all_to_all(sent, ("dp", "ctx"), 0, 0)
    sig_grad, step_grad = signal_part(
        end, sig_turned, in_map, start, sums, carry, leave, slope, sig_part, step_part
    )
    in_grad = input_part(end, sig_high, sig_low, in_part)
    summed = jnp.sum(received, axis=0) * (1.0 / (devices * T))
    return (
        sig_grad[None],
        in_grad[None],
        out_grad[None],
        step_grad[None],
        summed[0, :H],
        summed[1, :H],
        summed[0, H:],
    )


def solution(mesh):
    rows = P("dp", "ctx", None)
    placed = (rows, rows, rows, rows, P("dp", None, "ctx"), P(), P(), P())
    return jax.shard_map(
        local,
        mesh=mesh,
        in_specs=placed + (P("dp", "ctx", None, None, None),),
        out_specs=(rows, rows, rows, P("dp", None, "ctx"), P(), P(), P()),
        check_vma=False,
    )
```

time: 158 us -> 153 us (0.968)
  Pallas kernels: 58.5 us -> 52.2 us
  waiting for transfers between devices: 15.8 us -> 19.7 us
  starting transfers between devices: 17.8 us -> 15.3 us
    pallas_call x7 -> x6, Pallas kernels: 58.5 us -> 52.2 us  [call(): pl.pallas_call(kernel, grid=(grid,) if grid else (), in_specs=ins, out_sp...]
    all_to_all x2 -> x1, waiting for transfers between devices: 1.21 us -> 5.47 us  [local(): received = lax.all_to_all(sent, ('dp', 'ctx'), 0, 0)]
    all_to_all x2 -> x1, starting transfers between devices: 13.6 us -> 11.1 us  [local(): received = lax.all_to_all(sent, ('dp', 'ctx'), 0, 0)]
  transfers between devices with their start and end apart: 3 -> 2, of which waited for: 3 -> 2; matrix products, arithmetic and copies ran while one was open for 0% -> 0% of each run, Pallas kernels for 30% -> 29%
where the time goes in v3:
time: 153 us
  blocking collectives  63.8 us (42%)
  Pallas kernels  52.2 us (34%)
  waiting for transfers between devices  19.7 us (13%)
  starting transfers between devices  15.3 us (10%)
    all_to_all x1, blocking collectives, local(): ends = scan_states(lax.all_to_all(sent, 'ctx', 0, 0))  63.8 us
    pallas_call x6, Pallas kernels, call(): pl.pallas_call(kernel, grid=(grid,) if grid else (), in_specs=ins, out_sp...  52.2 us
    all_to_all x1, waiting for transfers between devices, local(): end = lax.all_to_all(ends, 'ctx', 0, 0).reshape(H * D, N)  14.3 us
    all_to_all x1, starting transfers between devices, local(): received = lax.all_to_all(sent, ('dp', 'ctx'), 0, 0)  11.1 us
    all_to_all x1, waiting for transfers between devices, local(): received = lax.all_to_all(sent, ('dp', 'ctx'), 0, 0)  5.47 us
    all_to_all x1, starting transfers between devices, local(): end = lax.all_to_all(ends, 'ctx', 0, 0).reshape(H * D, N)  4.24 us
  transfers between devices with their start and end apart: 2, of which 2 were waited for; matrix products, arithmetic and copies ran while one was open for 0% of the time, Pallas kernels for 29%

profile of v3, /device:TPU:1, one launch (start us, length us, event | category | flops | bytes accessed | tf_op | source)
XLA Modules:
  0.0 152.6 jit_solution(6096949485407105527)
XLA Ops:
  0.6 3.1 %shard_map.144 = f32[16,264,128]{2,1,0:T(8,128)S(1)} custom-call(bf16[256,4096]{1,0:T(8,128)(2,1)} %bitcast.24, bf16[256,1024]{1,0:T(8,128)(2,1)} %bitcast.31, f32[64,256]{1,0:T(8,128)} %bitcast.33, f32[1,64]{1,0:T(1,128)} %bitcast.35, f32[1,64]{1,0:T(1,128)} %bitcast.37), custom_call_target="tpu_custom_call" | custom-call | flops 536870912 | bytes 4850176 | tf_op jit(solution)/shard_map/pallas_call | solution.py:426
  3.8 63.8 %all_to_all.15.state_ref = f32[16,264,128]{2,1,0:T(8,128)S(1)} all-to-all(f32[16,264,128]{2,1,0:T(8,128)S(1)} %shard_map.144), channel_id=1, replica_groups=mesh['dp'=16,'ctx'=16] {'ctx'}, dimensions={0} | all-to-all | bytes 4325376 | tf_op jit(solution)/shard_map/all_to_all | solution.py:622
  67.6 1.4 shard_map.145
  69.0 4.2 %all-to-all-start.1 = ((f32[16,256,128]{2,1,0:T(8,128)}), f32[16,256,128]{2,1,0:T(8,128)S(1)}, u32[]{:S(2)}, u32[]{:S(2)}) async-start(f32[16,256,128]{2,1,0:T(8,128)} %shard_map.145), calls=%async_computation.1 | async-start | bytes 4194304 | tf_op jit(solution)/shard_map/all_to_all | solution.py:623
  73.2 34.3 %shard_map.146 = (f32[256,4096]{1,0:T(8,128)}, f32[256,1024]{1,0:T(8,128)}, f32[256,1024]{1,0:T(8,128)}, f32[64,256]{1,0:T(8,128)S(1)}, f32[4096,128]{1,0:T(8,12...) custom-call(bf16[256,4096]{1,0:T(8,128)(2,1)} %bitcast.40, ...), custom_call_target="tpu_custom_call" | custom-call | flops 10737418240 | bytes 23429888 | tf_op jit(solution)/shard_map/pallas_call | solution.py:426
  107.5 14.3 %all-to-all-done.1 = f32[16,256,128]{2,1,0:T(8,128)S(1)} async-done(((f32[16,256,128]{2,1,0:T(8,128)}), f32[16,256,128]{2,1,0:T(8,128)S(1)}, u32[]{:S(2)}, u32[]{:S(2)}) %all-to-all-start.1) | async-done | bytes 2097184 | tf_op jit(solution)/shard_map/all_to_all | solution.py:623
  121.8 3.3 %shard_map.149 = f32[64,8,128]{2,1,0:T(8,128)} custom-call(f32[4096,128]{1,0:T(8,128)S(1)} %bitcast.21, f32[64,128]{1,0:T(8,128)S(1)} %get-tuple-element.22.sums_ref, f32[4096,128]{1,0:T(8,128)} %get-tuple-element.35.by_decay_ref, f32[4096,128]{1,0:T(8,128)} %get-tuple-element.36.by_bias_ref), custom_call_target="tpu_custom_call" | custom-call | flops 2097152 | bytes 6586368 | tf_op jit(solution)/shard_map/pallas_call | solution.py:426
  125.1 11.1 %all-to-all-start.2 = ((f32[256,2,128]{2,1,0:T(2,128)}), f32[256,2,128]{2,1,0:T(2,128)S(1)}, u32[]{:S(2)}, u32[]{:S(2)}) async-start(f32[256,2,128]{2,1,0:T(2,128)} %bitcast.14), calls=%async_computation.2 | async-start | bytes 524288 | tf_op jit(solution)/shard_map/all_to_all | solution.py:642
  136.1 4.1 %shard_map.148 = f32[256,1024]{1,0:T(8,128)} custom-call(f32[4096,128]{1,0:T(8,128)S(1)} %bitcast.22, bf16[256,4096]{1,0:T(8,128)(2,1)} %get-tuple-element.30.sig_high_ref, bf16[256,4096]{1,0:T(8,128)(2,1)} %get-tuple-element.31.sig_low_ref, f32[256,1024]{1,0:T(8,128)} %get-tuple-element.32.in_part_ref), custom_call_target="tpu_custom_call" | custom-call | flops 805306368 | bytes 8388608 | tf_op jit(solution)/shard_map/pallas_call | solution.py:426
  140.3 6.0 %shard_map.147 = (f32[64,256]{1,0:T(8,128)}, f32[256,4096]{1,0:T(8,128)}) custom-call(f32[4096,128]{1,0:T(8,128)S(1)} %bitcast.23, f32[64,128]{1,0:T(8,128)S(1)} %get-tuple-element.22.sums_ref, f32[64,256]{1,0:T(8,128)S(1)} %get-tuple-element.23.carry_ref, f32[64,256]{1,0:T(8,128)S(1)} %get-tuple-element.24.leave_ref, ...), custom_call_target="tpu_custom_call" | custom-call | flops 1073741824 | bytes 14516224 | tf_op jit(solution)/shard_map/pallas_call | solution.py:426
  146.3 5.5 %all-to-all-done.2 = f32[256,2,128]{2,1,0:T(2,128)S(1)} async-done(((f32[256,2,128]{2,1,0:T(2,128)}), f32[256,2,128]{2,1,0:T(2,128)S(1)}, u32[]{:S(2)}, u32[]{:S(2)}) %all-to-all-start.2) | async-done | bytes 262176 | tf_op jit(solution)/shard_map/all_to_all | solution.py:642
  151.8 0.3 reduce_sum.9
  152.0 0.6 slice_bitcast_fusion
  (1 shorter events, 0.0 us)
Async XLA Ops:
  69.0 52.8 %all-to-all-start.1 = ((f32[16,256,128]{2,1,0:T(8,128)}), f32[16,256,128]{2,1,0:T(8,128)S(1)}, u32[]{:S(2)}, u32[]{:S(2)}) async-start(f32[16,256,128]{2,1,0:T(8,128)} %shard_map.145), calls=%async_computation.1 | async-start | bytes 4194304 | tf_op jit(solution)/shard_map/all_to_all | solution.py:623
  125.1 26.7 %all-to-all-start.2 = ((f32[256,2,128]{2,1,0:T(2,128)}), f32[256,2,128]{2,1,0:T(2,128)S(1)}, u32[]{:S(2)}, u32[]{:S(2)}) async-start(f32[256,2,128]{2,1,0:T(2,128)} %bitcast.14), calls=%async_computation.2 | async-start | bytes 524288 | tf_op jit(solution)/shard_map/all_to_all | solution.py:642

commit v4 on v3

--- a/solution.py
+++ b/solution.py
@@ -19,8 +19,7 @@
 MIB = 1024 * 1024
 STATE_BATCH = 4
 SUMS_BATCH = 2
-SIGNAL_BATCH = 3
-INPUT_BATCH = 3
+FINISH_BATCH = 3
 
 
 def split(x, parts):
@@ -313,44 +312,59 @@
     rows = jnp.transpose(kept[...])
     first = jnp.concatenate([rows[0:1, :H], rows[1:2, :H]], axis=1)
     odd = lax.broadcasted_iota(jnp.int32, (8, N), 0) % 2 == 1
-    both = jnp.where(odd, rows[2:3], first)
-    sent_ref[...] = jnp.broadcast_to(both[None], sent_ref.shape)
-
-
-def signal_kernel(
+    sent_ref[...] = jnp.where(odd, rows[2:3], first)
+
+
+def finish_kernel(
     end_ref,
     sums_ref,
     carry_ref,
     leave_ref,
     slope_ref,
     step_part_ref,
+    in_ref,
     sig_turned_ref,
-    in_ref,
     start_ref,
     sig_part_ref,
+    sig_high_ref,
+    sig_low_ref,
+    in_part_ref,
     step_grad_ref,
     sig_grad_ref,
+    in_grad_ref,
+    in_maps,
     sig_turned,
-    in_maps,
     start,
     sig_part,
+    sig_high,
+    sig_low,
+    in_part,
+    step_grads,
     sig_grad,
-    step_grads,
+    in_grad,
     got,
     gone,
 ):
     pairs = []
     for g in range(G):
-        pairs.append((in_ref.at[:, narrow(g)], in_maps.at[:, narrow(g)]))
-        pairs.append((sig_turned_ref.at[wide(g)], sig_turned.at[wide(g)]))
-        pairs.append((start_ref.at[wide(g)], start.at[wide(g)]))
-        pairs.append((sig_part_ref.at[:, wide(g)], sig_part.at[:, wide(g)]))
+        cols, rows, few = (slice(None), wide(g)), wide(g), (slice(None), narrow(g))
+        for at, source, target in (
+            (few, in_ref, in_maps),
+            (cols, sig_part_ref, sig_part),
+            (rows, sig_turned_ref, sig_turned),
+            (rows, start_ref, start),
+            (cols, sig_high_ref, sig_high),
+            (cols, sig_low_ref, sig_low),
+            (few, in_part_ref, in_part),
+        ):
+            pairs.append((source.at[at], target.at[at]))
+    each = len(pairs) // G
     copies = fetch(got, pairs)
     earlier = mask_of(lambda i, j: i < j)
     leaving = []
-    for batch in batches(SIGNAL_BATCH):
+    for batch in batches(FINISH_BATCH):
         for g in batch:
-            for copy in copies[4 * g : 4 * g + 4]:
+            for copy in copies[each * g : each * (g + 1)]:
                 copy.wait()
         for g in batch:
             head = slice(g * PER, (g + 1) * PER)
@@ -360,8 +374,13 @@
             total = sums_ref[head, 3:4]
             decay = sums_ref[head, 4:5]
             in_twice = jnp.concatenate([in_map, in_map], axis=1)
-            pieces = jnp.concatenate(split(end, 2), axis=1)
+            end_high, end_low = split(end, 2)
+            pieces = jnp.concatenate([end_high, end_low], axis=1)
             sig_grad[:, wide(g)] = sig_part[:, wide(g)] + spread(carry) * mm_nt(in_twice, pieces)
+            both = mm(sig_high[:, wide(g)], pieces)
+            in_grad[:, narrow(g)] = in_part[:, narrow(g)] + (
+                both[:, :N] + (both[:, N:] + mm(sig_low[:, wide(g)], end_high))
+            )
             turned = mm_nt(pieces, in_twice)
             pushed = (sig_turned[wide(g), :].astype(F32) * turned).reshape(PER, D, T)
             pushed = jnp.sum(pushed, axis=1)
@@ -370,52 +389,22 @@
             held = total * jnp.sum(held, axis=1, keepdims=True)
             step_grad = leave_ref[head, :] * pushed - decay * (before + held)
             step_grads[head, :] = (step_part_ref[head, :] + step_grad) * slope_ref[head, :]
-        at = pl.ds(batch[0] * WIDE, len(batch) * WIDE)
+        cols = pl.ds(batch[0] * WIDE, len(batch) * WIDE)
+        few = pl.ds(batch[0] * N, len(batch) * N)
         leaving.append(
-            pltpu.make_async_copy(sig_grad.at[:, at], sig_grad_ref.at[:, at], gone.at[batch[0]])
+            pltpu.make_async_copy(
+                sig_grad.at[:, cols], sig_grad_ref.at[:, cols], gone.at[2 * batch[0]]
+            )
         )
         leaving[-1].start()
-    leaving.append(pltpu.make_async_copy(step_grads, step_grad_ref, gone.at[G]))
-    leaving[-1].start()
-    for copy in leaving:
-        copy.wait()
-
-
-def input_kernel(
-    end_ref,
-    sig_high_ref,
-    sig_low_ref,
-    in_part_ref,
-    in_grad_ref,
-    sig_high,
-    sig_low,
-    in_part,
-    in_grad,
-    got,
-    gone,
-):
-    pairs = []
-    for g in range(G):
-        pairs.append((sig_high_ref.at[:, wide(g)], sig_high.at[:, wide(g)]))
-        pairs.append((sig_low_ref.at[:, wide(g)], sig_low.at[:, wide(g)]))
-        pairs.append((in_part_ref.at[:, narrow(g)], in_part.at[:, narrow(g)]))
-    copies = fetch(got, pairs)
-    leaving = []
-    for batch in batches(INPUT_BATCH):
-        for g in batch:
-            for copy in copies[3 * g : 3 * g + 3]:
-                copy.wait()
-        for g in batch:
-            end_high, end_low = split(end_ref[wide(g), :], 2)
-            both = mm(sig_high[:, wide(g)], jnp.concatenate([end_high, end_low], axis=1))
-            in_grad[:, narrow(g)] = in_part[:, narrow(g)] + (
-                both[:, :N] + (both[:, N:] + mm(sig_low[:, wide(g)], end_high))
+        leaving.append(
+            pltpu.make_async_copy(
+                in_grad.at[:, few], in_grad_ref.at[:, few], gone.at[2 * batch[0] + 1]
             )
-        at = pl.ds(batch[0] * N, len(batch) * N)
-        leaving.append(
-            pltpu.make_async_copy(in_grad.at[:, at], in_grad_ref.at[:, at], gone.at[batch[0]])
         )
         leaving[-1].start()
+    leaving.append(pltpu.make_async_copy(step_grads, step_grad_ref, gone.at[2 * G]))
+    leaving[-1].start()
     for copy in leaving:
         copy.wait()
 
@@ -543,12 +532,12 @@
     )
 
 
-def send_sums(end, by_decay, by_bias, sums, devices):
+def local_sums(end, by_decay, by_bias, sums):
     return call(
         sums_kernel,
         0,
         [HERE, HERE, ELSEWHERE, ELSEWHERE],
-        [(HERE, f32_near(devices // 4, 8, N))],
+        [(HERE, f32_near(8, N))],
         near(end, sums) + far(by_decay, by_bias),
         4 * H * D * N,
         16,
@@ -558,50 +547,54 @@
             pltpu.VMEM((N, N), F32),
             COPIES((2 * (G // SUMS_BATCH),)),
         ],
-    )[0].reshape(devices, 2, N)
-
-
-def signal_part(end, sig_turned, in_map, start, sums, carry, leave, slope, sig_part, step_part):
-    step_grad, sig_grad = call(
-        signal_kernel,
+    )[0]
+
+
+def finish_part(
+    end,
+    sums,
+    carry,
+    leave,
+    slope,
+    step_part,
+    in_map,
+    sig_turned,
+    start,
+    sig_part,
+    sig_high,
+    sig_low,
+    in_part,
+):
+    wide_float, narrow_float = pltpu.VMEM((T, H * D), F32), pltpu.VMEM((T, G * N), F32)
+    wide_half = pltpu.VMEM((T, H * D), BF16)
+    return call(
+        finish_kernel,
         0,
-        [HERE] * 6 + [ELSEWHERE] * 4,
-        [(ELSEWHERE, f32(H, T)), (ELSEWHERE, f32(T, H * D))],
-        near(end, sums, carry, leave, slope, step_part) + far(sig_turned, in_map, start, sig_part),
-        8 * H * D * N * T,
-        28,
+        [HERE] * 6 + [ELSEWHERE] * 7,
         [
+            (ELSEWHERE, f32(H, T)),
+            (ELSEWHERE, f32(T, H * D)),
+            (ELSEWHERE, f32(T, G * N)),
+        ],
+        near(end, sums, carry, leave, slope, step_part)
+        + far(in_map, sig_turned, start, sig_part, sig_high, sig_low, in_part),
+        14 * H * D * N * T,
+        36,
+        [
+            pltpu.VMEM((T, G * N), BF16),
             pltpu.VMEM((H * D, T), BF16),
-            pltpu.VMEM((T, G * N), BF16),
             pltpu.VMEM((H * D, N), BF16),
-            pltpu.VMEM((T, H * D), F32),
-            pltpu.VMEM((T, H * D), F32),
+            wide_float,
+            wide_half,
+            wide_half,
+            narrow_float,
             pltpu.VMEM((H, T), F32),
-            COPIES((4 * G,)),
-            COPIES((G + 1,)),
+            wide_float,
+            narrow_float,
+            COPIES((7 * G,)),
+            COPIES((2 * G + 1,)),
         ],
     )
-    return sig_grad, step_grad
-
-
-def input_part(end, sig_high, sig_low, in_part):
-    return call(
-        input_kernel,
-        0,
-        [HERE] + [ELSEWHERE] * 3,
-        [(ELSEWHERE, f32(T, G * N))],
-        near(end) + far(sig_high, sig_low, in_part),
-        6 * H * D * N * T,
-        20,
-        [
-            pltpu.VMEM((T, H * D), BF16),
-            pltpu.VMEM((T, H * D), BF16),
-            pltpu.VMEM((T, G * N), F32),
-            pltpu.VMEM((T, G * N), F32),
-            COPIES((3 * G,)),
-            COPIES((G,)),
-        ],
-    )[0]
 
 
 def local(
@@ -628,7 +621,7 @@
         step_part,
         by_decay,
         by_bias,
-        sums,
+        sums_here,
         carry,
         leave,
         slope,
@@ -638,12 +631,28 @@
     ) = inner_part(sig, cot, in_map, out_map, raw, decay_row, bias_row, skip_row, start)
 
     devices = blocks * deals
-    sent = send_sums(end, by_decay, by_bias, sums, devices)
-    received = lax.all_to_all(sent, ("dp", "ctx"), 0, 0)
-    sig_grad, step_grad = signal_part(
-        end, sig_turned, in_map, start, sums, carry, leave, slope, sig_part, step_part
-    )
-    in_grad = input_part(end, sig_high, sig_low, in_part)
+    sums = local_sums(end, by_decay, by_bias, sums_here)[:2]
+    sums = sums + lax.ppermute(sums, "dp", [(i, i ^ 1) for i in range(deals)])
+    cores = [
+        [d * blocks + c for d in range(core, deals, 2) for c in range(blocks)] for core in range(2)
+    ]
+    sent = jnp.broadcast_to(sums[None], (devices // 2, 2, N))
+    received = lax.all_to_all(sent, ("dp", "ctx"), 0, 0, axis_index_groups=cores)
+    step_grad, sig_grad, in_grad = finish_part(
+        end,
+        sums_here,
+        carry,
+        leave,
+        slope,
+        step_part,
+        in_map,
+        sig_turned,
+        start,
+        sig_part,
+        sig_high,
+        sig_low,
+        in_part,
+    )
     summed = jnp.sum(received, axis=0) * (1.0 / (devices * T))
     return (
         sig_grad[None],

time: 153 us -> 151 us (0.987)
  Pallas kernels: 52.2 us -> 49.3 us
  starting transfers between devices: 15.3 us -> 16.9 us
    ppermute x0 -> x1, starting transfers between devices: none -> 3.38 us  [local(): sums = sums + lax.ppermute(sums, 'dp', [(i, i ^ 1) for i in range(deals)])]
    pallas_call x6 -> x5, Pallas kernels: 52.2 us -> 49.3 us  [call(): pl.pallas_call(kernel, grid=(grid,) if grid else (), in_specs=ins, out_sp...]
    all_to_all x1, waiting for transfers between devices: 5.47 us -> 3.31 us  [local(): lax.all_to_all(sent, ('dp', 'ctx'), 0, 0, axis_index_groups=cores)]
    all_to_all x1, starting transfers between devices: 11.1 us -> 9.3 us  [local(): lax.all_to_all(sent, ('dp', 'ctx'), 0, 0, axis_index_groups=cores)]
  transfers between devices with their start and end apart: 2 -> 3, of which waited for: 2 -> 3; matrix products, arithmetic and copies ran while one was open for 0% -> 0% of each run, Pallas kernels for 29% -> 28%
where the time goes in v4:
time: 151 us
  blocking collectives  63.8 us (42%)
  Pallas kernels  49.3 us (33%)
  waiting for transfers between devices  18.5 us (12%)
  starting transfers between devices  16.9 us (11%)
    all_to_all x1, blocking collectives, local(): ends = scan_states(lax.all_to_all(sent, 'ctx', 0, 0))  63.8 us
    pallas_call x5, Pallas kernels, call(): pl.pallas_call(kernel, grid=(grid,) if grid else (), in_specs=ins, out_sp...  49.3 us
    all_to_all x1, waiting for transfers between devices, local(): end = lax.all_to_all(ends, 'ctx', 0, 0).reshape(H * D, N)  14.3 us
    all_to_all x1, starting transfers between devices, local(): lax.all_to_all(sent, ('dp', 'ctx'), 0, 0, axis_index_groups=cores)  9.3 us
    all_to_all x1, starting transfers between devices, local(): end = lax.all_to_all(ends, 'ctx', 0, 0).reshape(H * D, N)  4.24 us
    ppermute x1, starting transfers between devices, local(): sums = sums + lax.ppermute(sums, 'dp', [(i, i ^ 1) for i in range(deals)])  3.38 us
    all_to_all x1, waiting for transfers between devices, local(): lax.all_to_all(sent, ('dp', 'ctx'), 0, 0, axis_index_groups=cores)  3.31 us
  transfers between devices with their start and end apart: 3, of which 3 were waited for; matrix products, arithmetic and copies ran while one was open for 0% of the time, Pallas kernels for 28%

profile of v4, /device:TPU:1, one launch (start us, length us, event | category | flops | bytes accessed | tf_op | source)
XLA Modules:
  0.0 150.6 jit_solution(12945629747792741347)
XLA Ops:
  0.6 3.1 %shard_map.144 = f32[16,264,128]{2,1,0:T(8,128)S(1)} custom-call(bf16[256,4096]{1,0:T(8,128)(2,1)} %bitcast.22, bf16[256,1024]{1,0:T(8,128)(2,1)} %bitcast.26, f32[64,256]{1,0:T(8,128)} %bitcast.30, f32[1,64]{1,0:T(1,128)} %bitcast.32, f32[1,64]{1,0:T(1,128)} %bitcast.34), custom_call_target="tpu_custom_call" | custom-call | flops 536870912 | bytes 4850176 | tf_op jit(solution)/shard_map/pallas_call | solution.py:415
  3.8 63.8 %all_to_all.15.state_ref = f32[16,264,128]{2,1,0:T(8,128)S(1)} all-to-all(f32[16,264,128]{2,1,0:T(8,128)S(1)} %shard_map.144), channel_id=1, replica_groups=mesh['dp'=16,'ctx'=16] {'ctx'}, dimensions={0} | all-to-all | bytes 4325376 | tf_op jit(solution)/shard_map/all_to_all | solution.py:615
  67.6 1.4 shard_map.145
  69.0 4.2 %all-to-all-start.1 = ((f32[16,256,128]{2,1,0:T(8,128)}), f32[16,256,128]{2,1,0:T(8,128)S(1)}, u32[]{:S(2)}, u32[]{:S(2)}) async-start(f32[16,256,128]{2,1,0:T(8,128)} %shard_map.145), calls=%async_computation.1 | async-start | bytes 4194304 | tf_op jit(solution)/shard_map/all_to_all | solution.py:616
  73.2 34.3 %shard_map.146 = (f32[256,4096]{1,0:T(8,128)}, f32[256,1024]{1,0:T(8,128)}, f32[256,1024]{1,0:T(8,128)}, f32[64,256]{1,0:T(8,128)S(1)}, f32[4096,128]{1,0:T(8,12...) custom-call(bf16[256,4096]{1,0:T(8,128)(2,1)} %bitcast.37, ...), custom_call_target="tpu_custom_call" | custom-call | flops 10737418240 | bytes 23429888 | tf_op jit(solution)/shard_map/pallas_call | solution.py:415
  107.5 14.3 %all-to-all-done.1 = f32[16,256,128]{2,1,0:T(8,128)S(1)} async-done(((f32[16,256,128]{2,1,0:T(8,128)}), f32[16,256,128]{2,1,0:T(8,128)S(1)}, u32[]{:S(2)}, u32[]{:S(2)}) %all-to-all-start.1) | async-done | bytes 2097184 | tf_op jit(solution)/shard_map/all_to_all | solution.py:616
  121.8 2.5 %shard_map.148 = f32[8,128]{1,0:T(8,128)S(1)} custom-call(f32[4096,128]{1,0:T(8,128)S(1)} %bitcast.20, f32[64,128]{1,0:T(8,128)S(1)} %get-tuple-element.23.sums_ref, f32[4096,128]{1,0:T(8,128)} %get-tuple-element.37.by_decay_ref, f32[4096,128]{1,0:T(8,128)} %get-tuple-element.38.by_bias_ref), custom_call_target="tpu_custom_call" | custom-call | flops 2097152 | bytes 6328320 | tf_op jit(solution)/shard_map/pallas_call | solution.py:415
  124.4 3.4 %collective-permute-start = (f32[2,128]{1,0:T(2,128)S(1)}, f32[2,128]{1,0:T(2,128)S(1)}, u32[]{:S(2)}, u32[]{:S(2)}) collective-permute-start(f32[2,128]{1,0:T(2,128)S(1)} %slice.12), channel_id=1, source_target_pairs={{0,16},{16,0},{32,48},{48,32},{64,80},{80,64},{96,112},{112,96},{1... | collective-permute-start | bytes 3080 | tf_op jit(solution)/shard_map/ppermute | solution.py:635
  127.7 0.8 collective-permute-done
  128.6 0.7 broadcast_in_dim.34
  129.3 9.3 %all-to-all-start.2 = ((f32[128,2,128]{2,1,0:T(2,128)}), f32[128,2,128]{2,1,0:T(2,128)S(1)}, u32[]{:S(2)}, u32[]{:S(2)}) async-start(f32[128,2,128]{2,1,0:T(2,128)} %broadcast_in_dim.34), calls=%async_computation.2 | async-start | bytes 262144 | tf_op jit(solution)/shard_map/all_to_all | solution.py:640
  138.6 8.0 %shard_map.147 = (f32[64,256]{1,0:T(8,128)}, f32[256,4096]{1,0:T(8,128)}, f32[256,1024]{1,0:T(8,128)}) custom-call(f32[4096,128]{1,0:T(8,128)S(1)} %bitcast.21, f32[64,128]{1,0:T(8,128)S(1)} %get-tuple-element.23.sums_ref, f32[64,256]{1,0:T(8,128)S(1)} %get-tuple-element.24.carry_ref, f32[64,256]{1,0:T(8,128)S(1)} %get-tuple-element.25.leave_ref, ...), custom_call_target="tpu_custom_call" | custom-call | flops 1879048192 | bytes 20807680 | tf_op jit(solution)/shard_map/pallas_call | solution.py:415
  146.6 3.3 %all-to-all-done.2 = f32[128,2,128]{2,1,0:T(2,128)S(1)} async-done(((f32[128,2,128]{2,1,0:T(2,128)}), f32[128,2,128]{2,1,0:T(2,128)S(1)}, u32[]{:S(2)}, u32[]{:S(2)}) %all-to-all-start.2) | async-done | bytes 131104 | tf_op jit(solution)/shard_map/all_to_all | solution.py:640
  149.9 0.1 reduce_sum.9
  150.0 0.6 slice_bitcast_fusion
  (3 shorter events, 0.0 us)
Async XLA Ops:
  69.0 52.8 %all-to-all-start.1 = ((f32[16,256,128]{2,1,0:T(8,128)}), f32[16,256,128]{2,1,0:T(8,128)S(1)}, u32[]{:S(2)}, u32[]{:S(2)}) async-start(f32[16,256,128]{2,1,0:T(8,128)} %shard_map.145), calls=%async_computation.1 | async-start | bytes 4194304 | tf_op jit(solution)/shard_map/all_to_all | solution.py:616
  124.4 4.2 %collective-permute-start = (f32[2,128]{1,0:T(2,128)S(1)}, f32[2,128]{1,0:T(2,128)S(1)}, u32[]{:S(2)}, u32[]{:S(2)}) collective-permute-start(f32[2,128]{1,0:T(2,128)S(1)} %slice.12), channel_id=1, source_target_pairs={{0,16},{16,0},{32,48},{48,32},{64,80},{80,64},{96,112},{112,96},{1... | collective-permute-start | bytes 3080 | tf_op jit(solution)/shard_map/ppermute | solution.py:635
  129.3 20.6 %all-to-all-start.2 = ((f32[128,2,128]{2,1,0:T(2,128)}), f32[128,2,128]{2,1,0:T(2,128)S(1)}, u32[]{:S(2)}, u32[]{:S(2)}) async-start(f32[128,2,128]{2,1,0:T(2,128)} %broadcast_in_dim.34), calls=%async_computation.2 | async-start | bytes 262144 | tf_op jit(solution)/shard_map/all_to_all | solution.py:640

commit v5 on v4

--- a/solution.py
+++ b/solution.py
@@ -1,3 +1,4 @@
+import functools
 import math
 
 import jax
@@ -18,6 +19,7 @@
 BF16 = jnp.bfloat16
 MIB = 1024 * 1024
 STATE_BATCH = 4
+INNER_FIRST = 4
 SUMS_BATCH = 2
 FINISH_BATCH = 3
 
@@ -93,6 +95,20 @@
     return [range(g, min(g + size, G)) for g in range(0, G, size)]
 
 
+def group_of(slot, odd):
+    if slot in (0, 1):
+        return slot + 2 * odd
+    if slot in (2, 3):
+        return slot + 4 - 2 * odd
+    if slot in (4, 5):
+        return slot - 2 - 2 * odd
+    return slot - 2 + 2 * odd
+
+
+def chosen(g, size):
+    return pl.ds(pl.multiple_of(g * size, size), size)
+
+
 def wide(g):
     return pl.ds(g * WIDE, WIDE)
 
@@ -102,66 +118,171 @@
 
 
 def state_kernel(
+    odd_ref,
     cot_ref,
     out_ref,
     raw_ref,
     decay_ref,
     bias_ref,
-    sent_ref,
+    own_ref,
+    own_total_ref,
+    first_ref,
+    second_ref,
     cot,
     out,
     raw,
     decay,
     bias,
+    entries,
     got,
 ):
-    half = WIDE // 2
+    odd = odd_ref[0]
+    order = (4, 5, 6, 7, 0, 1, 2, 3)
     pairs = [(raw_ref, raw), (decay_ref, decay), (bias_ref, bias)]
-    for g in range(G):
-        pairs.append((cot_ref.at[:, wide(g)], cot.at[:, wide(g)]))
-        pairs.append((out_ref.at[:, narrow(g)], out.at[:, narrow(g)]))
+    for slot in order:
+        g = group_of(slot, odd)
+        pairs.append((cot_ref.at[:, chosen(g, WIDE)], cot.at[:, wide(slot)]))
+        pairs.append((out_ref.at[:, chosen(g, N)], out.at[:, narrow(slot)]))
     copies = fetch(got, pairs)
     for copy in copies[:3]:
         copy.wait()
     bias_column = column_of(bias[...], 0, H)
     decay_log = column_of(decay[...], 0, H)
-    entries = jnp.exp(steps_of(raw[...], bias_column, decay_log)[3])
+    entries[...] = jnp.exp(steps_of(raw[...], bias_column, decay_log)[3])
     for batch in batches(STATE_BATCH):
-        for g in batch:
-            copies[2 * g + 3].wait()
-            copies[2 * g + 4].wait()
-        for g in batch:
-            entry = entries[g * PER : (g + 1) * PER]
-            turned = jnp.transpose(cot[:, wide(g)]).astype(F32)
+        for k in batch:
+            copies[2 * k + 3].wait()
+            copies[2 * k + 4].wait()
+        for slot in [order[k] for k in batch]:
+            entry = entries[chosen(group_of(slot, odd), PER), :]
+            turned = jnp.transpose(cot[:, wide(slot)]).astype(F32)
             weighted = (turned.reshape(PER, D, T) * entry[:, None, :]).reshape(WIDE, T)
-            out_map = out[:, narrow(g)]
+            out_map = out[:, narrow(slot)]
             high, low = split(weighted, 2)
             state = mm(high, out_map) + mm(low, out_map)
             total = jnp.broadcast_to(entry[:, T - 1 :], (PER, N))
-            sent_ref[2 * g, :half] = state[:half]
-            sent_ref[2 * g + 1, :half] = state[half:]
-            sent_ref[2 * g, half:] = total
-            sent_ref[2 * g + 1, half:] = jnp.concatenate(
-                [total[PER // 2 :], total[: PER // 2]], axis=0
-            )
-
-
-def scan_kernel(state_ref, end_ref, end, gone):
-    blocks, rows, _ = end.shape
+            if slot < 4:
+                own_ref[wide(slot), :] = state
+                own_total_ref[slot * PER : (slot + 1) * PER, :] = total
+            else:
+                ref, k = (first_ref, slot - 4) if slot < 6 else (second_ref, slot - 6)
+                ref[wide(k), :] = state
+                ref[2 * WIDE + k * PER : 2 * WIDE + (k + 1) * PER, :] = total
+
+
+def flag_rows(flags_ref):
+    keep = flags_ref[2:3, :]
+    return (flags_ref[0:1, :], jnp.ones_like(keep)), (flags_ref[1:2, :], keep)
+
+
+def combine_kernel(
+    flags_ref,
+    own_ref,
+    own_total_ref,
+    first_ref,
+    second_ref,
+    after_ref,
+    sent_ref,
+    other_total_ref,
+    other_ref,
+    other,
+    gone,
+):
+    halves = flag_rows(flags_ref)
+    per_half = 2 * PER
+    each = sent_ref.shape[0]
+    got = per_half // each
+    totals = [[] for _ in range(each)]
+    other_totals = []
+    for half, ref in enumerate((first_ref, second_ref)):
+        earlier, keep = halves[half]
+        for h in range(per_half):
+            mine = half * per_half + h
+            state = own_ref[mine * D : (mine + 1) * D, :]
+            total = own_total_ref[mine : mine + 1, :]
+            met = ref[h * D : (h + 1) * D, :]
+            met_total = ref[per_half * D + h : per_half * D + h + 1, :]
+            by_own = jnp.where(earlier > 0, 1.0, met_total * keep)
+            by_met = jnp.where(earlier > 0, total * keep, 1.0)
+            at, q = h // got, half * got + h % got
+            sent_ref[at, q * D : (q + 1) * D, :] = by_own * state + by_met * met
+            totals[at].append(total * met_total)
+            other[mine * D : (mine + 1) * D, :] = jnp.where(earlier > 0, met, state)
+            other_totals.append(jnp.where(earlier > 0, met_total, total))
+    rows = 2 * got
+    for at in range(each):
+        pad = [jnp.zeros((8 - rows, N), F32)]
+        sent_ref[at, rows * D :, :] = jnp.concatenate(totals[at] + pad, axis=0)
+    other_total_ref[...] = jnp.concatenate(other_totals, axis=0)
+    copy = pltpu.make_async_copy(other, other_ref, gone.at[0])
+    copy.start()
+    copy.wait()
+
+
+def scan_kernel(odd_ref, state_ref, after_ref, end_ref, end, gone):
+    pairs, rows, _ = end.shape
+    heads = rows // D
     leaving = []
-    for h in range(rows // D):
+    for h in range(heads):
         at = pl.ds(h * D, D)
         carry = jnp.zeros((D, N), F32)
-        for b in reversed(range(blocks)):
-            end[b, at, :] = carry
-            carry = state_ref[b, at, :] + state_ref[b, rows + h : rows + h + 1, :] * carry
+        if h < heads // 2:
+            for b in reversed(range(pairs)):
+                end[b, at, :] = carry
+                carry = state_ref[b, at, :] + state_ref[b, rows + h : rows + h + 1, :] * carry
+        else:
+            for k in reversed(range(pairs)):
+                b = lax.rem(k + 1 - odd_ref[0], pairs)
+                if k < pairs - 1:
+                    end[b, at, :] = carry
+                total = state_ref[b, rows + h : rows + h + 1, :]
+                carry = state_ref[b, at, :] + total * carry
+            end[lax.rem(pairs - odd_ref[0], pairs), at, :] = carry
         leaving.append(pltpu.make_async_copy(end.at[:, at], end_ref.at[:, at], gone.at[h]))
         leaving[-1].start()
     for copy in leaving:
         copy.wait()
 
 
+def expand_kernel(
+    flags_ref,
+    end_ref,
+    other_total_ref,
+    other_ref,
+    after_ref,
+    own_ref,
+    first_ref,
+    second_ref,
+    other,
+    got,
+):
+    per_half = 2 * PER
+    pairs = [(other_ref.at[wide(k)], other.at[wide(k)]) for k in range(4)]
+    copies = fetch(got, pairs)
+    halves = flag_rows(flags_ref)
+    each = end_ref.shape[0]
+    share = per_half // each
+    for half, ref in enumerate((first_ref, second_ref)):
+        earlier, keep = halves[half]
+        later = 1.0 - earlier
+        for h in range(per_half):
+            mine = half * per_half + h
+            if h % PER == 0:
+                copies[mine // PER].wait()
+            q = half * share + h % share
+            end = end_ref[h // share, q * D : (q + 1) * D, :]
+            beside = other[mine * D : (mine + 1) * D, :]
+            total = other_total_ref[mine : mine + 1, :] * keep
+            own_ref[mine * D : (mine + 1) * D, :] = (earlier * keep) * beside + jnp.where(
+                earlier > 0, total, 1.0
+            ) * end
+            ref[h * D : (h + 1) * D, :] = (later * keep) * beside + jnp.where(
+                earlier > 0, 1.0, total
+            ) * end
+
+
 def inner_kernel(
+    first_group,
     sig_ref,
     cot_ref,
     in_ref,
@@ -171,21 +292,22 @@
     bias_ref,
     skip_ref,
     start_ref,
-    sig_grad_ref,
-    in_grad_ref,
-    out_grad_ref,
-    step_grad_ref,
-    by_decay_ref,
-    by_bias_ref,
-    sums_ref,
-    carry_ref,
-    leave_ref,
-    slope_ref,
-    sig_high_ref,
-    sig_low_ref,
-    sig_turned_ref,
+    after_ref,
+    *refs,
 ):
-    head = pl.program_id(0) * PER
+    (
+        sig_grad_ref,
+        in_grad_ref,
+        out_grad_ref,
+        step_grad_ref,
+        sums_ref,
+        carry_ref,
+        leave_ref,
+        slope_ref,
+        token_ref,
+    ) = refs[-9:]
+    token_ref[...] = jnp.zeros_like(token_ref)
+    head = (pl.program_id(0) + first_group) * PER
     bias = column_of(bias_ref[...], head, PER)
     decay_log = column_of(decay_ref[...], head, PER)
     pre_act, step, decay, cumul = steps_of(raw_ref[...], bias, decay_log)
@@ -198,7 +320,6 @@
     carry_ref[...] = carry
     leave_ref[...] = leave
     slope_ref[...] = slope
-    later = rows_times_mask(slope, mask_of(lambda i, j: i > j))
     cols = columns([cumul - jnp.log(step), entry])
     in_map = in_ref[...]
     out_map = out_ref[...]
@@ -254,8 +375,6 @@
     )
     skip = jnp.sum(own * column_of(skip_ref[...], head, PER), axis=0, keepdims=True)
     sig_grad_ref[...] = sig_grad_ref[...] + skip * cot_float
-    sig_turned_ref[...] = jnp.transpose(sig_ref[...])
-    sig_high_ref[...], sig_low_ref[...] = split(sig_float * spread(carry), 2)
     high, low = split(score_grad, 2)
     in_grad_ref[...] = mm(high, out_map) + mm(low, out_map)
     out_grad_ref[...] = out_grad + (mm_tn(high, in_map) + mm_tn(low, in_map))
@@ -266,16 +385,6 @@
     rate_grad = rows_times_mask(cumul_grad, mask_of(lambda i, j: i >= j))
     step_grad = col_sum / step - rate_grad * decay
     step_grad_ref[...] = step_grad
-    into_decay = (final - cumul) * carry
-    into_bias = leave * (slope - decay * step * later)
-    start = start_ref[...].astype(F32).reshape(PER, D, N)
-    for rows, weight, ref in (
-        (into_decay, final * total, by_decay_ref),
-        (into_bias, -decay * total * jnp.sum(slope, axis=1, keepdims=True), by_bias_ref),
-    ):
-        high, low = split(sig_float * spread(rows), 2)
-        grown = mm_tn(high, in_map) + mm_tn(low, in_map)
-        ref[...] = grown + (start * weight[:, :, None]).reshape(WIDE, N)
     skip_sum = jnp.sum(
         own * jnp.sum(sig_float * cot_float, axis=0, keepdims=True), axis=1, keepdims=True
     )
@@ -288,27 +397,88 @@
     sums_ref[...] = sums
 
 
+def prepare_kernel(
+    sig_ref,
+    in_ref,
+    raw_ref,
+    decay_ref,
+    bias_ref,
+    start_ref,
+    after_ref,
+    by_decay_ref,
+    by_bias_ref,
+    sig_high_ref,
+    sig_low_ref,
+    sig_turned_ref,
+):
+    head = pl.program_id(0) * PER
+    bias = column_of(bias_ref[...], head, PER)
+    decay_log = column_of(decay_ref[...], head, PER)
+    pre_act, step, decay, cumul = steps_of(raw_ref[...], bias, decay_log)
+    slope = jax.nn.sigmoid(pre_act)
+    final = cumul[:, T - 1 :]
+    total = jnp.exp(final)
+    leave = jnp.exp(final - cumul)
+    carry = leave * step
+    later = rows_times_mask(slope, mask_of(lambda i, j: i > j))
+    in_map = in_ref[...]
+    sig_float = sig_ref[...].astype(F32)
+    sig_turned_ref[...] = jnp.transpose(sig_ref[...])
+    sig_high_ref[...], sig_low_ref[...] = split(sig_float * spread(carry), 2)
+    into_decay = (final - cumul) * carry
+    into_bias = leave * (slope - decay * step * later)
+    start = start_ref[...].astype(F32).reshape(PER, D, N)
+    turned = jnp.transpose(sig_ref[...]).astype(F32).reshape(PER, D, T)
+    for rows, weight, ref in (
+        (into_decay, final * total, by_decay_ref),
+        (into_bias, -decay * total * jnp.sum(slope, axis=1, keepdims=True), by_bias_ref),
+    ):
+        high, low = split((turned * rows[:, None, :]).reshape(WIDE, T), 2)
+        grown = mm(high, in_map) + mm(low, in_map)
+        ref[...] = grown + (start * weight[:, :, None]).reshape(WIDE, N)
+
+
+def end_of(slot, own_ref, first_ref, second_ref):
+    if slot < 4:
+        return own_ref[wide(slot), :]
+    return first_ref[wide(slot - 4), :] if slot < 6 else second_ref[wide(slot - 6), :]
+
+
 def sums_kernel(
-    end_ref, sums_ref, by_decay_ref, by_bias_ref, sent_ref, by_decay, by_bias, kept, got
+    odd_ref,
+    own_ref,
+    first_ref,
+    second_ref,
+    sums_ref,
+    by_decay_ref,
+    by_bias_ref,
+    sent_ref,
+    by_decay,
+    by_bias,
+    kept,
+    got,
 ):
+    odd = odd_ref[0]
     pairs = []
-    for g in range(0, G, SUMS_BATCH):
-        at = pl.ds(g * WIDE, SUMS_BATCH * WIDE)
-        pairs.append((by_decay_ref.at[at], by_decay.at[at]))
-        pairs.append((by_bias_ref.at[at], by_bias.at[at]))
+    for slot in range(G):
+        at = chosen(group_of(slot, odd), WIDE)
+        pairs.append((by_decay_ref.at[at], by_decay.at[wide(slot)]))
+        pairs.append((by_bias_ref.at[at], by_bias.at[wide(slot)]))
     copies = fetch(got, pairs)
     which = lax.broadcasted_iota(jnp.int32, (PER, N), 1)
     kept[...] = jnp.zeros_like(kept)
-    for g in range(G):
-        if g % SUMS_BATCH == 0:
-            copies[2 * (g // SUMS_BATCH)].wait()
-            copies[2 * (g // SUMS_BATCH) + 1].wait()
-        end = end_ref[wide(g), :]
-        sums = sums_ref[g * PER : (g + 1) * PER, :]
-        for k, held in enumerate((by_decay, by_bias)):
-            partial = jnp.sum((end * held[wide(g), :]).reshape(PER, D, N), axis=1)
-            sums = sums + jnp.where(which == k, jnp.sum(partial, axis=1, keepdims=True), 0.0)
-        kept[g * PER : (g + 1) * PER, :] = sums
+    for batch in batches(SUMS_BATCH):
+        for slot in batch:
+            copies[2 * slot].wait()
+            copies[2 * slot + 1].wait()
+        for slot in batch:
+            end = end_of(slot, own_ref, first_ref, second_ref)
+            head = chosen(group_of(slot, odd), PER)
+            sums = sums_ref[head, :]
+            for k, held in enumerate((by_decay, by_bias)):
+                partial = jnp.sum((end * held[wide(slot), :]).reshape(PER, D, N), axis=1)
+                sums = sums + jnp.where(which == k, jnp.sum(partial, axis=1, keepdims=True), 0.0)
+            kept[head, :] = sums
     rows = jnp.transpose(kept[...])
     first = jnp.concatenate([rows[0:1, :H], rows[1:2, :H]], axis=1)
     odd = lax.broadcasted_iota(jnp.int32, (8, N), 0) % 2 == 1
@@ -316,7 +486,10 @@
 
 
 def finish_kernel(
-    end_ref,
+    odd_ref,
+    own_ref,
+    first_ref,
+    second_ref,
     sums_ref,
     carry_ref,
     leave_ref,
@@ -345,10 +518,15 @@
     got,
     gone,
 ):
+    odd = odd_ref[0]
     pairs = []
-    for g in range(G):
-        cols, rows, few = (slice(None), wide(g)), wide(g), (slice(None), narrow(g))
-        for at, source, target in (
+    every = slice(None)
+    for slot in range(G):
+        g = group_of(slot, odd)
+        cols = ((every, chosen(g, WIDE)), (every, wide(slot)))
+        rows = ((chosen(g, WIDE),), (wide(slot),))
+        few = ((every, chosen(g, N)), (every, narrow(slot)))
+        for (there, here), source, target in (
             (few, in_ref, in_maps),
             (cols, sig_part_ref, sig_part),
             (rows, sig_turned_ref, sig_turned),
@@ -357,7 +535,7 @@
             (cols, sig_low_ref, sig_low),
             (few, in_part_ref, in_part),
         ):
-            pairs.append((source.at[at], target.at[at]))
+            pairs.append((source.at[there], target.at[here]))
     each = len(pairs) // G
     copies = fetch(got, pairs)
     earlier = mask_of(lambda i, j: i < j)
@@ -367,12 +545,13 @@
             for copy in copies[each * g : each * (g + 1)]:
                 copy.wait()
         for g in batch:
-            head = slice(g * PER, (g + 1) * PER)
-            end = end_ref[wide(g), :]
+            head = chosen(group_of(g, odd), PER)
+            end = end_of(g, own_ref, first_ref, second_ref)
             in_map = in_maps[:, narrow(g)]
             carry = carry_ref[head, :]
-            total = sums_ref[head, 3:4]
-            decay = sums_ref[head, 4:5]
+            columns_here = sums_ref[head, :]
+            total = columns_here[:, 3:4]
+            decay = columns_here[:, 4:5]
             in_twice = jnp.concatenate([in_map, in_map], axis=1)
             end_high, end_low = split(end, 2)
             pieces = jnp.concatenate([end_high, end_low], axis=1)
@@ -389,27 +568,23 @@
             held = total * jnp.sum(held, axis=1, keepdims=True)
             step_grad = leave_ref[head, :] * pushed - decay * (before + held)
             step_grads[head, :] = (step_part_ref[head, :] + step_grad) * slope_ref[head, :]
-        cols = pl.ds(batch[0] * WIDE, len(batch) * WIDE)
-        few = pl.ds(batch[0] * N, len(batch) * N)
-        leaving.append(
-            pltpu.make_async_copy(
-                sig_grad.at[:, cols], sig_grad_ref.at[:, cols], gone.at[2 * batch[0]]
-            )
-        )
-        leaving[-1].start()
-        leaving.append(
-            pltpu.make_async_copy(
-                in_grad.at[:, few], in_grad_ref.at[:, few], gone.at[2 * batch[0] + 1]
-            )
-        )
-        leaving[-1].start()
+        for g in batch:
+            there = group_of(g, odd)
+            for k, (source, target) in enumerate(
+                (
+                    (sig_grad.at[:, wide(g)], sig_grad_ref.at[:, chosen(there, WIDE)]),
+                    (in_grad.at[:, narrow(g)], in_grad_ref.at[:, chosen(there, N)]),
+                )
+            ):
+                leaving.append(pltpu.make_async_copy(source, target, gone.at[2 * g + k]))
+                leaving[-1].start()
     leaving.append(pltpu.make_async_copy(step_grads, step_grad_ref, gone.at[2 * G]))
     leaving[-1].start()
     for copy in leaving:
         copy.wait()
 
 
-def call(kernel, grid, ins, outs, args, flops, mib, scratch=()):
+def call(kernel, grid, ins, outs, args, flops, mib, scratch=(), aliases={}):
     moved = sum(a.size * a.dtype.itemsize for a in args)
     moved += sum(math.prod(s.shape) * s.dtype.itemsize for _, s in outs)
     return pl.pallas_call(
@@ -419,6 +594,7 @@
         out_specs=[spec for spec, _ in outs],
         out_shape=[shape for _, shape in outs],
         scratch_shapes=list(scratch),
+        input_output_aliases=aliases,
         compiler_params=pltpu.CompilerParams(
             dimension_semantics=("arbitrary",) if grid else None, vmem_limit_bytes=mib * MIB
         ),
@@ -457,17 +633,23 @@
 
 ELSEWHERE = pl.BlockSpec(memory_space=pl.ANY)
 HERE = pl.BlockSpec(memory_space=pltpu.VMEM)
+SCALAR = pl.BlockSpec(memory_space=pltpu.SMEM)
 COPIES = pltpu.SemaphoreType.DMA
 
 
-def send_states(cot, out_map, raw, decay_row, bias_row, blocks):
-    rows = H * D // blocks + 8
+def block_states(odd, cot, out_map, raw, decay_row, bias_row):
+    halves = f32_near(H * D // 4 + H // 4, N)
     return call(
         state_kernel,
         0,
-        [ELSEWHERE] * 5,
-        [(HERE, f32_near(blocks, rows, N))],
-        far(cot, out_map, raw, decay_row, bias_row),
+        [SCALAR] + [ELSEWHERE] * 5,
+        [
+            (HERE, f32_near(H * D // 2, N)),
+            (HERE, f32_near(H // 2, N)),
+            (HERE, halves),
+            (HERE, halves),
+        ],
+        [odd] + far(cot, out_map, raw, decay_row, bias_row),
         4 * H * D * N * T,
         24,
         [
@@ -476,82 +658,135 @@
             pltpu.VMEM((H, T), F32),
             pltpu.VMEM((1, H), F32),
             pltpu.VMEM((1, H), F32),
+            pltpu.VMEM((H, T), F32),
             COPIES((2 * G + 3,)),
         ],
-    )[0]
-
-
-def scan_states(states):
-    blocks, rows, _ = states.shape
+    )
+
+
+def combine_states(flags, own, own_total, first, second, after, pairs):
+    return call(
+        combine_kernel,
+        0,
+        [HERE] * 5 + [ELSEWHERE],
+        [
+            (HERE, f32_near(pairs, H * D // 2 // pairs + 8, N)),
+            (HERE, f32_near(H // 2, N)),
+            (ELSEWHERE, f32(H * D // 2, N)),
+        ],
+        near(flags, own, own_total, first, second) + far(after),
+        4 * H * D * N,
+        16,
+        [pltpu.VMEM((H * D // 2, N), F32), COPIES((1,))],
+    )
+
+
+def scan_states(odd, states, after):
+    pairs, rows, _ = states.shape
     rows -= 8
     return call(
         scan_kernel,
         0,
-        [HERE],
-        [(ELSEWHERE, f32(blocks, rows, N))],
-        near(states),
-        2 * H * D * N,
+        [SCALAR, HERE, ELSEWHERE],
+        [(ELSEWHERE, f32(pairs, rows, N))],
+        [odd] + near(states) + far(after),
+        H * D * N,
         16,
-        [pltpu.VMEM((blocks, rows, N), F32), COPIES((rows // D,))],
+        [pltpu.VMEM((pairs, rows, N), F32), COPIES((rows // D,))],
     )[0]
 
 
-def inner_part(sig, cot, in_map, out_map, raw, decay_row, bias_row, skip_row, start):
+def expand_ends(flags, ends, other_total, other, after):
+    quarter = f32_near(H * D // 4, N)
     return call(
-        inner_kernel,
+        expand_kernel,
+        0,
+        [HERE] * 3 + [ELSEWHERE] * 2,
+        [(HERE, f32_near(H * D // 2, N)), (HERE, quarter), (HERE, quarter)],
+        near(flags, ends, other_total) + far(other, after),
+        4 * H * D * N,
+        16,
+        [pltpu.VMEM((H * D // 2, N), F32), COPIES((4,))],
+    )
+
+
+def inner_part(
+    groups, sig, cot, in_map, out_map, raw, decay_row, bias_row, skip_row, start, after, begun=()
+):
+    first = groups[0]
+    wide_cols = pl.BlockSpec((T, WIDE), lambda g: (0, g + first))
+    map_cols = pl.BlockSpec((T, N), lambda g: (0, g + first))
+    head_rows = pl.BlockSpec((PER, T), lambda g: (g + first, 0))
+    head_lanes = pl.BlockSpec((PER, N), lambda g: (g + first, 0))
+    state_rows = pl.BlockSpec((WIDE, N), lambda g: (g + first, 0))
+    ins = [wide_cols, wide_cols, map_cols, map_cols, head_rows] + [HEAD_ALL] * 3
+    ins += [state_rows] + [ELSEWHERE] * (1 + len(begun))
+    return call(
+        functools.partial(inner_kernel, first),
+        len(groups),
+        ins,
+        [
+            (wide_cols, f32(T, H * D)),
+            (map_cols, f32(T, G * N)),
+            (map_cols, f32(T, G * N)),
+            (head_rows, f32_near(H, T)),
+            (head_lanes, f32_near(H, N)),
+            (head_rows, f32_near(H, T)),
+            (head_rows, f32_near(H, T)),
+            (head_rows, f32_near(H, T)),
+            (pl.BlockSpec((8, N), lambda g: (0, 0)), f32(8, N)),
+        ],
+        far(sig, cot, in_map, out_map, raw, decay_row, bias_row, skip_row, start, after)
+        + far(*begun[:3])
+        + near(*begun[3:]),
+        len(groups) * PER * T * T * N * 15,
+        24,
+        aliases={10 + k: k for k in range(len(begun))},
+    )
+
+
+def prepared_part(sig, in_map, raw, decay_row, bias_row, start, after):
+    return call(
+        prepare_kernel,
         G,
+        [WIDE_COLS, MAP_COLS, HEAD_ROWS, HEAD_ALL, HEAD_ALL, STATE_ROWS]
+        + [pl.BlockSpec((H // 2, N), lambda g: (0, 0))],
         [
-            WIDE_COLS,
-            WIDE_COLS,
-            MAP_COLS,
-            MAP_COLS,
-            HEAD_ROWS,
-            HEAD_ALL,
-            HEAD_ALL,
-            HEAD_ALL,
-            STATE_ROWS,
-        ],
-        [
-            (WIDE_COLS, f32(T, H * D)),
-            (MAP_COLS, f32(T, G * N)),
-            (MAP_COLS, f32(T, G * N)),
-            (HEAD_ROWS, f32_near(H, T)),
             (STATE_ROWS, f32(H * D, N)),
             (STATE_ROWS, f32(H * D, N)),
-            (HEAD_LANES, f32_near(H, N)),
-            (HEAD_ROWS, f32_near(H, T)),
-            (HEAD_ROWS, f32_near(H, T)),
-            (HEAD_ROWS, f32_near(H, T)),
             (WIDE_COLS, bf16(T, H * D)),
             (WIDE_COLS, bf16(T, H * D)),
             (STATE_COLS, bf16(H * D, T)),
         ],
-        far(sig, cot, in_map, out_map, raw, decay_row, bias_row, skip_row, start),
-        H * T * T * N * 20,
+        far(sig, in_map, raw, decay_row, bias_row, start) + near(after),
+        H * T * T * N * 5,
         24,
     )
 
 
-def local_sums(end, by_decay, by_bias, sums):
+def local_sums(odd, own, first, second, sums, by_decay, by_bias):
     return call(
         sums_kernel,
         0,
-        [HERE, HERE, ELSEWHERE, ELSEWHERE],
+        [SCALAR] + [HERE] * 4 + [ELSEWHERE] * 2,
         [(HERE, f32_near(8, N))],
-        near(end, sums) + far(by_decay, by_bias),
+        [odd] + near(own, first, second, sums) + far(by_decay, by_bias),
         4 * H * D * N,
         16,
         [
             pltpu.VMEM((H * D, N), F32),
             pltpu.VMEM((H * D, N), F32),
             pltpu.VMEM((N, N), F32),
-            COPIES((2 * (G // SUMS_BATCH),)),
+            COPIES((2 * G,)),
         ],
     )[0]
 
 
 def finish_part(
-    end,
+    odd,
+    own,
+    first,
+    second,
     sums,
     carry,
     leave,
@@ -570,13 +805,14 @@
     return call(
         finish_kernel,
         0,
-        [HERE] * 6 + [ELSEWHERE] * 7,
+        [SCALAR] + [HERE] * 8 + [ELSEWHERE] * 7,
         [
             (ELSEWHERE, f32(H, T)),
             (ELSEWHERE, f32(T, H * D)),
             (ELSEWHERE, f32(T, G * N)),
         ],
-        near(end, sums, carry, leave, slope, step_part)
+        [odd]
+        + near(own, first, second, sums, carry, leave, slope, step_part)
         + far(in_map, sig_turned, start, sig_part, sig_high, sig_low, in_part),
         14 * H * D * N * T,
         36,
@@ -611,27 +847,47 @@
     start = checkpoints.reshape(H * D, N)
     blocks, deals = lax.axis_size("ctx"), lax.axis_size("dp")
 
-    sent = send_states(cot, out_map, raw, decay_row, bias_row, blocks)
-    ends = scan_states(lax.all_to_all(sent, "ctx", 0, 0))
-    end = lax.all_to_all(ends, "ctx", 0, 0).reshape(H * D, N)
+    at = lax.axis_index("ctx")
+    odd = lax.rem(at, 2)
+    edge = jnp.logical_or(at == 0, at == blocks - 1)
+    flags = jnp.stack([1 - odd, odd, 1 - edge.astype(jnp.int32)]).astype(F32)
+    flags = jnp.broadcast_to(jnp.pad(flags, (0, 5))[:, None], (8, N))
+    odd = odd[None]
+    inward = [(i, i ^ 1) for i in range(blocks)]
+    across = [(i, (i + 1 if i % 2 else i - 1) % blocks) for i in range(blocks)]
+    alike = [list(range(0, blocks, 2)), list(range(1, blocks, 2))]
+
+    own, own_total, first, second = block_states(odd, cot, out_map, raw, decay_row, bias_row)
+    first = lax.ppermute(first, "ctx", inward)
+    second = lax.ppermute(second, "ctx", across)
+    by_decay, by_bias, sig_high, sig_low, sig_turned = prepared_part(
+        sig, in_map, raw, decay_row, bias_row, start, own_total
+    )
+    sent, other_total, other = combine_states(
+        flags, own, own_total, first, second, sig_turned, blocks // 2
+    )
+    states = lax.all_to_all(sent, "ctx", 0, 0, axis_index_groups=alike)
+    operands = (sig, cot, in_map, out_map, raw, decay_row, bias_row, skip_row, start)
+    *begun, token = inner_part(range(INNER_FIRST), *operands, other)
+    ends = scan_states(odd, states, token)
     (
         sig_part,
         in_part,
         out_grad,
         step_part,
-        by_decay,
-        by_bias,
         sums_here,
         carry,
         leave,
         slope,
-        sig_high,
-        sig_low,
-        sig_turned,
-    ) = inner_part(sig, cot, in_map, out_map, raw, decay_row, bias_row, skip_row, start)
+        token,
+    ) = inner_part(range(INNER_FIRST, G), *operands, ends, begun)
+    ends = lax.all_to_all(ends, "ctx", 0, 0, axis_index_groups=alike)
+    own, first, second = expand_ends(flags, ends, other_total, other, token)
+    first = lax.ppermute(first, "ctx", inward)
+    second = lax.ppermute(second, "ctx", across)
 
     devices = blocks * deals
-    sums = local_sums(end, by_decay, by_bias, sums_here)[:2]
+    sums = local_sums(odd, own, first, second, sums_here, by_decay, by_bias)[:2]
     sums = sums + lax.ppermute(sums, "dp", [(i, i ^ 1) for i in range(deals)])
     cores = [
         [d * blocks + c for d in range(core, deals, 2) for c in range(blocks)] for core in range(2)
@@ -639,7 +895,10 @@
     sent = jnp.broadcast_to(sums[None], (devices // 2, 2, N))
     received = lax.all_to_all(sent, ("dp", "ctx"), 0, 0, axis_index_groups=cores)
     step_grad, sig_grad, in_grad = finish_part(
-        end,
+        odd,
+        own,
+        first,
+        second,
         sums_here,
         carry,
         leave,

time: 151 us -> 137 us (0.907)
  blocking collectives: 63.8 us -> 0 us
  starting transfers between devices: 16.9 us -> 41.3 us
  waiting for transfers between devices: 18.5 us -> 33 us
  Pallas kernels: 49.3 us -> 60.2 us
    all_to_all x1 -> x0, blocking collectives: 63.8 us -> none  [local(): ends = scan_states(lax.all_to_all(sent, 'ctx', 0, 0))]
    ppermute x0 -> x4, starting transfers between devices: none -> 19.2 us  [the longest x2 10.5 us: local(): first = lax.ppermute(first, 'ctx', inward)]
    ppermute x0 -> x4, waiting for transfers between devices: none -> 13.8 us  [the longest x2 8.66 us: local(): first = lax.ppermute(first, 'ctx', inward)]
    pallas_call x5 -> x9, Pallas kernels: 49.3 us -> 60.2 us  [call(): pl.pallas_call(kernel, grid=(grid,) if grid else (), in_specs=ins, out_sp...]
    all_to_all x1 -> x2, starting transfers between devices: 4.24 us -> 10.6 us  [the longest x1 5.64 us: local(): ends = lax.all_to_all(ends, 'ctx', 0, 0, axis_index_groups=alike)]
    all_to_all x1 -> x2, waiting for transfers between devices: 14.3 us -> 15.1 us  [the longest x1 7.62 us: local(): ends = lax.all_to_all(ends, 'ctx', 0, 0, axis_index_groups=alike)]
  transfers between devices with their start and end apart: 3 -> 8, of which waited for: 3 -> 7; matrix products, arithmetic and copies ran while one was open for 0% -> 0% of each run, Pallas kernels for 28% -> 37%
where the time goes in v5:
time: 137 us
  Pallas kernels  60.2 us (44%)
  starting transfers between devices  41.3 us (30%)
  waiting for transfers between devices  33 us (24%)
    pallas_call x9, Pallas kernels, call(): pl.pallas_call(kernel, grid=(grid,) if grid else (), in_specs=ins, out_sp...  60.2 us
    ppermute x2, starting transfers between devices, local(): first = lax.ppermute(first, 'ctx', inward)  10.5 us
    ppermute x2, starting transfers between devices, local(): second = lax.ppermute(second, 'ctx', across)  8.75 us
    ppermute x2, waiting for transfers between devices, local(): first = lax.ppermute(first, 'ctx', inward)  8.66 us
    all_to_all x1, starting transfers between devices, local(): lax.all_to_all(sent, ('dp', 'ctx'), 0, 0, axis_index_groups=cores)  8.18 us
    all_to_all x1, waiting for transfers between devices, local(): ends = lax.all_to_all(ends, 'ctx', 0, 0, axis_index_groups=alike)  7.62 us
    all_to_all x1, waiting for transfers between devices, local(): states = lax.all_to_all(sent, 'ctx', 0, 0, axis_index_groups=alike)  7.46 us
    all_to_all x1, starting transfers between devices, local(): ends = lax.all_to_all(ends, 'ctx', 0, 0, axis_index_groups=alike)  5.64 us
  transfers between devices with their start and end apart: 8, of which 7 were waited for; matrix products, arithmetic and copies ran while one was open for 0% of the time, Pallas kernels for 37%

profile of v5, /device:TPU:1, one launch (start us, length us, event | category | flops | bytes accessed | tf_op | source)
XLA Modules:
  0.0 136.8 jit_solution(11483344205653093382)
XLA Ops:
  0.6 3.1 %shard_map.144 = (f32[2048,128]{1,0:T(8,128)S(1)}, f32[32,128]{1,0:T(8,128)S(1)}, f32[1040,128]{1,0:T(8,128)S(1)}, f32[1040,128]{1,0:T(8,128)S(1)}) custom-call(s32[1]{0:T(128)} %bitcast.odd_ref, bf16[256,4096]{1,0:T(8,128)(2,1)} %bitcast.22, bf16[256,1024]{1,0:T(8,128)(2,1)} %bitcast.33, f32[64,256]{1,0:T(8,128)} %bitcast.36, f32[1,64]{1,0:T(1,128)} %bitcast.40, ...), custom_call_target="tpu_custom_call" | custom-call | flops 536870912 | bytes 4817412 | tf_op jit(solution)/shard_map/pallas_call | solution.py:590
  3.8 2.6 %collective-permute-start = (f32[1040,128]{1,0:T(8,128)S(1)}, f32[1040,128]{1,0:T(8,128)S(1)}, u32[]{:S(2)}, u32[]{:S(2)}) collective-permute-start(f32[1040,128]{1,0:T(8,128)S(1)} %get-tuple-element.45), channel_id=1, source_target_pairs={{0,1},{1,0},{2,3},{3,2},{4,5},{5,4},{6,7},{7,6},{8,9},{9,8},{10,11... | collective-permute-start | bytes 1597448 | tf_op jit(solution)/shard_map/ppermute | solution.py:861
  6.3 7.1 %collective-permute-start.1 = (f32[1040,128]{1,0:T(8,128)S(1)}, f32[1040,128]{1,0:T(8,128)S(1)}, u32[]{:S(2)}, u32[]{:S(2)}) collective-permute-start(f32[1040,128]{1,0:T(8,128)S(1)} %get-tuple-element.46), channel_id=1, source_target_pairs={{0,15},{1,2},{2,1},{3,4},{4,3},{5,6},{6,5},{7,8},{8,7},{9,10},{10,... | collective-permute-start | bytes 1597448 | tf_op jit(solution)/shard_map/ppermute | solution.py:862
  13.5 0.1 add_convert_fusion
  13.5 10.8 %shard_map.145 = (f32[4096,128]{1,0:T(8,128)}, f32[4096,128]{1,0:T(8,128)}, bf16[256,4096]{1,0:T(8,128)(2,1)}, bf16[256,4096]{1,0:T(8,128)(2,1)}, bf16[4096,256]{1,0:T(8,128)(2,1)}) custom-call(bf16[256,4096]{1,0:T(8,128)(2,1)} %bitcast.49, bf16[256,1024]{1,0:T(8,128)(2,1)} %bitcast.29, f32[64,256]{1,0:T(8,128)} %bitcast.37, f32[1,64]{1,0:T(1,128)} %bitcast.41, ...), custom_call_target="tpu_custom_call" | custom-call | flops 2684354560 | bytes 14238208 | tf_op jit(solution)/shard_map/pallas_call | solution.py:590
  24.3 0.0 collective-permute-done.first_ref
  24.3 0.7 collective-permute-done.1.second_ref
  25.0 0.1 broadcast_in_dim.37.flags_ref
  25.0 2.1 %shard_map.146 = (f32[8,264,128]{2,1,0:T(8,128)}, f32[32,128]{1,0:T(8,128)S(1)}, f32[2048,128]{1,0:T(8,128)}) custom-call(f32[8,128]{1,0:T(8,128)S(1)} %broadcast_in_dim.37.flags_ref, f32[2048,128]{1,0:T(8,128)S(1)} %get-tuple-element.43.own_ref, f32[32,128]{1,0:T(8,128)S(1)} %get-tuple-element.44.after_ref.own_total_ref, ...), custom_call_target="tpu_custom_call" | custom-call | flops 2097152 | bytes 6377472 | tf_op jit(solution)/shard_map/pallas_call | solution.py:590
  27.2 5.0 %all-to-all-start = ((f32[8,264,128]{2,1,0:T(8,128)}), f32[8,264,128]{2,1,0:T(8,128)S(1)}, u32[]{:S(2)}, u32[]{:S(2)}) async-start(f32[8,264,128]{2,1,0:T(8,128)} %get-tuple-element.48), calls=%async_computation | async-start | bytes 2162688 | tf_op jit(solution)/shard_map/all_to_all | solution.py:869
  32.2 15.6 %shard_map.147 = (f32[256,4096]{1,0:T(8,128)}, f32[256,1024]{1,0:T(8,128)}, f32[256,1024]{1,0:T(8,128)}, f32[64,256]{1,0:T(8,128)S(1)}, f32[64,128]{1,0:T(8,128)...) custom-call(bf16[256,4096]{1,0:T(8,128)(2,1)} %bitcast.50, ...), custom_call_target="tpu_custom_call" | custom-call | flops 4026531840 | bytes 13996800 | tf_op jit(solution)/shard_map/pallas_call | solution.py:590
  47.8 7.5 %all-to-all-done.state_ref = f32[8,264,128]{2,1,0:T(8,128)S(1)} async-done(((f32[8,264,128]{2,1,0:T(8,128)}), f32[8,264,128]{2,1,0:T(8,128)S(1)}, u32[]{:S(2)}, u32[]{:S(2)}) %all-to-all-start) | async-done | bytes 1081376 | tf_op jit(solution)/shard_map/all_to_all | solution.py:869
  55.2 1.1 shard_map.148.after_ref
  56.3 5.6 %all-to-all-start.1 = ((f32[8,256,128]{2,1,0:T(8,128)}), f32[8,256,128]{2,1,0:T(8,128)S(1)}, u32[]{:S(2)}, u32[]{:S(2)}) async-start(f32[8,256,128]{2,1,0:T(8,128)} %shard_map.148.after_ref), calls=%async_computation.1 | async-start | bytes 2097152 | tf_op jit(solution)/shard_map/all_to_all | solution.py:884
  62.0 15.6 %shard_map.149 = (f32[256,4096]{1,0:T(8,128)}, f32[256,1024]{1,0:T(8,128)}, f32[256,1024]{1,0:T(8,128)}, f32[64,256]{1,0:T(8,128)S(1)}, f32[64,128]{1,0:T(8,128)...) custom-call(bf16[256,4096]{1,0:T(8,128)(2,1)} %bitcast.51, ...), custom_call_target="tpu_custom_call", output_to_operand_aliasing={{0}: (10, {}), {1}: (11, {}), {2}: (12, {}), {3}: (13, {}),... | custom-call | flops 4026531840 | bytes 20583168 | tf_op jit(solution)/shard_map/pallas_call | solution.py:590
  77.5 7.6 %all-to-all-done.1.end_ref = f32[8,256,128]{2,1,0:T(8,128)S(1)} async-done(((f32[8,256,128]{2,1,0:T(8,128)}), f32[8,256,128]{2,1,0:T(8,128)S(1)}, u32[]{:S(2)}, u32[]{:S(2)}) %all-to-all-start.1) | async-done | bytes 1048608 | tf_op jit(solution)/shard_map/all_to_all | solution.py:884
  85.1 1.3 shard_map.150
  86.4 7.9 %collective-permute-start.2 = (f32[1024,128]{1,0:T(8,128)S(1)}, f32[1024,128]{1,0:T(8,128)S(1)}, u32[]{:S(2)}, u32[]{:S(2)}) collective-permute-start(f32[1024,128]{1,0:T(8,128)S(1)} %get-tuple-element.62), channel_id=1, source_target_pairs={{0,1},{1,0},{2,3},{3,2},{4,5},{5,4},{6,7},{7,6},{8,9},{9,8},{10,11... | collective-permute-start | bytes 1572872 | tf_op jit(solution)/shard_map/ppermute | solution.py:886
  94.4 1.6 %collective-permute-start.3 = (f32[1024,128]{1,0:T(8,128)S(1)}, f32[1024,128]{1,0:T(8,128)S(1)}, u32[]{:S(2)}, u32[]{:S(2)}) collective-permute-start(f32[1024,128]{1,0:T(8,128)S(1)} %get-tuple-element.63), channel_id=1, source_target_pairs={{0,15},{1,2},{2,1},{3,4},{4,3},{5,6},{6,5},{7,8},{8,7},{9,10},{10,... | collective-permute-start | bytes 1572872 | tf_op jit(solution)/shard_map/ppermute | solution.py:887
  96.0 8.7 %collective-permute-done.2.first_ref = f32[1024,128]{1,0:T(8,128)S(1)} collective-permute-done((f32[1024,128]{1,0:T(8,128)S(1)}, f32[1024,128]{1,0:T(8,128)S(1)}, u32[]{:S(2)}, u32[]{:S(2)}) %collective-permute-start.2) | collective-permute-done | bytes 524320 | tf_op jit(solution)/shard_map/ppermute | solution.py:886
  104.7 4.5 %collective-permute-done.3.second_ref = f32[1024,128]{1,0:T(8,128)S(1)} collective-permute-done((f32[1024,128]{1,0:T(8,128)S(1)}, f32[1024,128]{1,0:T(8,128)S(1)}, u32[]{:S(2)}, u32[]{:S(2)}) %collective-permute-start.3) | collective-permute-done | bytes 524320 | tf_op jit(solution)/shard_map/ppermute | solution.py:887
  109.2 2.6 %shard_map.152 = f32[8,128]{1,0:T(8,128)S(1)} custom-call(s32[1]{0:T(128)} %bitcast.odd_ref, f32[2048,128]{1,0:T(8,128)S(1)} %get-tuple-element.61.own_ref, f32[1024,128]{1,0:T(8,128)S(1)} %collective-permute-done.2.first_ref, f32[1024,128]{1,0:T(8,128)S(1)} %collective-permute-done.3.second_ref, f32[64,128]{1,0:T(8,128)S(1)} %get-tuple-element.64.sums_ref, ...), custom_call_target="tpu_custom_call" | custom-call | flops 2097152 | bytes 6328324 | tf_op jit(solution)/shard_map/pallas_call | solution.py:590
  111.8 3.2 %collective-permute-start.4 = (f32[2,128]{1,0:T(2,128)S(1)}, f32[2,128]{1,0:T(2,128)S(1)}, u32[]{:S(2)}, u32[]{:S(2)}) collective-permute-start(f32[2,128]{1,0:T(2,128)S(1)} %slice.12), channel_id=1, source_target_pairs={{0,16},{16,0},{32,48},{48,32},{64,80},{80,64},{96,112},{112,96},{1... | collective-permute-start | bytes 3080 | tf_op jit(solution)/shard_map/ppermute | solution.py:891
  115.1 0.8 collective-permute-done.4
  115.9 0.7 broadcast_in_dim.45
  116.6 8.2 %all-to-all-start.2 = ((f32[128,2,128]{2,1,0:T(2,128)}), f32[128,2,128]{2,1,0:T(2,128)S(1)}, u32[]{:S(2)}, u32[]{:S(2)}) async-start(f32[128,2,128]{2,1,0:T(2,128)} %broadcast_in_dim.45), calls=%async_computation.2 | async-start | bytes 262144 | tf_op jit(solution)/shard_map/all_to_all | solution.py:896
  124.8 8.0 %shard_map.151 = (f32[64,256]{1,0:T(8,128)}, f32[256,4096]{1,0:T(8,128)}, f32[256,1024]{1,0:T(8,128)}) custom-call(s32[1]{0:T(128)} %bitcast.odd_ref, f32[2048,128]{1,0:T(8,128)S(1)} %get-tuple-element.61.own_ref, f32[1024,128]{1,0:T(8,128)S(1)} %collective-permute-done.2.first_ref, f32[1024,128]{1,0:T(8,128)S(1)} %collective-permute-done.3.second_ref, ...), custom_call_target="tpu_custom_call" | custom-call | flops 1879048192 | bytes 20807684 | tf_op jit(solution)/shard_map/pallas_call | solution.py:590
  132.8 3.2 %all-to-all-done.2 = f32[128,2,128]{2,1,0:T(2,128)S(1)} async-done(((f32[128,2,128]{2,1,0:T(2,128)}), f32[128,2,128]{2,1,0:T(2,128)S(1)}, u32[]{:S(2)}, u32[]{:S(2)}) %all-to-all-start.2) | async-done | bytes 131104 | tf_op jit(solution)/shard_map/all_to_all | solution.py:896
  136.1 0.1 reduce_sum.9
  136.2 0.6 slice_bitcast_fusion
  (4 shorter events, 0.0 us)
Async XLA Ops:
  3.8 20.5 %collective-permute-start = (f32[1040,128]{1,0:T(8,128)S(1)}, f32[1040,128]{1,0:T(8,128)S(1)}, u32[]{:S(2)}, u32[]{:S(2)}) collective-permute-start(f32[1040,128]{1,0:T(8,128)S(1)} %get-tuple-element.45), channel_id=1, source_target_pairs={{0,1},{1,0},{2,3},{3,2},{4,5},{5,4},{6,7},{7,6},{8,9},{9,8},{10,11... | collective-permute-start | bytes 1597448 | tf_op jit(solution)/shard_map/ppermute | solution.py:861
  6.3 18.6 %collective-permute-start.1 = (f32[1040,128]{1,0:T(8,128)S(1)}, f32[1040,128]{1,0:T(8,128)S(1)}, u32[]{:S(2)}, u32[]{:S(2)}) collective-permute-start(f32[1040,128]{1,0:T(8,128)S(1)} %get-tuple-element.46), channel_id=1, source_target_pairs={{0,15},{1,2},{2,1},{3,4},{4,3},{5,6},{6,5},{7,8},{8,7},{9,10},{10,... | collective-permute-start | bytes 1597448 | tf_op jit(solution)/shard_map/ppermute | solution.py:862
  27.2 28.0 %all-to-all-start = ((f32[8,264,128]{2,1,0:T(8,128)}), f32[8,264,128]{2,1,0:T(8,128)S(1)}, u32[]{:S(2)}, u32[]{:S(2)}) async-start(f32[8,264,128]{2,1,0:T(8,128)} %get-tuple-element.48), calls=%async_computation | async-start | bytes 2162688 | tf_op jit(solution)/shard_map/all_to_all | solution.py:869
  56.3 28.8 %all-to-all-start.1 = ((f32[8,256,128]{2,1,0:T(8,128)}), f32[8,256,128]{2,1,0:T(8,128)S(1)}, u32[]{:S(2)}, u32[]{:S(2)}) async-start(f32[8,256,128]{2,1,0:T(8,128)} %shard_map.148.after_ref), calls=%async_computation.1 | async-start | bytes 2097152 | tf_op jit(solution)/shard_map/all_to_all | solution.py:884
  86.4 18.2 %collective-permute-start.2 = (f32[1024,128]{1,0:T(8,128)S(1)}, f32[1024,128]{1,0:T(8,128)S(1)}, u32[]{:S(2)}, u32[]{:S(2)}) collective-permute-start(f32[1024,128]{1,0:T(8,128)S(1)} %get-tuple-element.62), channel_id=1, source_target_pairs={{0,1},{1,0},{2,3},{3,2},{4,5},{5,4},{6,7},{7,6},{8,9},{9,8},{10,11... | collective-permute-start | bytes 1572872 | tf_op jit(solution)/shard_map/ppermute | solution.py:886
  94.4 14.8 %collective-permute-start.3 = (f32[1024,128]{1,0:T(8,128)S(1)}, f32[1024,128]{1,0:T(8,128)S(1)}, u32[]{:S(2)}, u32[]{:S(2)}) collective-permute-start(f32[1024,128]{1,0:T(8,128)S(1)} %get-tuple-element.63), channel_id=1, source_target_pairs={{0,15},{1,2},{2,1},{3,4},{4,3},{5,6},{6,5},{7,8},{8,7},{9,10},{10,... | collective-permute-start | bytes 1572872 | tf_op jit(solution)/shard_map/ppermute | solution.py:887
  111.8 4.1 %collective-permute-start.4 = (f32[2,128]{1,0:T(2,128)S(1)}, f32[2,128]{1,0:T(2,128)S(1)}, u32[]{:S(2)}, u32[]{:S(2)}) collective-permute-start(f32[2,128]{1,0:T(2,128)S(1)} %slice.12), channel_id=1, source_target_pairs={{0,16},{16,0},{32,48},{48,32},{64,80},{80,64},{96,112},{112,96},{1... | collective-permute-start | bytes 3080 | tf_op jit(solution)/shard_map/ppermute | solution.py:891
  116.6 19.5 %all-to-all-start.2 = ((f32[128,2,128]{2,1,0:T(2,128)}), f32[128,2,128]{2,1,0:T(2,128)S(1)}, u32[]{:S(2)}, u32[]{:S(2)}) async-start(f32[128,2,128]{2,1,0:T(2,128)} %broadcast_in_dim.45), calls=%async_computation.2 | async-start | bytes 262144 | tf_op jit(solution)/shard_map/all_to_all | solution.py:896

commit v6 on v5

--- a/solution.py
+++ b/solution.py
@@ -19,9 +19,11 @@
 BF16 = jnp.bfloat16
 MIB = 1024 * 1024
 STATE_BATCH = 4
+OWN = (0, 1, 2, 3)
+MET = (4, 5, 6, 7)
 INNER_FIRST = 4
 SUMS_BATCH = 2
-FINISH_BATCH = 3
+FINISH_BATCH = 2
 
 
 def split(x, parts):
@@ -91,8 +93,8 @@
     return copies
 
 
-def batches(size):
-    return [range(g, min(g + size, G)) for g in range(0, G, size)]
+def batches(size, count):
+    return [range(k, min(k + size, count)) for k in range(0, count, size)]
 
 
 def group_of(slot, odd):
@@ -149,7 +151,7 @@
     bias_column = column_of(bias[...], 0, H)
     decay_log = column_of(decay[...], 0, H)
     entries[...] = jnp.exp(steps_of(raw[...], bias_column, decay_log)[3])
-    for batch in batches(STATE_BATCH):
+    for batch in batches(STATE_BATCH, G):
         for k in batch:
             copies[2 * k + 3].wait()
             copies[2 * k + 4].wait()
@@ -179,8 +181,8 @@
     flags_ref,
     own_ref,
     own_total_ref,
+    second_ref,
     first_ref,
-    second_ref,
     after_ref,
     sent_ref,
     other_total_ref,
@@ -194,6 +196,7 @@
     got = per_half // each
     totals = [[] for _ in range(each)]
     other_totals = []
+    leaving = []
     for half, ref in enumerate((first_ref, second_ref)):
         earlier, keep = halves[half]
         for h in range(per_half):
@@ -209,14 +212,20 @@
             totals[at].append(total * met_total)
             other[mine * D : (mine + 1) * D, :] = jnp.where(earlier > 0, met, state)
             other_totals.append(jnp.where(earlier > 0, met_total, total))
+            if h % PER == PER - 1:
+                part = wide(mine // PER)
+                copy = pltpu.make_async_copy(
+                    other.at[part], other_ref.at[part], gone.at[mine // PER]
+                )
+                copy.start()
+                leaving.append(copy)
     rows = 2 * got
     for at in range(each):
         pad = [jnp.zeros((8 - rows, N), F32)]
         sent_ref[at, rows * D :, :] = jnp.concatenate(totals[at] + pad, axis=0)
     other_total_ref[...] = jnp.concatenate(other_totals, axis=0)
-    copy = pltpu.make_async_copy(other, other_ref, gone.at[0])
-    copy.start()
-    copy.wait()
+    for copy in leaving:
+        copy.wait()
 
 
 def scan_kernel(odd_ref, state_ref, after_ref, end_ref, end, gone):
@@ -438,17 +447,43 @@
         ref[...] = grown + (start * weight[:, :, None]).reshape(WIDE, N)
 
 
-def end_of(slot, own_ref, first_ref, second_ref):
-    if slot < 4:
-        return own_ref[wide(slot), :]
-    return first_ref[wide(slot - 4), :] if slot < 6 else second_ref[wide(slot - 6), :]
+def add_sums(slots, odd, ends, sums_ref, sources, targets, kept, got):
+    pairs = []
+    for k, slot in enumerate(slots):
+        at = chosen(group_of(slot, odd), WIDE)
+        for source, target in zip(sources, targets, strict=True):
+            pairs.append((source.at[at], target.at[wide(k)]))
+    copies = fetch(got, pairs)
+    which = lax.broadcasted_iota(jnp.int32, (PER, N), 1)
+    for batch in batches(SUMS_BATCH, len(slots)):
+        for k in batch:
+            copies[2 * k].wait()
+            copies[2 * k + 1].wait()
+        for k in batch:
+            end = ends[k][...]
+            head = chosen(group_of(slots[k], odd), PER)
+            sums = sums_ref[head, :]
+            for column, held in enumerate(targets):
+                partial = jnp.sum((end * held[wide(k), :]).reshape(PER, D, N), axis=1)
+                partial = jnp.sum(partial, axis=1, keepdims=True)
+                sums = sums + jnp.where(which == column, partial, 0.0)
+            kept[head, :] = sums
+
+
+def own_sums_kernel(
+    odd_ref, own_ref, sums_ref, by_decay_ref, by_bias_ref, kept_ref, by_decay, by_bias, got
+):
+    ends = [own_ref.at[wide(k)] for k in range(4)]
+    kept_ref[...] = jnp.zeros_like(kept_ref)
+    sources, targets = (by_decay_ref, by_bias_ref), (by_decay, by_bias)
+    add_sums(OWN, odd_ref[0], ends, sums_ref, sources, targets, kept_ref, got)
 
 
 def sums_kernel(
     odd_ref,
-    own_ref,
+    second_ref,
     first_ref,
-    second_ref,
+    kept_ref,
     sums_ref,
     by_decay_ref,
     by_bias_ref,
@@ -458,74 +493,35 @@
     kept,
     got,
 ):
-    odd = odd_ref[0]
-    pairs = []
-    for slot in range(G):
-        at = chosen(group_of(slot, odd), WIDE)
-        pairs.append((by_decay_ref.at[at], by_decay.at[wide(slot)]))
-        pairs.append((by_bias_ref.at[at], by_bias.at[wide(slot)]))
-    copies = fetch(got, pairs)
-    which = lax.broadcasted_iota(jnp.int32, (PER, N), 1)
-    kept[...] = jnp.zeros_like(kept)
-    for batch in batches(SUMS_BATCH):
-        for slot in batch:
-            copies[2 * slot].wait()
-            copies[2 * slot + 1].wait()
-        for slot in batch:
-            end = end_of(slot, own_ref, first_ref, second_ref)
-            head = chosen(group_of(slot, odd), PER)
-            sums = sums_ref[head, :]
-            for k, held in enumerate((by_decay, by_bias)):
-                partial = jnp.sum((end * held[wide(slot), :]).reshape(PER, D, N), axis=1)
-                sums = sums + jnp.where(which == k, jnp.sum(partial, axis=1, keepdims=True), 0.0)
-            kept[head, :] = sums
+    ends = [ref.at[wide(k)] for ref in (first_ref, second_ref) for k in range(2)]
+    kept[...] = kept_ref[...]
+    sources, targets = (by_decay_ref, by_bias_ref), (by_decay, by_bias)
+    add_sums(MET, odd_ref[0], ends, sums_ref, sources, targets, kept, got)
     rows = jnp.transpose(kept[...])
     first = jnp.concatenate([rows[0:1, :H], rows[1:2, :H]], axis=1)
     odd = lax.broadcasted_iota(jnp.int32, (8, N), 0) % 2 == 1
     sent_ref[...] = jnp.where(odd, rows[2:3], first)
 
 
-def finish_kernel(
-    odd_ref,
-    own_ref,
-    first_ref,
-    second_ref,
-    sums_ref,
-    carry_ref,
-    leave_ref,
-    slope_ref,
-    step_part_ref,
-    in_ref,
-    sig_turned_ref,
-    start_ref,
-    sig_part_ref,
-    sig_high_ref,
-    sig_low_ref,
-    in_part_ref,
-    step_grad_ref,
-    sig_grad_ref,
-    in_grad_ref,
-    in_maps,
-    sig_turned,
-    start,
-    sig_part,
-    sig_high,
-    sig_low,
-    in_part,
-    step_grads,
-    sig_grad,
-    in_grad,
-    got,
-    gone,
-):
+def finish_kernel(odd_ref, own_ref, second_ref, first_ref, *refs):
+    slots = OWN + MET
+    ends = [own_ref.at[wide(k)] for k in range(4)]
+    ends += [ref.at[wide(k)] for ref in (first_ref, second_ref) for k in range(2)]
+    sums_ref, carry_ref, leave_ref, slope_ref, step_part_ref = refs[:5]
+    in_ref, sig_turned_ref, start_ref, sig_part_ref, sig_high_ref, sig_low_ref, in_part_ref = refs[
+        5:12
+    ]
+    step_grad_ref, sig_grad_ref, in_grad_ref = refs[-15:-12]
+    in_maps, sig_turned, start, sig_part, sig_high, sig_low, in_part = refs[-12:-5]
+    step_grads, sig_grad, in_grad, got, gone = refs[-5:]
     odd = odd_ref[0]
     pairs = []
     every = slice(None)
-    for slot in range(G):
+    for k, slot in enumerate(slots):
         g = group_of(slot, odd)
-        cols = ((every, chosen(g, WIDE)), (every, wide(slot)))
-        rows = ((chosen(g, WIDE),), (wide(slot),))
-        few = ((every, chosen(g, N)), (every, narrow(slot)))
+        cols = ((every, chosen(g, WIDE)), (every, wide(k)))
+        rows = ((chosen(g, WIDE),), (wide(k),))
+        few = ((every, chosen(g, N)), (every, narrow(k)))
         for (there, here), source, target in (
             (few, in_ref, in_maps),
             (cols, sig_part_ref, sig_part),
@@ -536,18 +532,18 @@
             (few, in_part_ref, in_part),
         ):
             pairs.append((source.at[there], target.at[here]))
-    each = len(pairs) // G
+    each = len(pairs) // len(slots)
     copies = fetch(got, pairs)
     earlier = mask_of(lambda i, j: i < j)
     leaving = []
-    for batch in batches(FINISH_BATCH):
-        for g in batch:
-            for copy in copies[each * g : each * (g + 1)]:
+    for batch in batches(FINISH_BATCH, len(slots)):
+        for k in batch:
+            for copy in copies[each * k : each * (k + 1)]:
                 copy.wait()
-        for g in batch:
-            head = chosen(group_of(g, odd), PER)
-            end = end_of(g, own_ref, first_ref, second_ref)
-            in_map = in_maps[:, narrow(g)]
+        for k in batch:
+            head = chosen(group_of(slots[k], odd), PER)
+            end = ends[k][...]
+            in_map = in_maps[:, narrow(k)]
             carry = carry_ref[head, :]
             columns_here = sums_ref[head, :]
             total = columns_here[:, 3:4]
@@ -555,31 +551,32 @@
             in_twice = jnp.concatenate([in_map, in_map], axis=1)
             end_high, end_low = split(end, 2)
             pieces = jnp.concatenate([end_high, end_low], axis=1)
-            sig_grad[:, wide(g)] = sig_part[:, wide(g)] + spread(carry) * mm_nt(in_twice, pieces)
-            both = mm(sig_high[:, wide(g)], pieces)
-            in_grad[:, narrow(g)] = in_part[:, narrow(g)] + (
-                both[:, :N] + (both[:, N:] + mm(sig_low[:, wide(g)], end_high))
+            sig_grad[:, wide(k)] = sig_part[:, wide(k)] + spread(carry) * mm_nt(in_twice, pieces)
+            both = mm(sig_high[:, wide(k)], pieces)
+            in_grad[:, narrow(k)] = in_part[:, narrow(k)] + (
+                both[:, :N] + (both[:, N:] + mm(sig_low[:, wide(k)], end_high))
             )
             turned = mm_nt(pieces, in_twice)
-            pushed = (sig_turned[wide(g), :].astype(F32) * turned).reshape(PER, D, T)
+            pushed = (sig_turned[wide(k), :].astype(F32) * turned).reshape(PER, D, T)
             pushed = jnp.sum(pushed, axis=1)
             before = rows_times_mask(carry * pushed, earlier)
-            held = jnp.sum((end * start[wide(g), :].astype(F32)).reshape(PER, D, N), axis=1)
+            held = jnp.sum((end * start[wide(k), :].astype(F32)).reshape(PER, D, N), axis=1)
             held = total * jnp.sum(held, axis=1, keepdims=True)
             step_grad = leave_ref[head, :] * pushed - decay * (before + held)
-            step_grads[head, :] = (step_part_ref[head, :] + step_grad) * slope_ref[head, :]
-        for g in batch:
-            there = group_of(g, odd)
-            for k, (source, target) in enumerate(
+            step_grads[k * PER : (k + 1) * PER, :] = (
+                step_part_ref[head, :] + step_grad
+            ) * slope_ref[head, :]
+        for k in batch:
+            g = group_of(slots[k], odd)
+            for at, (source, target) in enumerate(
                 (
-                    (sig_grad.at[:, wide(g)], sig_grad_ref.at[:, chosen(there, WIDE)]),
-                    (in_grad.at[:, narrow(g)], in_grad_ref.at[:, chosen(there, N)]),
+                    (sig_grad.at[:, wide(k)], sig_grad_ref.at[:, chosen(g, WIDE)]),
+                    (in_grad.at[:, narrow(k)], in_grad_ref.at[:, chosen(g, N)]),
+                    (step_grads.at[pl.ds(k * PER, PER)], step_grad_ref.at[chosen(g, PER)]),
                 )
             ):
-                leaving.append(pltpu.make_async_copy(source, target, gone.at[2 * g + k]))
+                leaving.append(pltpu.make_async_copy(source, target, gone.at[3 * k + at]))
                 leaving[-1].start()
-    leaving.append(pltpu.make_async_copy(step_grads, step_grad_ref, gone.at[2 * G]))
-    leaving[-1].start()
     for copy in leaving:
         copy.wait()
 
@@ -674,10 +671,10 @@
             (HERE, f32_near(H // 2, N)),
             (ELSEWHERE, f32(H * D // 2, N)),
         ],
-        near(flags, own, own_total, first, second) + far(after),
+        near(flags, own, own_total, second, first) + far(after),
         4 * H * D * N,
         16,
-        [pltpu.VMEM((H * D // 2, N), F32), COPIES((1,))],
+        [pltpu.VMEM((H * D // 2, N), F32), COPIES((4,))],
     )
 
 
@@ -764,56 +761,50 @@
     )
 
 
-def local_sums(odd, own, first, second, sums, by_decay, by_bias):
+def own_sums(odd, own, sums, by_decay, by_bias):
+    return call(
+        own_sums_kernel,
+        0,
+        [SCALAR, HERE, HERE, ELSEWHERE, ELSEWHERE],
+        [(HERE, f32_near(N, N))],
+        [odd] + near(own, sums) + far(by_decay, by_bias),
+        2 * H * D * N,
+        12,
+        [pltpu.VMEM((H * D // 2, N), F32), pltpu.VMEM((H * D // 2, N), F32), COPIES((G,))],
+    )[0]
+
+
+def all_sums(odd, first, second, kept, sums, by_decay, by_bias):
     return call(
         sums_kernel,
         0,
         [SCALAR] + [HERE] * 4 + [ELSEWHERE] * 2,
         [(HERE, f32_near(8, N))],
-        [odd] + near(own, first, second, sums) + far(by_decay, by_bias),
-        4 * H * D * N,
-        16,
+        [odd] + near(second, first, kept, sums) + far(by_decay, by_bias),
+        2 * H * D * N,
+        12,
         [
-            pltpu.VMEM((H * D, N), F32),
-            pltpu.VMEM((H * D, N), F32),
+            pltpu.VMEM((H * D // 2, N), F32),
+            pltpu.VMEM((H * D // 2, N), F32),
             pltpu.VMEM((N, N), F32),
-            COPIES((2 * G,)),
+            COPIES((G,)),
         ],
     )[0]
 
 
-def finish_part(
-    odd,
-    own,
-    first,
-    second,
-    sums,
-    carry,
-    leave,
-    slope,
-    step_part,
-    in_map,
-    sig_turned,
-    start,
-    sig_part,
-    sig_high,
-    sig_low,
-    in_part,
-):
+def finish_part(odd, ends, rows, elsewhere):
     wide_float, narrow_float = pltpu.VMEM((T, H * D), F32), pltpu.VMEM((T, G * N), F32)
     wide_half = pltpu.VMEM((T, H * D), BF16)
     return call(
         finish_kernel,
         0,
-        [SCALAR] + [HERE] * 8 + [ELSEWHERE] * 7,
+        [SCALAR] + [HERE] * (len(ends) + len(rows)) + [ELSEWHERE] * len(elsewhere),
         [
             (ELSEWHERE, f32(H, T)),
             (ELSEWHERE, f32(T, H * D)),
             (ELSEWHERE, f32(T, G * N)),
         ],
-        [odd]
-        + near(own, first, second, sums, carry, leave, slope, step_part)
-        + far(in_map, sig_turned, start, sig_part, sig_high, sig_low, in_part),
+        [odd] + near(*ends, *rows) + far(*elsewhere),
         14 * H * D * N * T,
         36,
         [
@@ -828,7 +819,7 @@
             wide_float,
             narrow_float,
             COPIES((7 * G,)),
-            COPIES((2 * G + 1,)),
+            COPIES((3 * G,)),
         ],
     )
 
@@ -858,8 +849,8 @@
     alike = [list(range(0, blocks, 2)), list(range(1, blocks, 2))]
 
     own, own_total, first, second = block_states(odd, cot, out_map, raw, decay_row, bias_row)
+    second = lax.ppermute(second, "ctx", across)
     first = lax.ppermute(first, "ctx", inward)
-    second = lax.ppermute(second, "ctx", across)
     by_decay, by_bias, sig_high, sig_low, sig_turned = prepared_part(
         sig, in_map, raw, decay_row, bias_row, start, own_total
     )
@@ -883,34 +874,22 @@
     ) = inner_part(range(INNER_FIRST, G), *operands, ends, begun)
     ends = lax.all_to_all(ends, "ctx", 0, 0, axis_index_groups=alike)
     own, first, second = expand_ends(flags, ends, other_total, other, token)
+    second = lax.ppermute(second, "ctx", across)
     first = lax.ppermute(first, "ctx", inward)
-    second = lax.ppermute(second, "ctx", across)
-
+
+    kept = own_sums(odd, own, sums_here, by_decay, by_bias)
+
+    sums = all_sums(odd, first, second, kept, sums_here, by_decay, by_bias)[:2]
+    sums = sums + lax.ppermute(sums, "dp", [(i, i ^ 1) for i in range(deals)])
     devices = blocks * deals
-    sums = local_sums(odd, own, first, second, sums_here, by_decay, by_bias)[:2]
-    sums = sums + lax.ppermute(sums, "dp", [(i, i ^ 1) for i in range(deals)])
-    cores = [
-        [d * blocks + c for d in range(core, deals, 2) for c in range(blocks)] for core in range(2)
-    ]
+    equal = [[d * blocks + c for d in range(k, deals, 2) for c in range(blocks)] for k in range(2)]
     sent = jnp.broadcast_to(sums[None], (devices // 2, 2, N))
-    received = lax.all_to_all(sent, ("dp", "ctx"), 0, 0, axis_index_groups=cores)
+    received = lax.all_to_all(sent, ("dp", "ctx"), 0, 0, axis_index_groups=equal)
     step_grad, sig_grad, in_grad = finish_part(
         odd,
-        own,
-        first,
-        second,
-        sums_here,
-        carry,
-        leave,
-        slope,
-        step_part,
-        in_map,
-        sig_turned,
-        start,
-        sig_part,
-        sig_high,
-        sig_low,
-        in_part,
+        (own, second, first),
+        (sums_here, carry, leave, slope, step_part),
+        (in_map, sig_turned, start, sig_part, sig_high, sig_low, in_part),
     )
     summed = jnp.sum(received, axis=0) * (1.0 / (devices * T))
     return (

time: 137 us -> 136 us (level)
  waiting for transfers between devices: 33 us -> 25.2 us
  starting transfers between devices: 41.3 us -> 46.4 us
  Pallas kernels: 60.2 us -> 61.6 us
    ppermute x2, starting transfers between devices: 8.75 us -> 23.3 us  [local(): second = lax.ppermute(second, 'ctx', across)]
    ppermute x2, starting transfers between devices: 10.5 us -> 2.47 us  [local(): first = lax.ppermute(first, 'ctx', inward)]
    ppermute x2, waiting for transfers between devices: 8.66 us -> 3.22 us  [local(): first = lax.ppermute(first, 'ctx', inward)]
    all_to_all x1, waiting for transfers between devices: 7.62 us -> 2.95 us  [local(): ends = lax.all_to_all(ends, 'ctx', 0, 0, axis_index_groups=alike)]
    ppermute x2, waiting for transfers between devices: 5.17 us -> 7.64 us  [local(): second = lax.ppermute(second, 'ctx', across)]
    pallas_call x9 -> x10, Pallas kernels: 60.2 us -> 61.6 us  [call(): pl.pallas_call(kernel, grid=(grid,) if grid else (), in_specs=ins, out_sp...]
  transfers between devices with their start and end apart: 8 -> 8, of which waited for: 7 -> 8; matrix products, arithmetic and copies ran while one was open for 0% -> 0% of each run, Pallas kernels for 37% -> 38%
where the time goes in v6:
time: 136 us
  Pallas kernels  61.6 us (45%)
  starting transfers between devices  46.4 us (34%)
  waiting for transfers between devices  25.2 us (19%)
  local copies, waits for them, and re-layouts  1.36 us (1%)
    pallas_call x10, Pallas kernels, call(): pl.pallas_call(kernel, grid=(grid,) if grid else (), in_specs=ins, out_sp...  61.6 us
    ppermute x2, starting transfers between devices, local(): second = lax.ppermute(second, 'ctx', across)  23.3 us
    all_to_all x1, starting transfers between devices, local(): lax.all_to_all(sent, ('dp', 'ctx'), 0, 0, axis_index_groups=equal)  9.09 us
    all_to_all x1, waiting for transfers between devices, local(): states = lax.all_to_all(sent, 'ctx', 0, 0, axis_index_groups=alike)  7.74 us
    ppermute x2, waiting for transfers between devices, local(): second = lax.ppermute(second, 'ctx', across)  7.64 us
    all_to_all x1, starting transfers between devices, local(): ends = lax.all_to_all(ends, 'ctx', 0, 0, axis_index_groups=alike)  5.33 us
    all_to_all x1, starting transfers between devices, local(): states = lax.all_to_all(sent, 'ctx', 0, 0, axis_index_groups=alike)  4.15 us
    ppermute x2, waiting for transfers between devices, local(): first = lax.ppermute(first, 'ctx', inward)  3.22 us
  transfers between devices with their start and end apart: 8, of which 8 were waited for; matrix products, arithmetic and copies ran while one was open for 0% of the time, Pallas kernels for 38%

profile of v6, /device:TPU:1, one launch (start us, length us, event | category | flops | bytes accessed | tf_op | source)
XLA Modules:
  0.0 135.6 jit_solution(5325222003420338834)
XLA Ops:
  0.6 3.1 %shard_map.144 = (f32[2048,128]{1,0:T(8,128)S(1)}, f32[32,128]{1,0:T(8,128)S(1)}, f32[1040,128]{1,0:T(8,128)S(1)}, f32[1040,128]{1,0:T(8,128)S(1)}) custom-call(s32[1]{0:T(128)} %bitcast.odd_ref, bf16[256,4096]{1,0:T(8,128)(2,1)} %bitcast.22, bf16[256,1024]{1,0:T(8,128)(2,1)} %bitcast.33, f32[64,256]{1,0:T(8,128)} %bitcast.36, f32[1,64]{1,0:T(1,128)} %bitcast.40, ...), custom_call_target="tpu_custom_call" | custom-call | flops 536870912 | bytes 4817412 | tf_op jit(solution)/shard_map/pallas_call | solution.py:587
  3.8 8.9 %collective-permute-start = (f32[1040,128]{1,0:T(8,128)S(1)}, f32[1040,128]{1,0:T(8,128)S(1)}, u32[]{:S(2)}, u32[]{:S(2)}) collective-permute-start(f32[1040,128]{1,0:T(8,128)S(1)} %get-tuple-element.45), channel_id=1, source_target_pairs={{0,15},{1,2},{2,1},{3,4},{4,3},{5,6},{6,5},{7,8},{8,7},{9,10},{10,... | collective-permute-start | bytes 1597448 | tf_op jit(solution)/shard_map/ppermute | solution.py:852
  12.7 0.0 collective-permute-start.1
  12.7 0.1 add_convert_fusion
  12.8 10.8 %shard_map.145 = (f32[4096,128]{1,0:T(8,128)}, f32[4096,128]{1,0:T(8,128)}, bf16[256,4096]{1,0:T(8,128)(2,1)}, bf16[256,4096]{1,0:T(8,128)(2,1)}, bf16[4096,256]{1,0:T(8,128)(2,1)}) custom-call(bf16[256,4096]{1,0:T(8,128)(2,1)} %bitcast.49, bf16[256,1024]{1,0:T(8,128)(2,1)} %bitcast.29, f32[64,256]{1,0:T(8,128)} %bitcast.37, f32[1,64]{1,0:T(1,128)} %bitcast.41, ...), custom_call_target="tpu_custom_call" | custom-call | flops 2684354560 | bytes 14238208 | tf_op jit(solution)/shard_map/pallas_call | solution.py:587
  23.6 1.0 collective-permute-done.second_ref
  24.6 0.8 collective-permute-done.1.first_ref
  25.4 0.1 broadcast_in_dim.37.flags_ref
  25.4 2.1 %shard_map.146 = (f32[8,264,128]{2,1,0:T(8,128)}, f32[32,128]{1,0:T(8,128)S(1)}, f32[2048,128]{1,0:T(8,128)}) custom-call(f32[8,128]{1,0:T(8,128)S(1)} %broadcast_in_dim.37.flags_ref, f32[2048,128]{1,0:T(8,128)S(1)} %get-tuple-element.43.own_ref, f32[32,128]{1,0:T(8,128)S(1)} %get-tuple-element.44.after_ref.own_total_ref, ...), custom_call_target="tpu_custom_call" | custom-call | flops 2097152 | bytes 6377472 | tf_op jit(solution)/shard_map/pallas_call | solution.py:587
  27.5 4.1 %all-to-all-start = ((f32[8,264,128]{2,1,0:T(8,128)}), f32[8,264,128]{2,1,0:T(8,128)S(1)}, u32[]{:S(2)}, u32[]{:S(2)}) async-start(f32[8,264,128]{2,1,0:T(8,128)} %get-tuple-element.48), calls=%async_computation | async-start | bytes 2162688 | tf_op jit(solution)/shard_map/all_to_all | solution.py:860
  31.7 15.6 %shard_map.147 = (f32[256,4096]{1,0:T(8,128)}, f32[256,1024]{1,0:T(8,128)}, f32[256,1024]{1,0:T(8,128)}, f32[64,256]{1,0:T(8,128)S(1)}, f32[64,128]{1,0:T(8,128)...) custom-call(bf16[256,4096]{1,0:T(8,128)(2,1)} %bitcast.50, ...), custom_call_target="tpu_custom_call" | custom-call | flops 4026531840 | bytes 13996800 | tf_op jit(solution)/shard_map/pallas_call | solution.py:587
  47.3 7.7 %all-to-all-done.state_ref = f32[8,264,128]{2,1,0:T(8,128)S(1)} async-done(((f32[8,264,128]{2,1,0:T(8,128)}), f32[8,264,128]{2,1,0:T(8,128)S(1)}, u32[]{:S(2)}, u32[]{:S(2)}) %all-to-all-start) | async-done | bytes 1081376 | tf_op jit(solution)/shard_map/all_to_all | solution.py:860
  55.0 1.1 shard_map.148.after_ref
  56.1 5.3 %all-to-all-start.1 = ((f32[8,256,128]{2,1,0:T(8,128)}), f32[8,256,128]{2,1,0:T(8,128)S(1)}, u32[]{:S(2)}, u32[]{:S(2)}) async-start(f32[8,256,128]{2,1,0:T(8,128)} %shard_map.148.after_ref), calls=%async_computation.1 | async-start | bytes 2097152 | tf_op jit(solution)/shard_map/all_to_all | solution.py:875
  61.4 15.6 %shard_map.149 = (f32[256,4096]{1,0:T(8,128)}, f32[256,1024]{1,0:T(8,128)}, f32[256,1024]{1,0:T(8,128)}, f32[64,256]{1,0:T(8,128)S(1)}, f32[64,128]{1,0:T(8,128)...) custom-call(bf16[256,4096]{1,0:T(8,128)(2,1)} %bitcast.51, ...), custom_call_target="tpu_custom_call", output_to_operand_aliasing={{0}: (10, {}), {1}: (11, {}), {2}: (12, {}), {3}: (13, {}),... | custom-call | flops 4026531840 | bytes 20583168 | tf_op jit(solution)/shard_map/pallas_call | solution.py:587
  77.0 3.0 %all-to-all-done.1.end_ref = f32[8,256,128]{2,1,0:T(8,128)S(1)} async-done(((f32[8,256,128]{2,1,0:T(8,128)}), f32[8,256,128]{2,1,0:T(8,128)S(1)}, u32[]{:S(2)}, u32[]{:S(2)}) %all-to-all-start.1) | async-done | bytes 1048608 | tf_op jit(solution)/shard_map/all_to_all | solution.py:875
  80.0 1.3 shard_map.150
  81.3 14.3 %collective-permute-start.2 = (f32[1024,128]{1,0:T(8,128)S(1)}, f32[1024,128]{1,0:T(8,128)S(1)}, u32[]{:S(2)}, u32[]{:S(2)}) collective-permute-start(f32[1024,128]{1,0:T(8,128)S(1)} %get-tuple-element.62), channel_id=1, source_target_pairs={{0,15},{1,2},{2,1},{3,4},{4,3},{5,6},{6,5},{7,8},{8,7},{9,10},{10,... | collective-permute-start | bytes 1572872 | tf_op jit(solution)/shard_map/ppermute | solution.py:877
  95.6 2.5 %collective-permute-start.3 = (f32[1024,128]{1,0:T(8,128)S(1)}, f32[1024,128]{1,0:T(8,128)S(1)}, u32[]{:S(2)}, u32[]{:S(2)}) collective-permute-start(f32[1024,128]{1,0:T(8,128)S(1)} %get-tuple-element.63), channel_id=1, source_target_pairs={{0,1},{1,0},{2,3},{3,2},{4,5},{5,4},{6,7},{7,6},{8,9},{9,8},{10,11... | collective-permute-start | bytes 1572872 | tf_op jit(solution)/shard_map/ppermute | solution.py:878
  98.1 1.8 %shard_map.152.kept_ref = f32[128,128]{1,0:T(8,128)S(1)} custom-call(s32[1]{0:T(128)} %bitcast.odd_ref, f32[2048,128]{1,0:T(8,128)S(1)} %get-tuple-element.61.own_ref, f32[64,128]{1,0:T(8,128)S(1)} %get-tuple-element.64.refs_0_.sums_ref, f32[4096,128]{1,0:T(8,128)} %get-tuple-element.77.by_decay_ref, f32[4096,128]{1,0:T(8,128)} %get-tuple-element.78.by_bias_ref), custom_call_target="tpu_custom_call" | custom-call | flops 1048576 | bytes 5341188 | tf_op jit(solution)/shard_map/pallas_call | solution.py:587
  99.8 6.7 %collective-permute-done.2.second_ref = f32[1024,128]{1,0:T(8,128)S(1)} collective-permute-done((f32[1024,128]{1,0:T(8,128)S(1)}, f32[1024,128]{1,0:T(8,128)S(1)}, u32[]{:S(2)}, u32[]{:S(2)}) %collective-permute-start.2) | collective-permute-done | bytes 524320 | tf_op jit(solution)/shard_map/ppermute | solution.py:877
  106.5 2.4 %collective-permute-done.3.first_ref = f32[1024,128]{1,0:T(8,128)S(1)} collective-permute-done((f32[1024,128]{1,0:T(8,128)S(1)}, f32[1024,128]{1,0:T(8,128)S(1)}, u32[]{:S(2)}, u32[]{:S(2)}) %collective-permute-start.3) | collective-permute-done | bytes 524320 | tf_op jit(solution)/shard_map/ppermute | solution.py:878
  108.9 1.9 %shard_map.153 = f32[8,128]{1,0:T(8,128)S(1)} custom-call(s32[1]{0:T(128)} %bitcast.odd_ref, f32[1024,128]{1,0:T(8,128)S(1)} %collective-permute-done.2.second_ref, f32[1024,128]{1,0:T(8,128)S(1)} %collective-permute-done.3.first_ref, f32[128,128]{1,0:T(8,128)S(1)} %shard_map.152.kept_ref, f32[64,128]{1,0:T(8,128)S(1)} %get-tuple-element.64.refs_0_.sums_ref, ...), custom_call_target="tpu_custom_call" | custom-call | flops 1048576 | bytes 5345284 | tf_op jit(solution)/shard_map/pallas_call | solution.py:587
  110.9 2.1 %collective-permute-start.4 = (f32[2,128]{1,0:T(2,128)S(1)}, f32[2,128]{1,0:T(2,128)S(1)}, u32[]{:S(2)}, u32[]{:S(2)}) collective-permute-start(f32[2,128]{1,0:T(2,128)S(1)} %slice.12), channel_id=1, source_target_pairs={{0,16},{16,0},{32,48},{48,32},{64,80},{80,64},{96,112},{112,96},{1... | collective-permute-start | bytes 3080 | tf_op jit(solution)/shard_map/ppermute | solution.py:883
  113.0 0.8 collective-permute-done.4
  113.8 0.7 broadcast_in_dim.45
  114.5 9.1 %all-to-all-start.2 = ((f32[128,2,128]{2,1,0:T(2,128)}), f32[128,2,128]{2,1,0:T(2,128)S(1)}, u32[]{:S(2)}, u32[]{:S(2)}) async-start(f32[128,2,128]{2,1,0:T(2,128)} %broadcast_in_dim.45), calls=%async_computation.2 | async-start | bytes 262144 | tf_op jit(solution)/shard_map/all_to_all | solution.py:887
  123.6 8.4 %shard_map.151 = (f32[64,256]{1,0:T(8,128)}, f32[256,4096]{1,0:T(8,128)}, f32[256,1024]{1,0:T(8,128)}) custom-call(s32[1]{0:T(128)} %bitcast.odd_ref, f32[2048,128]{1,0:T(8,128)S(1)} %get-tuple-element.61.own_ref, f32[1024,128]{1,0:T(8,128)S(1)} %collective-permute-done.2.second_ref, f32[1024,128]{1,0:T(8,128)S(1)} %collective-permute-done.3.first_ref, ...), custom_call_target="tpu_custom_call" | custom-call | flops 1879048192 | bytes 20807684 | tf_op jit(solution)/shard_map/pallas_call | solution.py:587
  132.0 2.9 %all-to-all-done.2 = f32[128,2,128]{2,1,0:T(2,128)S(1)} async-done(((f32[128,2,128]{2,1,0:T(2,128)}), f32[128,2,128]{2,1,0:T(2,128)S(1)}, u32[]{:S(2)}, u32[]{:S(2)}) %all-to-all-start.2) | async-done | bytes 131104 | tf_op jit(solution)/shard_map/all_to_all | solution.py:887
  134.9 0.1 reduce_sum.9
  135.0 0.6 slice_bitcast_fusion
  (4 shorter events, 0.0 us)
Async XLA Ops:
  3.8 20.8 %collective-permute-start = (f32[1040,128]{1,0:T(8,128)S(1)}, f32[1040,128]{1,0:T(8,128)S(1)}, u32[]{:S(2)}, u32[]{:S(2)}) collective-permute-start(f32[1040,128]{1,0:T(8,128)S(1)} %get-tuple-element.45), channel_id=1, source_target_pairs={{0,15},{1,2},{2,1},{3,4},{4,3},{5,6},{6,5},{7,8},{8,7},{9,10},{10,... | collective-permute-start | bytes 1597448 | tf_op jit(solution)/shard_map/ppermute | solution.py:852
  12.7 12.6 %collective-permute-start.1 = (f32[1040,128]{1,0:T(8,128)S(1)}, f32[1040,128]{1,0:T(8,128)S(1)}, u32[]{:S(2)}, u32[]{:S(2)}) collective-permute-start(f32[1040,128]{1,0:T(8,128)S(1)} %get-tuple-element.46), channel_id=1, source_target_pairs={{0,1},{1,0},{2,3},{3,2},{4,5},{5,4},{6,7},{7,6},{8,9},{9,8},{10,11... | collective-permute-start | bytes 1597448 | tf_op jit(solution)/shard_map/ppermute | solution.py:853
  27.5 27.5 %all-to-all-start = ((f32[8,264,128]{2,1,0:T(8,128)}), f32[8,264,128]{2,1,0:T(8,128)S(1)}, u32[]{:S(2)}, u32[]{:S(2)}) async-start(f32[8,264,128]{2,1,0:T(8,128)} %get-tuple-element.48), calls=%async_computation | async-start | bytes 2162688 | tf_op jit(solution)/shard_map/all_to_all | solution.py:860
  56.1 23.8 %all-to-all-start.1 = ((f32[8,256,128]{2,1,0:T(8,128)}), f32[8,256,128]{2,1,0:T(8,128)S(1)}, u32[]{:S(2)}, u32[]{:S(2)}) async-start(f32[8,256,128]{2,1,0:T(8,128)} %shard_map.148.after_ref), calls=%async_computation.1 | async-start | bytes 2097152 | tf_op jit(solution)/shard_map/all_to_all | solution.py:875
  81.3 25.3 %collective-permute-start.2 = (f32[1024,128]{1,0:T(8,128)S(1)}, f32[1024,128]{1,0:T(8,128)S(1)}, u32[]{:S(2)}, u32[]{:S(2)}) collective-permute-start(f32[1024,128]{1,0:T(8,128)S(1)} %get-tuple-element.62), channel_id=1, source_target_pairs={{0,15},{1,2},{2,1},{3,4},{4,3},{5,6},{6,5},{7,8},{8,7},{9,10},{10,... | collective-permute-start | bytes 1572872 | tf_op jit(solution)/shard_map/ppermute | solution.py:877
  95.6 13.3 %collective-permute-start.3 = (f32[1024,128]{1,0:T(8,128)S(1)}, f32[1024,128]{1,0:T(8,128)S(1)}, u32[]{:S(2)}, u32[]{:S(2)}) collective-permute-start(f32[1024,128]{1,0:T(8,128)S(1)} %get-tuple-element.63), channel_id=1, source_target_pairs={{0,1},{1,0},{2,3},{3,2},{4,5},{5,4},{6,7},{7,6},{8,9},{9,8},{10,11... | collective-permute-start | bytes 1572872 | tf_op jit(solution)/shard_map/ppermute | solution.py:878
  110.9 2.9 %collective-permute-start.4 = (f32[2,128]{1,0:T(2,128)S(1)}, f32[2,128]{1,0:T(2,128)S(1)}, u32[]{:S(2)}, u32[]{:S(2)}) collective-permute-start(f32[2,128]{1,0:T(2,128)S(1)} %slice.12), channel_id=1, source_target_pairs={{0,16},{16,0},{32,48},{48,32},{64,80},{80,64},{96,112},{112,96},{1... | collective-permute-start | bytes 3080 | tf_op jit(solution)/shard_map/ppermute | solution.py:883
  114.5 20.4 %all-to-all-start.2 = ((f32[128,2,128]{2,1,0:T(2,128)}), f32[128,2,128]{2,1,0:T(2,128)S(1)}, u32[]{:S(2)}, u32[]{:S(2)}) async-start(f32[128,2,128]{2,1,0:T(2,128)} %broadcast_in_dim.45), calls=%async_computation.2 | async-start | bytes 262144 | tf_op jit(solution)/shard_map/all_to_all | solution.py:887

commit v7 on v6

--- a/solution.py
+++ b/solution.py
@@ -178,25 +178,14 @@
 
 
 def combine_kernel(
-    flags_ref,
-    own_ref,
-    own_total_ref,
-    second_ref,
-    first_ref,
-    after_ref,
-    sent_ref,
-    other_total_ref,
-    other_ref,
-    other,
-    gone,
+    flags_ref, own_ref, own_total_ref, second_ref, first_ref, after_ref, sent_ref, token_ref
 ):
+    token_ref[...] = jnp.zeros_like(token_ref)
     halves = flag_rows(flags_ref)
     per_half = 2 * PER
     each = sent_ref.shape[0]
     got = per_half // each
     totals = [[] for _ in range(each)]
-    other_totals = []
-    leaving = []
     for half, ref in enumerate((first_ref, second_ref)):
         earlier, keep = halves[half]
         for h in range(per_half):
@@ -210,19 +199,40 @@
             at, q = h // got, half * got + h % got
             sent_ref[at, q * D : (q + 1) * D, :] = by_own * state + by_met * met
             totals[at].append(total * met_total)
-            other[mine * D : (mine + 1) * D, :] = jnp.where(earlier > 0, met, state)
-            other_totals.append(jnp.where(earlier > 0, met_total, total))
-            if h % PER == PER - 1:
-                part = wide(mine // PER)
-                copy = pltpu.make_async_copy(
-                    other.at[part], other_ref.at[part], gone.at[mine // PER]
-                )
-                copy.start()
-                leaving.append(copy)
     rows = 2 * got
     for at in range(each):
         pad = [jnp.zeros((8 - rows, N), F32)]
         sent_ref[at, rows * D :, :] = jnp.concatenate(totals[at] + pad, axis=0)
+
+
+def later_kernel(
+    flags_ref,
+    own_ref,
+    own_total_ref,
+    second_ref,
+    first_ref,
+    token_ref,
+    other_total_ref,
+    other_ref,
+    other,
+    gone,
+):
+    halves = flag_rows(flags_ref)
+    per_half = 2 * PER
+    other_totals = []
+    leaving = []
+    for half, ref in enumerate((first_ref, second_ref)):
+        earlier, _ = halves[half]
+        for k in range(2):
+            part = wide(2 * half + k)
+            other[part, :] = jnp.where(earlier > 0, ref[wide(k), :], own_ref[part, :])
+            leaving.append(
+                pltpu.make_async_copy(other.at[part], other_ref.at[part], gone.at[2 * half + k])
+            )
+            leaving[-1].start()
+        mine = slice(half * per_half, (half + 1) * per_half)
+        met_totals = ref[per_half * D : per_half * D + per_half, :]
+        other_totals.append(jnp.where(earlier > 0, met_totals, own_total_ref[mine, :]))
     other_total_ref[...] = jnp.concatenate(other_totals, axis=0)
     for copy in leaving:
         copy.wait()
@@ -668,12 +678,23 @@
         [HERE] * 5 + [ELSEWHERE],
         [
             (HERE, f32_near(pairs, H * D // 2 // pairs + 8, N)),
-            (HERE, f32_near(H // 2, N)),
-            (ELSEWHERE, f32(H * D // 2, N)),
+            (HERE, f32_near(8, N)),
         ],
         near(flags, own, own_total, second, first) + far(after),
         4 * H * D * N,
-        16,
+        12,
+    )
+
+
+def later_states(flags, own, own_total, first, second, token):
+    return call(
+        later_kernel,
+        0,
+        [HERE] * 6,
+        [(HERE, f32_near(H // 2, N)), (ELSEWHERE, f32(H * D // 2, N))],
+        near(flags, own, own_total, second, first, token),
+        H * D * N,
+        12,
         [pltpu.VMEM((H * D // 2, N), F32), COPIES((4,))],
     )
 
@@ -854,11 +875,10 @@
     by_decay, by_bias, sig_high, sig_low, sig_turned = prepared_part(
         sig, in_map, raw, decay_row, bias_row, start, own_total
     )
-    sent, other_total, other = combine_states(
-        flags, own, own_total, first, second, sig_turned, blocks // 2
-    )
+    sent, token = combine_states(flags, own, own_total, first, second, sig_turned, blocks // 2)
     states = lax.all_to_all(sent, "ctx", 0, 0, axis_index_groups=alike)
     operands = (sig, cot, in_map, out_map, raw, decay_row, bias_row, skip_row, start)
+    other_total, other = later_states(flags, own, own_total, first, second, token)
     *begun, token = inner_part(range(INNER_FIRST), *operands, other)
     ends = scan_states(odd, states, token)
     (

time: 136 us -> 136 us (level)
    pallas_call x10 -> x11, Pallas kernels: 61.6 us -> 60.7 us  [call(): pl.pallas_call(kernel, grid=(grid,) if grid else (), in_specs=ins, out_sp...]
  transfers between devices with their start and end apart: 8 -> 8, of which waited for: 8 -> 8; matrix products, arithmetic and copies ran while one was open for 0% -> 0% of each run, Pallas kernels for 38% -> 39%
where the time goes in v7:
time: 136 us; the launch traced here: 135 us
  Pallas kernels  60.7 us (45%)
  starting transfers between devices  46.4 us (34%)
  waiting for transfers between devices  24.5 us (18%)
  local copies, waits for them, and re-layouts  2.37 us (2%)
    pallas_call x11, Pallas kernels, call(): pl.pallas_call(kernel, grid=(grid,) if grid else (), in_specs=ins, out_sp...  60.7 us
    ppermute x2, starting transfers between devices, local(): second = lax.ppermute(second, 'ctx', across)  23.3 us
    all_to_all x1, starting transfers between devices, local(): lax.all_to_all(sent, ('dp', 'ctx'), 0, 0, axis_index_groups=equal)  9.09 us
    ppermute x2, waiting for transfers between devices, local(): second = lax.ppermute(second, 'ctx', across)  7.64 us
    all_to_all x1, waiting for transfers between devices, local(): states = lax.all_to_all(sent, 'ctx', 0, 0, axis_index_groups=alike)  6.76 us
    all_to_all x1, starting transfers between devices, local(): ends = lax.all_to_all(ends, 'ctx', 0, 0, axis_index_groups=alike)  5.33 us
    all_to_all x1, starting transfers between devices, local(): states = lax.all_to_all(sent, 'ctx', 0, 0, axis_index_groups=alike)  4.14 us
    ppermute x2, waiting for transfers between devices, local(): first = lax.ppermute(first, 'ctx', inward)  3.22 us
  transfers between devices with their start and end apart: 8, of which 8 were waited for; matrix products, arithmetic and copies ran while one was open for 0% of the time, Pallas kernels for 39%

profile of v7, /device:TPU:1, one launch (start us, length us, event | category | flops | bytes accessed | tf_op | source)
XLA Modules:
  0.0 135.0 jit_solution(944763715610341246)
XLA Ops:
  0.6 3.1 %shard_map.144 = (f32[2048,128]{1,0:T(8,128)S(1)}, f32[32,128]{1,0:T(8,128)S(1)}, f32[1040,128]{1,0:T(8,128)S(1)}, f32[1040,128]{1,0:T(8,128)S(1)}) custom-call(s32[1]{0:T(128)} %bitcast.odd_ref, bf16[256,4096]{1,0:T(8,128)(2,1)} %bitcast.22, bf16[256,1024]{1,0:T(8,128)(2,1)} %bitcast.33, f32[64,256]{1,0:T(8,128)} %bitcast.36, f32[1,64]{1,0:T(1,128)} %bitcast.40, ...), custom_call_target="tpu_custom_call" | custom-call | flops 536870912 | bytes 4817412 | tf_op jit(solution)/shard_map/pallas_call | solution.py:597
  3.8 8.9 %collective-permute-start = (f32[1040,128]{1,0:T(8,128)S(1)}, f32[1040,128]{1,0:T(8,128)S(1)}, u32[]{:S(2)}, u32[]{:S(2)}) collective-permute-start(f32[1040,128]{1,0:T(8,128)S(1)} %get-tuple-element.46), channel_id=1, source_target_pairs={{0,15},{1,2},{2,1},{3,4},{4,3},{5,6},{6,5},{7,8},{8,7},{9,10},{10,... | collective-permute-start | bytes 1597448 | tf_op jit(solution)/shard_map/ppermute | solution.py:873
  12.7 0.0 collective-permute-start.1
  12.7 0.1 add_convert_fusion
  12.8 10.8 %shard_map.145 = (f32[4096,128]{1,0:T(8,128)}, f32[4096,128]{1,0:T(8,128)}, bf16[256,4096]{1,0:T(8,128)(2,1)}, bf16[256,4096]{1,0:T(8,128)(2,1)}, bf16[4096,256]{1,0:T(8,128)(2,1)}) custom-call(bf16[256,4096]{1,0:T(8,128)(2,1)} %bitcast.49, bf16[256,1024]{1,0:T(8,128)(2,1)} %bitcast.29, f32[64,256]{1,0:T(8,128)} %bitcast.37, f32[1,64]{1,0:T(1,128)} %bitcast.41, ...), custom_call_target="tpu_custom_call" | custom-call | flops 2684354560 | bytes 14238208 | tf_op jit(solution)/shard_map/pallas_call | solution.py:597
  23.6 1.0 collective-permute-done.second_ref
  24.6 0.8 collective-permute-done.1.first_ref
  25.4 0.1 broadcast_in_dim.37.flags_ref
  25.4 0.2 shard_map.146
  25.6 0.0 copy-start
  25.6 1.0 copy-done
  26.7 4.1 %all-to-all-start = ((f32[8,264,128]{2,1,0:T(8,128)}), f32[8,264,128]{2,1,0:T(8,128)S(1)}, u32[]{:S(2)}, u32[]{:S(2)}) async-start(f32[8,264,128]{2,1,0:T(8,128)} %copy-done), calls=%async_computation | async-start | bytes 2162688 | tf_op jit(solution)/shard_map/all_to_all | solution.py:879
  30.8 1.0 shard_map.147
  31.8 15.5 %shard_map.148 = (f32[256,4096]{1,0:T(8,128)}, f32[256,1024]{1,0:T(8,128)}, f32[256,1024]{1,0:T(8,128)}, f32[64,256]{1,0:T(8,128)S(1)}, f32[64,128]{1,0:T(8,128)...) custom-call(bf16[256,4096]{1,0:T(8,128)(2,1)} %bitcast.50, ...), custom_call_target="tpu_custom_call" | custom-call | flops 4026531840 | bytes 13996800 | tf_op jit(solution)/shard_map/pallas_call | solution.py:597
  47.4 6.8 %all-to-all-done.state_ref = f32[8,264,128]{2,1,0:T(8,128)S(1)} async-done(((f32[8,264,128]{2,1,0:T(8,128)}), f32[8,264,128]{2,1,0:T(8,128)S(1)}, u32[]{:S(2)}, u32[]{:S(2)}) %all-to-all-start) | async-done | bytes 1081376 | tf_op jit(solution)/shard_map/all_to_all | solution.py:879
  54.2 1.1 shard_map.149.after_ref
  55.3 5.3 %all-to-all-start.1 = ((f32[8,256,128]{2,1,0:T(8,128)}), f32[8,256,128]{2,1,0:T(8,128)S(1)}, u32[]{:S(2)}, u32[]{:S(2)}) async-start(f32[8,256,128]{2,1,0:T(8,128)} %shard_map.149.after_ref), calls=%async_computation.1 | async-start | bytes 2097152 | tf_op jit(solution)/shard_map/all_to_all | solution.py:895
  60.6 15.5 %shard_map.150 = (f32[256,4096]{1,0:T(8,128)}, f32[256,1024]{1,0:T(8,128)}, f32[256,1024]{1,0:T(8,128)}, f32[64,256]{1,0:T(8,128)S(1)}, f32[64,128]{1,0:T(8,128)...) custom-call(bf16[256,4096]{1,0:T(8,128)(2,1)} %bitcast.51, ...), custom_call_target="tpu_custom_call", output_to_operand_aliasing={{0}: (10, {}), {1}: (11, {}), {2}: (12, {}), {3}: (13, {}),... | custom-call | flops 4026531840 | bytes 20583168 | tf_op jit(solution)/shard_map/pallas_call | solution.py:597
  76.1 3.0 %all-to-all-done.1.end_ref = f32[8,256,128]{2,1,0:T(8,128)S(1)} async-done(((f32[8,256,128]{2,1,0:T(8,128)}), f32[8,256,128]{2,1,0:T(8,128)S(1)}, u32[]{:S(2)}, u32[]{:S(2)}) %all-to-all-start.1) | async-done | bytes 1048608 | tf_op jit(solution)/shard_map/all_to_all | solution.py:895
  79.1 1.3 shard_map.151
  80.4 14.3 %collective-permute-start.2 = (f32[1024,128]{1,0:T(8,128)S(1)}, f32[1024,128]{1,0:T(8,128)S(1)}, u32[]{:S(2)}, u32[]{:S(2)}) collective-permute-start(f32[1024,128]{1,0:T(8,128)S(1)} %get-tuple-element.64), channel_id=1, source_target_pairs={{0,15},{1,2},{2,1},{3,4},{4,3},{5,6},{6,5},{7,8},{8,7},{9,10},{10,... | collective-permute-start | bytes 1572872 | tf_op jit(solution)/shard_map/ppermute | solution.py:897
  94.7 2.5 %collective-permute-start.3 = (f32[1024,128]{1,0:T(8,128)S(1)}, f32[1024,128]{1,0:T(8,128)S(1)}, u32[]{:S(2)}, u32[]{:S(2)}) collective-permute-start(f32[1024,128]{1,0:T(8,128)S(1)} %get-tuple-element.65), channel_id=1, source_target_pairs={{0,1},{1,0},{2,3},{3,2},{4,5},{5,4},{6,7},{7,6},{8,9},{9,8},{10,11... | collective-permute-start | bytes 1572872 | tf_op jit(solution)/shard_map/ppermute | solution.py:898
  97.2 1.8 %shard_map.153.kept_ref = f32[128,128]{1,0:T(8,128)S(1)} custom-call(s32[1]{0:T(128)} %bitcast.odd_ref, f32[2048,128]{1,0:T(8,128)S(1)} %get-tuple-element.63.own_ref, f32[64,128]{1,0:T(8,128)S(1)} %get-tuple-element.66.refs_0_.sums_ref, f32[4096,128]{1,0:T(8,128)} %get-tuple-element.79.by_decay_ref, f32[4096,128]{1,0:T(8,128)} %get-tuple-element.80.by_bias_ref), custom_call_target="tpu_custom_call" | custom-call | flops 1048576 | bytes 5341188 | tf_op jit(solution)/shard_map/pallas_call | solution.py:597
  99.0 6.7 %collective-permute-done.2.second_ref = f32[1024,128]{1,0:T(8,128)S(1)} collective-permute-done((f32[1024,128]{1,0:T(8,128)S(1)}, f32[1024,128]{1,0:T(8,128)S(1)}, u32[]{:S(2)}, u32[]{:S(2)}) %collective-permute-start.2) | collective-permute-done | bytes 524320 | tf_op jit(solution)/shard_map/ppermute | solution.py:897
  105.6 2.4 %collective-permute-done.3.first_ref = f32[1024,128]{1,0:T(8,128)S(1)} collective-permute-done((f32[1024,128]{1,0:T(8,128)S(1)}, f32[1024,128]{1,0:T(8,128)S(1)}, u32[]{:S(2)}, u32[]{:S(2)}) %collective-permute-start.3) | collective-permute-done | bytes 524320 | tf_op jit(solution)/shard_map/ppermute | solution.py:898
  108.0 1.9 %shard_map.154 = f32[8,128]{1,0:T(8,128)S(1)} custom-call(s32[1]{0:T(128)} %bitcast.odd_ref, f32[1024,128]{1,0:T(8,128)S(1)} %collective-permute-done.2.second_ref, f32[1024,128]{1,0:T(8,128)S(1)} %collective-permute-done.3.first_ref, f32[128,128]{1,0:T(8,128)S(1)} %shard_map.153.kept_ref, f32[64,128]{1,0:T(8,128)S(1)} %get-tuple-element.66.refs_0_.sums_ref, ...), custom_call_target="tpu_custom_call" | custom-call | flops 1048576 | bytes 5345284 | tf_op jit(solution)/shard_map/pallas_call | solution.py:597
  110.0 2.1 %collective-permute-start.4 = (f32[2,128]{1,0:T(2,128)S(1)}, f32[2,128]{1,0:T(2,128)S(1)}, u32[]{:S(2)}, u32[]{:S(2)}) collective-permute-start(f32[2,128]{1,0:T(2,128)S(1)} %slice.12), channel_id=1, source_target_pairs={{0,16},{16,0},{32,48},{48,32},{64,80},{80,64},{96,112},{112,96},{1... | collective-permute-start | bytes 3080 | tf_op jit(solution)/shard_map/ppermute | solution.py:903
  112.1 0.8 collective-permute-done.4
  112.9 0.7 broadcast_in_dim.45
  113.6 9.1 %all-to-all-start.2 = ((f32[128,2,128]{2,1,0:T(2,128)}), f32[128,2,128]{2,1,0:T(2,128)S(1)}, u32[]{:S(2)}, u32[]{:S(2)}) async-start(f32[128,2,128]{2,1,0:T(2,128)} %broadcast_in_dim.45), calls=%async_computation.2 | async-start | bytes 262144 | tf_op jit(solution)/shard_map/all_to_all | solution.py:907
  122.7 8.4 %shard_map.152 = (f32[64,256]{1,0:T(8,128)}, f32[256,4096]{1,0:T(8,128)}, f32[256,1024]{1,0:T(8,128)}) custom-call(s32[1]{0:T(128)} %bitcast.odd_ref, f32[2048,128]{1,0:T(8,128)S(1)} %get-tuple-element.63.own_ref, f32[1024,128]{1,0:T(8,128)S(1)} %collective-permute-done.2.second_ref, f32[1024,128]{1,0:T(8,128)S(1)} %collective-permute-done.3.first_ref, ...), custom_call_target="tpu_custom_call" | custom-call | flops 1879048192 | bytes 20807684 | tf_op jit(solution)/shard_map/pallas_call | solution.py:597
  131.2 3.1 %all-to-all-done.2 = f32[128,2,128]{2,1,0:T(2,128)S(1)} async-done(((f32[128,2,128]{2,1,0:T(2,128)}), f32[128,2,128]{2,1,0:T(2,128)S(1)}, u32[]{:S(2)}, u32[]{:S(2)}) %all-to-all-start.2) | async-done | bytes 131104 | tf_op jit(solution)/shard_map/all_to_all | solution.py:907
  134.3 0.1 reduce_sum.9
  134.4 0.6 slice_bitcast_fusion
  (4 shorter events, 0.0 us)
Async XLA Ops:
  3.8 20.8 %collective-permute-start = (f32[1040,128]{1,0:T(8,128)S(1)}, f32[1040,128]{1,0:T(8,128)S(1)}, u32[]{:S(2)}, u32[]{:S(2)}) collective-permute-start(f32[1040,128]{1,0:T(8,128)S(1)} %get-tuple-element.46), channel_id=1, source_target_pairs={{0,15},{1,2},{2,1},{3,4},{4,3},{5,6},{6,5},{7,8},{8,7},{9,10},{10,... | collective-permute-start | bytes 1597448 | tf_op jit(solution)/shard_map/ppermute | solution.py:873
  12.7 12.6 %collective-permute-start.1 = (f32[1040,128]{1,0:T(8,128)S(1)}, f32[1040,128]{1,0:T(8,128)S(1)}, u32[]{:S(2)}, u32[]{:S(2)}) collective-permute-start(f32[1040,128]{1,0:T(8,128)S(1)} %get-tuple-element.47), channel_id=1, source_target_pairs={{0,1},{1,0},{2,3},{3,2},{4,5},{5,4},{6,7},{7,6},{8,9},{9,8},{10,11... | collective-permute-start | bytes 1597448 | tf_op jit(solution)/shard_map/ppermute | solution.py:874
  25.6 1.0 copy-start
  26.7 27.5 %all-to-all-start = ((f32[8,264,128]{2,1,0:T(8,128)}), f32[8,264,128]{2,1,0:T(8,128)S(1)}, u32[]{:S(2)}, u32[]{:S(2)}) async-start(f32[8,264,128]{2,1,0:T(8,128)} %copy-done), calls=%async_computation | async-start | bytes 2162688 | tf_op jit(solution)/shard_map/all_to_all | solution.py:879
  55.3 23.8 %all-to-all-start.1 = ((f32[8,256,128]{2,1,0:T(8,128)}), f32[8,256,128]{2,1,0:T(8,128)S(1)}, u32[]{:S(2)}, u32[]{:S(2)}) async-start(f32[8,256,128]{2,1,0:T(8,128)} %shard_map.149.after_ref), calls=%async_computation.1 | async-start | bytes 2097152 | tf_op jit(solution)/shard_map/all_to_all | solution.py:895
  80.4 25.3 %collective-permute-start.2 = (f32[1024,128]{1,0:T(8,128)S(1)}, f32[1024,128]{1,0:T(8,128)S(1)}, u32[]{:S(2)}, u32[]{:S(2)}) collective-permute-start(f32[1024,128]{1,0:T(8,128)S(1)} %get-tuple-element.64), channel_id=1, source_target_pairs={{0,15},{1,2},{2,1},{3,4},{4,3},{5,6},{6,5},{7,8},{8,7},{9,10},{10,... | collective-permute-start | bytes 1572872 | tf_op jit(solution)/shard_map/ppermute | solution.py:897
  94.7 13.3 %collective-permute-start.3 = (f32[1024,128]{1,0:T(8,128)S(1)}, f32[1024,128]{1,0:T(8,128)S(1)}, u32[]{:S(2)}, u32[]{:S(2)}) collective-permute-start(f32[1024,128]{1,0:T(8,128)S(1)} %get-tuple-element.65), channel_id=1, source_target_pairs={{0,1},{1,0},{2,3},{3,2},{4,5},{5,4},{6,7},{7,6},{8,9},{9,8},{10,11... | collective-permute-start | bytes 1572872 | tf_op jit(solution)/shard_map/ppermute | solution.py:898
  110.0 2.9 %collective-permute-start.4 = (f32[2,128]{1,0:T(2,128)S(1)}, f32[2,128]{1,0:T(2,128)S(1)}, u32[]{:S(2)}, u32[]{:S(2)}) collective-permute-start(f32[2,128]{1,0:T(2,128)S(1)} %slice.12), channel_id=1, source_target_pairs={{0,16},{16,0},{32,48},{48,32},{64,80},{80,64},{96,112},{112,96},{1... | collective-permute-start | bytes 3080 | tf_op jit(solution)/shard_map/ppermute | solution.py:903
  113.6 20.6 %all-to-all-start.2 = ((f32[128,2,128]{2,1,0:T(2,128)}), f32[128,2,128]{2,1,0:T(2,128)S(1)}, u32[]{:S(2)}, u32[]{:S(2)}) async-start(f32[128,2,128]{2,1,0:T(2,128)} %broadcast_in_dim.45), calls=%async_computation.2 | async-start | bytes 262144 | tf_op jit(solution)/shard_map/all_to_all | solution.py:907

commit v8 on v7

--- a/solution.py
+++ b/solution.py
@@ -23,7 +23,7 @@
 MET = (4, 5, 6, 7)
 INNER_FIRST = 4
 SUMS_BATCH = 2
-FINISH_BATCH = 2
+FINISH_BATCH = 3
 
 
 def split(x, parts):

time: 136 us -> 136 us (level)
  no operation moved by 1% of the time
where the time goes in v8:
time: 136 us; the launch traced here: 135 us
  Pallas kernels  60.4 us (44%)
  starting transfers between devices  46.4 us (34%)
  waiting for transfers between devices  24.8 us (18%)
  local copies, waits for them, and re-layouts  2.37 us (2%)
    pallas_call x11, Pallas kernels, call(): pl.pallas_call(kernel, grid=(grid,) if grid else (), in_specs=ins, out_sp...  60.4 us
    ppermute x2, starting transfers between devices, local(): second = lax.ppermute(second, 'ctx', across)  23.3 us
    all_to_all x1, starting transfers between devices, local(): lax.all_to_all(sent, ('dp', 'ctx'), 0, 0, axis_index_groups=equal)  9.09 us
    ppermute x2, waiting for transfers between devices, local(): second = lax.ppermute(second, 'ctx', across)  7.64 us
    all_to_all x1, waiting for transfers between devices, local(): states = lax.all_to_all(sent, 'ctx', 0, 0, axis_index_groups=alike)  6.76 us
    all_to_all x1, starting transfers between devices, local(): ends = lax.all_to_all(ends, 'ctx', 0, 0, axis_index_groups=alike)  5.33 us
    all_to_all x1, starting transfers between devices, local(): states = lax.all_to_all(sent, 'ctx', 0, 0, axis_index_groups=alike)  4.14 us
    all_to_all x1, waiting for transfers between devices, local(): lax.all_to_all(sent, ('dp', 'ctx'), 0, 0, axis_index_groups=equal)  3.43 us
  transfers between devices with their start and end apart: 8, of which 8 were waited for; matrix products, arithmetic and copies ran while one was open for 0% of the time, Pallas kernels for 39%

profile of v8, /device:TPU:1, one launch (start us, length us, event | category | flops | bytes accessed | tf_op | source)
XLA Modules:
  0.0 135.0 jit_solution(6920098320689008803)
XLA Ops:
  0.6 3.1 %shard_map.144 = (f32[2048,128]{1,0:T(8,128)S(1)}, f32[32,128]{1,0:T(8,128)S(1)}, f32[1040,128]{1,0:T(8,128)S(1)}, f32[1040,128]{1,0:T(8,128)S(1)}) custom-call(s32[1]{0:T(128)} %bitcast.odd_ref, bf16[256,4096]{1,0:T(8,128)(2,1)} %bitcast.22, bf16[256,1024]{1,0:T(8,128)(2,1)} %bitcast.33, f32[64,256]{1,0:T(8,128)} %bitcast.36, f32[1,64]{1,0:T(1,128)} %bitcast.40, ...), custom_call_target="tpu_custom_call" | custom-call | flops 536870912 | bytes 4817412 | tf_op jit(solution)/shard_map/pallas_call | solution.py:597
  3.8 8.9 %collective-permute-start = (f32[1040,128]{1,0:T(8,128)S(1)}, f32[1040,128]{1,0:T(8,128)S(1)}, u32[]{:S(2)}, u32[]{:S(2)}) collective-permute-start(f32[1040,128]{1,0:T(8,128)S(1)} %get-tuple-element.46), channel_id=1, source_target_pairs={{0,15},{1,2},{2,1},{3,4},{4,3},{5,6},{6,5},{7,8},{8,7},{9,10},{10,... | collective-permute-start | bytes 1597448 | tf_op jit(solution)/shard_map/ppermute | solution.py:873
  12.7 0.0 collective-permute-start.1
  12.7 0.1 add_convert_fusion
  12.8 10.8 %shard_map.145 = (f32[4096,128]{1,0:T(8,128)}, f32[4096,128]{1,0:T(8,128)}, bf16[256,4096]{1,0:T(8,128)(2,1)}, bf16[256,4096]{1,0:T(8,128)(2,1)}, bf16[4096,256]{1,0:T(8,128)(2,1)}) custom-call(bf16[256,4096]{1,0:T(8,128)(2,1)} %bitcast.49, bf16[256,1024]{1,0:T(8,128)(2,1)} %bitcast.29, f32[64,256]{1,0:T(8,128)} %bitcast.37, f32[1,64]{1,0:T(1,128)} %bitcast.41, ...), custom_call_target="tpu_custom_call" | custom-call | flops 2684354560 | bytes 14238208 | tf_op jit(solution)/shard_map/pallas_call | solution.py:597
  23.6 1.0 collective-permute-done.second_ref
  24.6 0.8 collective-permute-done.1.first_ref
  25.4 0.1 broadcast_in_dim.37.flags_ref
  25.4 0.2 shard_map.146
  25.6 0.0 copy-start
  25.6 1.0 copy-done
  26.7 4.1 %all-to-all-start = ((f32[8,264,128]{2,1,0:T(8,128)}), f32[8,264,128]{2,1,0:T(8,128)S(1)}, u32[]{:S(2)}, u32[]{:S(2)}) async-start(f32[8,264,128]{2,1,0:T(8,128)} %copy-done), calls=%async_computation | async-start | bytes 2162688 | tf_op jit(solution)/shard_map/all_to_all | solution.py:879
  30.8 1.0 shard_map.147
  31.8 15.5 %shard_map.148 = (f32[256,4096]{1,0:T(8,128)}, f32[256,1024]{1,0:T(8,128)}, f32[256,1024]{1,0:T(8,128)}, f32[64,256]{1,0:T(8,128)S(1)}, f32[64,128]{1,0:T(8,128)...) custom-call(bf16[256,4096]{1,0:T(8,128)(2,1)} %bitcast.50, ...), custom_call_target="tpu_custom_call" | custom-call | flops 4026531840 | bytes 13996800 | tf_op jit(solution)/shard_map/pallas_call | solution.py:597
  47.4 6.8 %all-to-all-done.state_ref = f32[8,264,128]{2,1,0:T(8,128)S(1)} async-done(((f32[8,264,128]{2,1,0:T(8,128)}), f32[8,264,128]{2,1,0:T(8,128)S(1)}, u32[]{:S(2)}, u32[]{:S(2)}) %all-to-all-start) | async-done | bytes 1081376 | tf_op jit(solution)/shard_map/all_to_all | solution.py:879
  54.2 1.1 shard_map.149.after_ref
  55.3 5.3 %all-to-all-start.1 = ((f32[8,256,128]{2,1,0:T(8,128)}), f32[8,256,128]{2,1,0:T(8,128)S(1)}, u32[]{:S(2)}, u32[]{:S(2)}) async-start(f32[8,256,128]{2,1,0:T(8,128)} %shard_map.149.after_ref), calls=%async_computation.1 | async-start | bytes 2097152 | tf_op jit(solution)/shard_map/all_to_all | solution.py:895
  60.6 15.5 %shard_map.150 = (f32[256,4096]{1,0:T(8,128)}, f32[256,1024]{1,0:T(8,128)}, f32[256,1024]{1,0:T(8,128)}, f32[64,256]{1,0:T(8,128)S(1)}, f32[64,128]{1,0:T(8,128)...) custom-call(bf16[256,4096]{1,0:T(8,128)(2,1)} %bitcast.51, ...), custom_call_target="tpu_custom_call", output_to_operand_aliasing={{0}: (10, {}), {1}: (11, {}), {2}: (12, {}), {3}: (13, {}),... | custom-call | flops 4026531840 | bytes 20583168 | tf_op jit(solution)/shard_map/pallas_call | solution.py:597
  76.1 3.0 %all-to-all-done.1.end_ref = f32[8,256,128]{2,1,0:T(8,128)S(1)} async-done(((f32[8,256,128]{2,1,0:T(8,128)}), f32[8,256,128]{2,1,0:T(8,128)S(1)}, u32[]{:S(2)}, u32[]{:S(2)}) %all-to-all-start.1) | async-done | bytes 1048608 | tf_op jit(solution)/shard_map/all_to_all | solution.py:895
  79.1 1.3 shard_map.151
  80.4 14.3 %collective-permute-start.2 = (f32[1024,128]{1,0:T(8,128)S(1)}, f32[1024,128]{1,0:T(8,128)S(1)}, u32[]{:S(2)}, u32[]{:S(2)}) collective-permute-start(f32[1024,128]{1,0:T(8,128)S(1)} %get-tuple-element.64), channel_id=1, source_target_pairs={{0,15},{1,2},{2,1},{3,4},{4,3},{5,6},{6,5},{7,8},{8,7},{9,10},{10,... | collective-permute-start | bytes 1572872 | tf_op jit(solution)/shard_map/ppermute | solution.py:897
  94.7 2.5 %collective-permute-start.3 = (f32[1024,128]{1,0:T(8,128)S(1)}, f32[1024,128]{1,0:T(8,128)S(1)}, u32[]{:S(2)}, u32[]{:S(2)}) collective-permute-start(f32[1024,128]{1,0:T(8,128)S(1)} %get-tuple-element.65), channel_id=1, source_target_pairs={{0,1},{1,0},{2,3},{3,2},{4,5},{5,4},{6,7},{7,6},{8,9},{9,8},{10,11... | collective-permute-start | bytes 1572872 | tf_op jit(solution)/shard_map/ppermute | solution.py:898
  97.2 1.8 %shard_map.153.kept_ref = f32[128,128]{1,0:T(8,128)S(1)} custom-call(s32[1]{0:T(128)} %bitcast.odd_ref, f32[2048,128]{1,0:T(8,128)S(1)} %get-tuple-element.63.own_ref, f32[64,128]{1,0:T(8,128)S(1)} %get-tuple-element.66.refs_0_.sums_ref, f32[4096,128]{1,0:T(8,128)} %get-tuple-element.79.by_decay_ref, f32[4096,128]{1,0:T(8,128)} %get-tuple-element.80.by_bias_ref), custom_call_target="tpu_custom_call" | custom-call | flops 1048576 | bytes 5341188 | tf_op jit(solution)/shard_map/pallas_call | solution.py:597
  99.0 6.7 %collective-permute-done.2.second_ref = f32[1024,128]{1,0:T(8,128)S(1)} collective-permute-done((f32[1024,128]{1,0:T(8,128)S(1)}, f32[1024,128]{1,0:T(8,128)S(1)}, u32[]{:S(2)}, u32[]{:S(2)}) %collective-permute-start.2) | collective-permute-done | bytes 524320 | tf_op jit(solution)/shard_map/ppermute | solution.py:897
  105.6 2.4 %collective-permute-done.3.first_ref = f32[1024,128]{1,0:T(8,128)S(1)} collective-permute-done((f32[1024,128]{1,0:T(8,128)S(1)}, f32[1024,128]{1,0:T(8,128)S(1)}, u32[]{:S(2)}, u32[]{:S(2)}) %collective-permute-start.3) | collective-permute-done | bytes 524320 | tf_op jit(solution)/shard_map/ppermute | solution.py:898
  108.0 1.9 %shard_map.154 = f32[8,128]{1,0:T(8,128)S(1)} custom-call(s32[1]{0:T(128)} %bitcast.odd_ref, f32[1024,128]{1,0:T(8,128)S(1)} %collective-permute-done.2.second_ref, f32[1024,128]{1,0:T(8,128)S(1)} %collective-permute-done.3.first_ref, f32[128,128]{1,0:T(8,128)S(1)} %shard_map.153.kept_ref, f32[64,128]{1,0:T(8,128)S(1)} %get-tuple-element.66.refs_0_.sums_ref, ...), custom_call_target="tpu_custom_call" | custom-call | flops 1048576 | bytes 5345284 | tf_op jit(solution)/shard_map/pallas_call | solution.py:597
  110.0 2.1 %collective-permute-start.4 = (f32[2,128]{1,0:T(2,128)S(1)}, f32[2,128]{1,0:T(2,128)S(1)}, u32[]{:S(2)}, u32[]{:S(2)}) collective-permute-start(f32[2,128]{1,0:T(2,128)S(1)} %slice.12), channel_id=1, source_target_pairs={{0,16},{16,0},{32,48},{48,32},{64,80},{80,64},{96,112},{112,96},{1... | collective-permute-start | bytes 3080 | tf_op jit(solution)/shard_map/ppermute | solution.py:903
  112.1 0.8 collective-permute-done.4
  112.9 0.7 broadcast_in_dim.45
  113.6 9.1 %all-to-all-start.2 = ((f32[128,2,128]{2,1,0:T(2,128)}), f32[128,2,128]{2,1,0:T(2,128)S(1)}, u32[]{:S(2)}, u32[]{:S(2)}) async-start(f32[128,2,128]{2,1,0:T(2,128)} %broadcast_in_dim.45), calls=%async_computation.2 | async-start | bytes 262144 | tf_op jit(solution)/shard_map/all_to_all | solution.py:907
  122.7 8.1 %shard_map.152 = (f32[64,256]{1,0:T(8,128)}, f32[256,4096]{1,0:T(8,128)}, f32[256,1024]{1,0:T(8,128)}) custom-call(s32[1]{0:T(128)} %bitcast.odd_ref, f32[2048,128]{1,0:T(8,128)S(1)} %get-tuple-element.63.own_ref, f32[1024,128]{1,0:T(8,128)S(1)} %collective-permute-done.2.second_ref, f32[1024,128]{1,0:T(8,128)S(1)} %collective-permute-done.3.first_ref, ...), custom_call_target="tpu_custom_call" | custom-call | flops 1879048192 | bytes 20807684 | tf_op jit(solution)/shard_map/pallas_call | solution.py:597
  130.8 3.4 %all-to-all-done.2 = f32[128,2,128]{2,1,0:T(2,128)S(1)} async-done(((f32[128,2,128]{2,1,0:T(2,128)}), f32[128,2,128]{2,1,0:T(2,128)S(1)}, u32[]{:S(2)}, u32[]{:S(2)}) %all-to-all-start.2) | async-done | bytes 131104 | tf_op jit(solution)/shard_map/all_to_all | solution.py:907
  134.3 0.1 reduce_sum.9
  134.4 0.6 slice_bitcast_fusion
  (4 shorter events, 0.0 us)
Async XLA Ops:
  3.8 20.8 %collective-permute-start = (f32[1040,128]{1,0:T(8,128)S(1)}, f32[1040,128]{1,0:T(8,128)S(1)}, u32[]{:S(2)}, u32[]{:S(2)}) collective-permute-start(f32[1040,128]{1,0:T(8,128)S(1)} %get-tuple-element.46), channel_id=1, source_target_pairs={{0,15},{1,2},{2,1},{3,4},{4,3},{5,6},{6,5},{7,8},{8,7},{9,10},{10,... | collective-permute-start | bytes 1597448 | tf_op jit(solution)/shard_map/ppermute | solution.py:873
  12.7 12.6 %collective-permute-start.1 = (f32[1040,128]{1,0:T(8,128)S(1)}, f32[1040,128]{1,0:T(8,128)S(1)}, u32[]{:S(2)}, u32[]{:S(2)}) collective-permute-start(f32[1040,128]{1,0:T(8,128)S(1)} %get-tuple-element.47), channel_id=1, source_target_pairs={{0,1},{1,0},{2,3},{3,2},{4,5},{5,4},{6,7},{7,6},{8,9},{9,8},{10,11... | collective-permute-start | bytes 1597448 | tf_op jit(solution)/shard_map/ppermute | solution.py:874
  25.6 1.0 copy-start
  26.7 27.5 %all-to-all-start = ((f32[8,264,128]{2,1,0:T(8,128)}), f32[8,264,128]{2,1,0:T(8,128)S(1)}, u32[]{:S(2)}, u32[]{:S(2)}) async-start(f32[8,264,128]{2,1,0:T(8,128)} %copy-done), calls=%async_computation | async-start | bytes 2162688 | tf_op jit(solution)/shard_map/all_to_all | solution.py:879
  55.3 23.8 %all-to-all-start.1 = ((f32[8,256,128]{2,1,0:T(8,128)}), f32[8,256,128]{2,1,0:T(8,128)S(1)}, u32[]{:S(2)}, u32[]{:S(2)}) async-start(f32[8,256,128]{2,1,0:T(8,128)} %shard_map.149.after_ref), calls=%async_computation.1 | async-start | bytes 2097152 | tf_op jit(solution)/shard_map/all_to_all | solution.py:895
  80.4 25.3 %collective-permute-start.2 = (f32[1024,128]{1,0:T(8,128)S(1)}, f32[1024,128]{1,0:T(8,128)S(1)}, u32[]{:S(2)}, u32[]{:S(2)}) collective-permute-start(f32[1024,128]{1,0:T(8,128)S(1)} %get-tuple-element.64), channel_id=1, source_target_pairs={{0,15},{1,2},{2,1},{3,4},{4,3},{5,6},{6,5},{7,8},{8,7},{9,10},{10,... | collective-permute-start | bytes 1572872 | tf_op jit(solution)/shard_map/ppermute | solution.py:897
  94.7 13.3 %collective-permute-start.3 = (f32[1024,128]{1,0:T(8,128)S(1)}, f32[1024,128]{1,0:T(8,128)S(1)}, u32[]{:S(2)}, u32[]{:S(2)}) collective-permute-start(f32[1024,128]{1,0:T(8,128)S(1)} %get-tuple-element.65), channel_id=1, source_target_pairs={{0,1},{1,0},{2,3},{3,2},{4,5},{5,4},{6,7},{7,6},{8,9},{9,8},{10,11... | collective-permute-start | bytes 1572872 | tf_op jit(solution)/shard_map/ppermute | solution.py:898
  110.0 2.9 %collective-permute-start.4 = (f32[2,128]{1,0:T(2,128)S(1)}, f32[2,128]{1,0:T(2,128)S(1)}, u32[]{:S(2)}, u32[]{:S(2)}) collective-permute-start(f32[2,128]{1,0:T(2,128)S(1)} %slice.12), channel_id=1, source_target_pairs={{0,16},{16,0},{32,48},{48,32},{64,80},{80,64},{96,112},{112,96},{1... | collective-permute-start | bytes 3080 | tf_op jit(solution)/shard_map/ppermute | solution.py:903
  113.6 20.6 %all-to-all-start.2 = ((f32[128,2,128]{2,1,0:T(2,128)}), f32[128,2,128]{2,1,0:T(2,128)S(1)}, u32[]{:S(2)}, u32[]{:S(2)}) async-start(f32[128,2,128]{2,1,0:T(2,128)} %broadcast_in_dim.45), calls=%async_computation.2 | async-start | bytes 262144 | tf_op jit(solution)/shard_map/all_to_all | solution.py:907
